TPU v7x, 32 devices: a whole 2x2x4 slice. The times are simulated.
32 devices in a mesh: section: 2 (over x), ctx: 8 (over z, y), fsdp: 2 (over core).
Axes of the slice: x: 2, y: 2, z: 4, core: 2. Of those that a mesh axis runs over, the one named last changes fastest.
Arguments:
- inputs: bfloat16 [2, 2, 1024, 640], P(None, 'fsdp', 'ctx'), may hold values from -6 to 6
- out_cotangent: bfloat16 [2, 2, 1024, 640], P(None, 'fsdp', 'ctx'), may hold values from -6 to 6
- block_order: int32 [16], replicated, may hold values from 0 to 15, as said below
- w_query: bfloat16 [2, 640, 1024], P('section', 'fsdp'), may hold values from -0.25 to 0.25
- w_key: bfloat16 [2, 640, 256], P('section', 'fsdp'), may hold values from -0.25 to 0.25
- w_value: bfloat16 [2, 640, 256], P('section', 'fsdp'), may hold values from -0.25 to 0.25
- w_output: bfloat16 [2, 1024, 640], P('section', 'fsdp'), may hold values from -0.1875 to 0.1875
- w_gate: bfloat16 [2, 640, 2048], P('section', 'fsdp'), may hold values from -0.25 to 0.25
- w_up: bfloat16 [2, 640, 2048], P('section', 'fsdp'), may hold values from -0.25 to 0.25
- w_down: bfloat16 [2, 2048, 640], P('section', 'fsdp'), may hold values from -0.125 to 0.125
- g_input: bfloat16 [2, 640], P('section', 'fsdp'), may hold values from 0.5 to 1.5
- g_query: bfloat16 [2, 256], P('section', 'fsdp'), may hold values from 0.5 to 1.5
- g_key: bfloat16 [2, 256], P('section', 'fsdp'), may hold values from 0.5 to 1.5
- g_post_attn: bfloat16 [2, 640], P('section', 'fsdp'), may hold values from 0.5 to 1.5
- g_pre_ffw: bfloat16 [2, 640], P('section', 'fsdp'), may hold values from 0.5 to 1.5
- g_post_ffw: bfloat16 [2, 640], P('section', 'fsdp'), may hold values from 0.5 to 1.5
Outputs:
- acts: bfloat16 [2, 2, 2, 1024, 640], P('section', None, 'fsdp', 'ctx')
- input_grads: bfloat16 [2, 2, 2, 1024, 640], P('section', None, 'fsdp', 'ctx')
- grad_w_query: float32 [2, 640, 1024], P('section', 'fsdp')
- grad_w_key: float32 [2, 640, 256], P('section', 'fsdp')
- grad_w_value: float32 [2, 640, 256], P('section', 'fsdp')
- grad_w_output: float32 [2, 1024, 640], P('section', 'fsdp')
- grad_w_gate: float32 [2, 640, 2048], P('section', 'fsdp')
- grad_w_up: float32 [2, 640, 2048], P('section', 'fsdp')
- grad_w_down: float32 [2, 2048, 640], P('section', 'fsdp')
- grad_g_input: float32 [2, 640], P('section', 'fsdp')
- grad_g_query: float32 [2, 256], P('section', 'fsdp')
- grad_g_key: float32 [2, 256], P('section', 'fsdp')
- grad_g_post_attn: float32 [2, 640], P('section', 'fsdp')
- grad_g_pre_ffw: float32 [2, 640], P('section', 'fsdp')
- grad_g_post_ffw: float32 [2, 640], P('section', 'fsdp')
Inputs may be any that keep to these rules, and one draw needn't show every extreme that they name: block_order is a permutation of 0 to 15 whose entries 2i and 2i + 1 add up to 15.
All inputs are finite; a program needn't handle non-finite values.
Results may differ from a plain program's by a relative error of at most 0.038.
Values may be sent and summed in bfloat16 or wider, within the bound.
No kernel may reach another device: no remote copies, remote signals or barrier semaphores. Data moves between devices by JAX's collectives and lax.ppermute only.
A program may use at most 192 MiB of HBM per device.

v0:
```python
import jax
import jax.numpy as jnp
from jax import lax
from jax.sharding import PartitionSpec as P

epsilon = 1e-06
rope_base = 1000000.0
masked = -1e30
score_scale = 0.0625


def from_behind(shard, axis, by):
    count = lax.axis_size(axis)
    pairs = [(i, i + by) for i in range(count) if 0 <= i + by < count]
    return lax.ppermute(shard, axis, pairs)


def gelu_fn(values_in):
    return jax.nn.gelu(values_in, approximate=True)


def norm_apply(values_in, gain_vec):
    factor = lax.rsqrt(jnp.mean(values_in * values_in, axis=-1, keepdims=True) + epsilon)
    return values_in * factor * gain_vec


def norm_back(values_in, gain_vec, grad_out):
    factor = lax.rsqrt(jnp.mean(values_in * values_in, axis=-1, keepdims=True) + epsilon)
    scaled = grad_out * gain_vec
    grad_in = factor * (
        scaled - values_in * factor * factor * jnp.mean(scaled * values_in, axis=-1, keepdims=True)
    )
    grad_gain = jnp.sum((grad_out * values_in * factor).reshape(-1, values_in.shape[-1]), axis=0)
    return (grad_in, grad_gain)


def rotate(values_in, cos_table, sin_table):
    half_width = values_in.shape[-1] // 2
    former = values_in[..., :half_width]
    latter = values_in[..., half_width:]
    return jnp.concatenate(
        [former * cos_table - latter * sin_table, latter * cos_table + former * sin_table], axis=-1
    )


def unrotate(grad_in, cos_table, sin_table):
    half_width = grad_in.shape[-1] // 2
    former = grad_in[..., :half_width]
    latter = grad_in[..., half_width:]
    return jnp.concatenate(
        [former * cos_table + latter * sin_table, latter * cos_table - former * sin_table], axis=-1
    )


def rotation_tables(positions, half_width):
    frequency = rope_base ** (-jnp.arange(half_width, dtype=jnp.float32) / half_width)
    angles = positions.astype(jnp.float32)[:, None] * frequency[None, :]
    return (jnp.cos(angles), jnp.sin(angles))


def token_positions(block_order, first_row, row_count, block_len):
    slot_ids = lax.dynamic_slice_in_dim(block_order, first_row // block_len, row_count // block_len)
    offsets = jnp.arange(block_len, dtype=jnp.int32)
    return (slot_ids[:, None] * block_len + offsets[None, :]).reshape(-1)


def head_rows(values_in, head_count):
    groups, tokens, row_width = values_in.shape
    split = values_in.reshape(groups, tokens, head_count, row_width // head_count)
    return jnp.transpose(split, (0, 2, 1, 3)).reshape(
        groups, head_count * tokens, row_width // head_count
    )


def token_major(rows_in, head_count):
    groups, row_count, row_width = rows_in.shape
    tokens = row_count // head_count
    split = rows_in.reshape(groups, head_count, tokens, row_width)
    return jnp.transpose(split, (0, 2, 1, 3)).reshape(groups, tokens, head_count * row_width)


def put_slot(buffer, array_leaf, slot_index, is_valid):
    current = lax.dynamic_index_in_dim(buffer, slot_index, 0, keepdims=False)
    return lax.dynamic_update_index_in_dim(
        buffer, jnp.where(is_valid, array_leaf, current), slot_index, 0
    )


def attend_step(query_rows, query_pos, block_order, block_len, state_in, block_in, first_row):
    key_block, value_block = block_in
    key_pos = token_positions(block_order, first_row, key_block.shape[1], block_len)
    scores = (
        jnp.einsum("sqd,skd->sqk", query_rows, key_block, preferred_element_type=jnp.float32)
        * score_scale
    )
    allowed = key_pos[None, None, :] <= query_pos[None, :, None]
    running_max, running_total, running_sum = state_in
    new_max = jnp.maximum(running_max, jnp.max(jnp.where(allowed, scores, masked), axis=-1))
    weights = jnp.exp(jnp.where(allowed, scores - new_max[..., None], masked))
    new_total = jnp.sum(weights, axis=-1)
    new_sum = jnp.einsum(
        "sqk,skd->sqd",
        weights.astype(jnp.bfloat16),
        value_block,
        preferred_element_type=jnp.float32,
    )
    return (new_max, new_total, new_sum)


def grad_step(
    query_rows, grad_rows, log_total, row_delta, query_pos, key_block, value_block, key_pos
):
    scores = (
        jnp.einsum("sqd,skd->sqk", query_rows, key_block, preferred_element_type=jnp.float32)
        * score_scale
    )
    allowed = key_pos[None, None, :] <= query_pos[None, :, None]
    attn_probs = jnp.exp(jnp.where(allowed, scores - log_total[..., None], masked))
    prob_grad = jnp.einsum(
        "sqd,skd->sqk", grad_rows, value_block, preferred_element_type=jnp.float32
    )
    score_grad = (attn_probs * (prob_grad - row_delta[..., None])).astype(jnp.bfloat16)
    query_grad = None
    key_grad = None
    value_grad = None
    query_grad = (
        jnp.einsum("sqk,skd->sqd", score_grad, key_block, preferred_element_type=jnp.float32)
        * score_scale
    )
    key_grad = (
        jnp.einsum("sqk,sqd->skd", score_grad, query_rows, preferred_element_type=jnp.float32)
        * score_scale
    )
    value_grad = jnp.einsum(
        "sqk,sqd->skd",
        attn_probs.astype(jnp.bfloat16),
        grad_rows,
        preferred_element_type=jnp.float32,
    )
    return (query_grad, key_grad, value_grad)


def on_device(
    inputs,
    out_cotangent,
    block_order,
    w_query,
    w_key,
    w_value,
    w_output,
    w_gate,
    w_up,
    w_down,
    g_input,
    g_query,
    g_key,
    g_post_attn,
    g_pre_ffw,
    g_post_ffw,
):
    gathered = (
        lax.all_gather(w_query[0], "fsdp", axis=0, tiled=True),
        lax.all_gather(w_key[0], "fsdp", axis=0, tiled=True),
        lax.all_gather(w_value[0], "fsdp", axis=0, tiled=True),
        lax.all_gather(w_output[0], "fsdp", axis=0, tiled=True),
        lax.all_gather(w_gate[0], "fsdp", axis=0, tiled=True),
        lax.all_gather(w_up[0], "fsdp", axis=0, tiled=True),
        lax.all_gather(w_down[0], "fsdp", axis=0, tiled=True),
        lax.all_gather(g_input[0], "fsdp", axis=0, tiled=True),
        lax.all_gather(g_query[0], "fsdp", axis=0, tiled=True),
        lax.all_gather(g_key[0], "fsdp", axis=0, tiled=True),
        lax.all_gather(g_post_attn[0], "fsdp", axis=0, tiled=True),
        lax.all_gather(g_pre_ffw[0], "fsdp", axis=0, tiled=True),
        lax.all_gather(g_post_ffw[0], "fsdp", axis=0, tiled=True),
    )
    (
        full_query,
        full_key,
        full_value,
        full_output,
        full_gate,
        full_up,
        full_down,
        gain_input,
        gain_query,
        gain_key,
        gain_attn,
        gain_pre,
        gain_post,
    ) = gathered
    w_project = jnp.concatenate([full_query, full_key, full_value], axis=1)
    w_ffw_in = jnp.concatenate([full_gate, full_up], axis=1)
    gain_input = gain_input.astype(jnp.float32)
    gain_query = gain_query.astype(jnp.float32)
    gain_key = gain_key.astype(jnp.float32)
    gain_attn = gain_attn.astype(jnp.float32)
    gain_pre = gain_pre.astype(jnp.float32)
    gain_post = gain_post.astype(jnp.float32)
    head_dim = gain_query.shape[0]
    query_cols = full_output.shape[0]
    head_count = query_cols // head_dim
    ff_width = full_down.shape[0]
    micro_count, seq_local, tokens, model_width = inputs.shape
    block_len = tokens // 2
    ctx_size = lax.axis_size("ctx")
    key_span = tokens * min(8, ctx_size)
    section_index = lax.axis_index("section")
    ctx_index = lax.axis_index("ctx")
    local_pos = token_positions(block_order, ctx_index * tokens, tokens, block_len)
    query_pos = jnp.tile(local_pos, head_count)
    cos_table, sin_table = rotation_tables(local_pos, head_dim // 2)
    received = jnp.zeros((seq_local, tokens, model_width), jnp.bfloat16)
    acts_out = jnp.zeros((micro_count, seq_local, tokens, model_width), jnp.bfloat16)
    stored = None
    for step_index in range(micro_count + 1):
        micro_index = step_index - section_index
        is_valid = (micro_index >= 0) & (micro_index < micro_count)
        slot_index = jnp.clip(micro_index, 0, micro_count - 1)
        own_input = lax.dynamic_index_in_dim(inputs, slot_index, 0, keepdims=False)
        hidden = jnp.where(section_index == 0, own_input, received).astype(jnp.float32)
        layer_flat_in = hidden.reshape(-1, model_width)
        layer_normed = norm_apply(layer_flat_in, gain_input).astype(jnp.bfloat16)
        layer_projected = jnp.dot(layer_normed, w_project, preferred_element_type=jnp.float32)
        layer_query_heads = layer_projected[:, :query_cols].reshape(
            seq_local, tokens, head_count, head_dim
        )
        layer_key_lin = layer_projected[:, query_cols : query_cols + head_dim].reshape(
            seq_local, tokens, head_dim
        )
        layer_value_low = (
            layer_projected[:, query_cols + head_dim :]
            .reshape(seq_local, tokens, head_dim)
            .astype(jnp.bfloat16)
        )
        query_rot = rotate(
            norm_apply(layer_query_heads, gain_query),
            cos_table[None, :, None, :],
            sin_table[None, :, None, :],
        ).astype(jnp.bfloat16)
        layer_key_rot = rotate(
            norm_apply(layer_key_lin, gain_key), cos_table[None], sin_table[None]
        ).astype(jnp.bfloat16)
        layer_query_tok = query_rot.reshape(seq_local, tokens, query_cols)
        layer_query_rows = head_rows(layer_query_tok, head_count)
        row_shape = layer_query_rows.shape[:2]
        start_state = (
            jnp.full(row_shape, masked, jnp.float32),
            jnp.zeros(row_shape, jnp.float32),
            jnp.zeros(layer_query_rows.shape, jnp.float32),
        )
        row_max, row_total, row_sum = attend_step(
            layer_query_rows,
            query_pos,
            block_order,
            block_len,
            start_state,
            (
                lax.all_gather(layer_key_rot, "ctx", axis=1, tiled=True),
                lax.all_gather(layer_value_low, "ctx", axis=1, tiled=True),
            ),
            jnp.int32(0),
        )
        layer_attn_rows = row_sum / row_total[..., None]
        layer_log_total = row_max + jnp.log(row_total)
        layer_attn_low = (
            token_major(layer_attn_rows, head_count).reshape(-1, query_cols).astype(jnp.bfloat16)
        )
        layer_branch = jnp.dot(layer_attn_low, full_output, preferred_element_type=jnp.float32)
        layer_middle = layer_flat_in + norm_apply(layer_branch, gain_attn)
        layer_pre_ffw = norm_apply(layer_middle, gain_pre).astype(jnp.bfloat16)
        layer_gate_up = jnp.dot(layer_pre_ffw, w_ffw_in, preferred_element_type=jnp.float32)
        layer_hidden_ffw = (
            gelu_fn(layer_gate_up[:, :ff_width]) * layer_gate_up[:, ff_width:]
        ).astype(jnp.bfloat16)
        layer_down_out = jnp.dot(layer_hidden_ffw, full_down, preferred_element_type=jnp.float32)
        result = layer_middle + norm_apply(layer_down_out, gain_post)
        layer_saved_parts = (
            layer_flat_in,
            layer_normed,
            layer_projected,
            layer_query_tok,
            layer_key_rot,
            layer_value_low,
            layer_attn_rows,
            layer_log_total,
            layer_attn_low,
            layer_branch,
            layer_middle,
            layer_pre_ffw,
            layer_gate_up,
            layer_hidden_ffw,
            layer_down_out,
        )
        result, saved_parts = (result.reshape(seq_local, tokens, model_width), layer_saved_parts)
        result_low = result.astype(jnp.bfloat16)
        if stored is None:
            stored = jax.tree.map(
                lambda array_leaf: jnp.zeros((micro_count,) + array_leaf.shape, array_leaf.dtype),
                saved_parts,
            )
        stored = jax.tree.map(
            lambda buffer, array_leaf: put_slot(buffer, array_leaf, slot_index, is_valid),
            stored,
            saved_parts,
        )
        acts_out = put_slot(acts_out, result_low, slot_index, is_valid)
        if step_index < micro_count:
            received = from_behind(result_low, "section", 1)
    grad_received = jnp.zeros((seq_local, tokens, model_width), jnp.bfloat16)
    grad_inputs = jnp.zeros((micro_count, seq_local, tokens, model_width), jnp.bfloat16)
    totals = None
    for step_index in range(micro_count + 1):
        micro_index = step_index - (1 - section_index)
        is_valid = (micro_index >= 0) & (micro_index < micro_count)
        slot_index = jnp.clip(micro_index, 0, micro_count - 1)
        own_grad = lax.dynamic_index_in_dim(out_cotangent, slot_index, 0, keepdims=False)
        grad_out = jnp.where(section_index == 1, own_grad, grad_received).astype(jnp.float32)
        saved_parts = jax.tree.map(
            lambda buffer: lax.dynamic_index_in_dim(buffer, slot_index, 0, keepdims=False), stored
        )
        (
            flat_in,
            normed,
            projected,
            query_tok,
            key_rot,
            value_low,
            attn_rows,
            log_total,
            attn_low,
            branch,
            middle,
            pre_ffw,
            gate_up,
            hidden_ffw,
            down_out,
        ) = saved_parts[:15]
        grad_flat = grad_out.reshape(-1, model_width)
        down_part, grad_gain_post = norm_back(down_out, gain_post, grad_flat)
        down_grad = down_part.astype(jnp.bfloat16)
        layer_grad_down = jnp.einsum(
            "rf,rd->fd", hidden_ffw, down_grad, preferred_element_type=jnp.float32
        )
        ffw_grad = jnp.einsum("rd,fd->rf", down_grad, full_down, preferred_element_type=jnp.float32)
        gate_part = gate_up[:, :ff_width]
        up_part = gate_up[:, ff_width:]
        activated, gelu_back = jax.vjp(gelu_fn, gate_part)
        gate_grad = gelu_back(ffw_grad * up_part)[0]
        gate_up_grad = jnp.concatenate([gate_grad, ffw_grad * activated], axis=1).astype(
            jnp.bfloat16
        )
        layer_grad_ffw_in = jnp.einsum(
            "rd,rf->df", pre_ffw, gate_up_grad, preferred_element_type=jnp.float32
        )
        pre_grad = jnp.einsum(
            "rf,df->rd", gate_up_grad, w_ffw_in, preferred_element_type=jnp.float32
        )
        middle_part, grad_gain_pre = norm_back(middle, gain_pre, pre_grad)
        middle_grad = grad_flat + middle_part
        branch_part, grad_gain_attn = norm_back(branch, gain_attn, middle_grad)
        branch_grad = branch_part.astype(jnp.bfloat16)
        layer_grad_output = jnp.einsum(
            "rc,rd->cd", attn_low, branch_grad, preferred_element_type=jnp.float32
        )
        attn_grad = jnp.einsum(
            "rd,cd->rc", branch_grad, full_output, preferred_element_type=jnp.float32
        ).astype(jnp.bfloat16)
        grad_tok = attn_grad.reshape(seq_local, tokens, query_cols)
        grad_rows = head_rows(grad_tok, head_count)
        row_delta = jnp.sum(grad_rows.astype(jnp.float32) * attn_rows, axis=-1)
        query_rows = head_rows(query_tok, head_count)
        whole_keys = lax.all_gather(key_rot, "ctx", axis=1, tiled=True)
        whole_values = lax.all_gather(value_low, "ctx", axis=1, tiled=True)
        span_count = whole_keys.shape[1] // key_span

        def key_slices(block_index):
            first_row = block_index * key_span
            key_block = lax.dynamic_slice_in_dim(whole_keys, first_row, key_span, 1)
            value_block = lax.dynamic_slice_in_dim(whole_values, first_row, key_span, 1)
            return (
                first_row,
                key_block,
                value_block,
                token_positions(block_order, first_row, key_span, block_len),
            )

        query_zero = jnp.zeros(query_rows.shape, jnp.float32)
        whole_zero = jnp.zeros(whole_keys.shape, jnp.float32)

        def all_parts(block_index, state_in):
            first_row, key_block, value_block, key_pos = key_slices(block_index)
            parts = grad_step(
                query_rows,
                grad_rows,
                log_total,
                row_delta,
                query_pos,
                key_block,
                value_block,
                key_pos,
            )
            key_full = lax.dynamic_update_slice_in_dim(state_in[1], parts[1], first_row, 1)
            value_full = lax.dynamic_update_slice_in_dim(state_in[2], parts[2], first_row, 1)
            return (state_in[0] + parts[0], key_full, value_full)

        query_grad, key_full, value_full = lax.fori_loop(
            0, span_count, all_parts, (query_zero, whole_zero, whole_zero)
        )
        key_grad = lax.psum_scatter(key_full, "ctx", scatter_dimension=1, tiled=True)
        value_grad = lax.psum_scatter(value_full, "ctx", scatter_dimension=1, tiled=True)
        query_tok_grad = token_major(query_grad, head_count).reshape(
            seq_local, tokens, head_count, head_dim
        )
        query_heads = projected[:, :query_cols].reshape(seq_local, tokens, head_count, head_dim)
        query_lin_grad, grad_gain_query = norm_back(
            query_heads,
            gain_query,
            unrotate(query_tok_grad, cos_table[None, :, None, :], sin_table[None, :, None, :]),
        )
        key_lin = projected[:, query_cols : query_cols + head_dim].reshape(
            seq_local, tokens, head_dim
        )
        key_lin_grad, grad_gain_key = norm_back(
            key_lin, gain_key, unrotate(key_grad, cos_table[None], sin_table[None])
        )
        projected_grad = jnp.concatenate(
            [
                query_lin_grad.reshape(-1, query_cols),
                key_lin_grad.reshape(-1, head_dim),
                value_grad.reshape(-1, head_dim),
            ],
            axis=1,
        ).astype(jnp.bfloat16)
        layer_grad_project = jnp.einsum(
            "rd,rc->dc", normed, projected_grad, preferred_element_type=jnp.float32
        )
        normed_grad = jnp.einsum(
            "rc,dc->rd", projected_grad, w_project, preferred_element_type=jnp.float32
        )
        input_part, grad_gain_input = norm_back(flat_in, gain_input, normed_grad)
        input_grad = middle_grad + input_part
        grads = (
            layer_grad_project,
            layer_grad_output,
            layer_grad_ffw_in,
            layer_grad_down,
            grad_gain_input,
            grad_gain_query,
            grad_gain_key,
            grad_gain_attn,
            grad_gain_pre,
            grad_gain_post,
        )
        input_grad, grads = (input_grad.reshape(seq_local, tokens, model_width), grads)
        valid_weight = is_valid.astype(jnp.float32)
        grads = jax.tree.map(lambda array_leaf: array_leaf * valid_weight, grads)
        totals = grads if totals is None else jax.tree.map(jnp.add, totals, grads)
        grad_low = input_grad.astype(jnp.bfloat16)
        grad_inputs = put_slot(grad_inputs, grad_low, slot_index, is_valid)
        if step_index < micro_count:
            grad_received = from_behind(grad_low, "section", -1)
    (
        grad_project,
        grad_output,
        grad_ffw_in,
        grad_down,
        grad_g_input,
        grad_g_query,
        grad_g_key,
        grad_g_attn,
        grad_g_pre,
        grad_g_post,
    ) = totals
    grad_query = grad_project[:, :query_cols]
    grad_key = grad_project[:, query_cols : query_cols + head_dim]
    grad_value = grad_project[:, query_cols + head_dim :]
    grad_gate = grad_ffw_in[:, :ff_width]
    grad_up = grad_ffw_in[:, ff_width:]
    shard_parts = (
        lax.psum_scatter(
            grad_query.astype(jnp.bfloat16), "fsdp", scatter_dimension=0, tiled=True
        ).astype(jnp.float32),
        lax.psum_scatter(
            grad_key.astype(jnp.bfloat16), "fsdp", scatter_dimension=0, tiled=True
        ).astype(jnp.float32),
        lax.psum_scatter(
            grad_value.astype(jnp.bfloat16), "fsdp", scatter_dimension=0, tiled=True
        ).astype(jnp.float32),
        lax.psum_scatter(
            grad_output.astype(jnp.bfloat16), "fsdp", scatter_dimension=0, tiled=True
        ).astype(jnp.float32),
        lax.psum_scatter(
            grad_gate.astype(jnp.bfloat16), "fsdp", scatter_dimension=0, tiled=True
        ).astype(jnp.float32),
        lax.psum_scatter(
            grad_up.astype(jnp.bfloat16), "fsdp", scatter_dimension=0, tiled=True
        ).astype(jnp.float32),
        lax.psum_scatter(
            grad_down.astype(jnp.bfloat16), "fsdp", scatter_dimension=0, tiled=True
        ).astype(jnp.float32),
        lax.psum_scatter(
            grad_g_input.astype(jnp.bfloat16), "fsdp", scatter_dimension=0, tiled=True
        ).astype(jnp.float32),
        lax.psum_scatter(
            grad_g_query.astype(jnp.bfloat16), "fsdp", scatter_dimension=0, tiled=True
        ).astype(jnp.float32),
        lax.psum_scatter(
            grad_g_key.astype(jnp.bfloat16), "fsdp", scatter_dimension=0, tiled=True
        ).astype(jnp.float32),
        lax.psum_scatter(
            grad_g_attn.astype(jnp.bfloat16), "fsdp", scatter_dimension=0, tiled=True
        ).astype(jnp.float32),
        lax.psum_scatter(
            grad_g_pre.astype(jnp.bfloat16), "fsdp", scatter_dimension=0, tiled=True
        ).astype(jnp.float32),
        lax.psum_scatter(
            grad_g_post.astype(jnp.bfloat16), "fsdp", scatter_dimension=0, tiled=True
        ).astype(jnp.float32),
    )
    (
        part_query,
        part_key,
        part_value,
        part_output,
        part_gate,
        part_up,
        part_down,
        part_input,
        part_gquery,
        part_gkey,
        part_attn,
        part_pre,
        part_post,
    ) = shard_parts
    summed = lax.psum(
        (
            part_query,
            part_key,
            part_value,
            part_output,
            part_gate,
            part_up,
            part_down,
            part_input,
            part_gquery,
            part_gkey,
            part_attn,
            part_pre,
            part_post,
        ),
        "ctx",
    )
    return (acts_out[None], grad_inputs[None]) + tuple((member[None] for member in summed))


def solution(mesh):
    in_specs = (
        P(None, "fsdp", "ctx", None),
        P(None, "fsdp", "ctx", None),
        P(),
        P("section", "fsdp", None),
        P("section", "fsdp", None),
        P("section", "fsdp", None),
        P("section", "fsdp", None),
        P("section", "fsdp", None),
        P("section", "fsdp", None),
        P("section", "fsdp", None),
        P("section", "fsdp"),
        P("section", "fsdp"),
        P("section", "fsdp"),
        P("section", "fsdp"),
        P("section", "fsdp"),
        P("section", "fsdp"),
    )
    out_specs = (
        P("section", None, "fsdp", "ctx", None),
        P("section", None, "fsdp", "ctx", None),
        P("section", "fsdp", None),
        P("section", "fsdp", None),
        P("section", "fsdp", None),
        P("section", "fsdp", None),
        P("section", "fsdp", None),
        P("section", "fsdp", None),
        P("section", "fsdp", None),
        P("section", "fsdp"),
        P("section", "fsdp"),
        P("section", "fsdp"),
        P("section", "fsdp"),
        P("section", "fsdp"),
        P("section", "fsdp"),
    )
    return jax.shard_map(
        on_device, mesh=mesh, in_specs=in_specs, out_specs=out_specs, check_vma=False
    )
```

profile of v0, /device:TPU:0, one launch (start us, length us, event | category | flops | bytes accessed | tf_op | source)
XLA Modules:
  0.0 1365.5 jit_solution(14947542736049808252)
XLA Ops:
  29.7 35.3 %all_gather.81 = bf16[1,1024,256]{2,1,0:T(8,128)(2,1)} all-gather(bf16[1,128,256]{2,1,0:T(8,128)(2,1)S(1)} %pad_maximum_fusion.26), channel_id=1, replica_groups=mesh['section'=2,'ctx'=8,'fsdp'=2] {'ctx'}, dimensions={1}, use_global_device_ids=true | all-gather | bytes 589824 | tf_op jit(solution)/shard_map/all_gather | solution.py:258
  68.5 31.3 %all-gather.6 = bf16[1024,256]{1,0:T(8,128)(2,1)S(1)} all-gather(bf16[128,256]{1,0:T(8,128)(2,1)S(1)} %get-tuple-element.308), channel_id=8, replica_groups=mesh['section'=2,'ctx'=8,'fsdp'=2] {'ctx'}, dimensions={0}, use_global_device_ids=true | all-gather | bytes 589824 | tf_op jit(solution)/shard_map/all_gather | solution.py:259
  113.9 4.1 bitcast_dynamic-update-slice_fusion.2
  122.5 3.4 collective-permute-start
  134.0 34.0 %all-gather.14 = bf16[1024,256]{1,0:T(8,128)(2,1)} all-gather(bf16[128,256]{1,0:T(8,128)(2,1)S(1)} %get-tuple-element.306), channel_id=16, replica_groups=mesh['section'=2,'ctx'=8,'fsdp'=2] {'ctx'}, dimensions={0}, use_global_device_ids=true | all-gather | bytes 589824 | tf_op jit(solution)/shard_map/all_gather | solution.py:259
  168.5 33.2 %all_gather.90 = bf16[1,1024,256]{2,1,0:T(8,128)(2,1)} all-gather(bf16[1,128,256]{2,1,0:T(8,128)(2,1)S(1)} %pad_maximum_fusion.27), channel_id=1, replica_groups=mesh['section'=2,'ctx'=8,'fsdp'=2] {'ctx'}, dimensions={1}, use_global_device_ids=true | all-gather | bytes 589824 | tf_op jit(solution)/shard_map/all_gather | solution.py:258
  214.0 4.9 bitcast_dynamic-update-slice_fusion.1
  236.0 33.3 %all-gather.15 = bf16[1024,256]{1,0:T(8,128)(2,1)} all-gather(bf16[128,256]{1,0:T(8,128)(2,1)S(1)} %get-tuple-element.304), channel_id=17, replica_groups=mesh['section'=2,'ctx'=8,'fsdp'=2] {'ctx'}, dimensions={0}, use_global_device_ids=true | all-gather | bytes 589824 | tf_op jit(solution)/shard_map/all_gather | solution.py:259
  269.7 33.7 %all_gather.92 = bf16[1,1024,256]{2,1,0:T(8,128)(2,1)} all-gather(bf16[1,128,256]{2,1,0:T(8,128)(2,1)S(1)} %pad_maximum_fusion.28), channel_id=1, replica_groups=mesh['section'=2,'ctx'=8,'fsdp'=2] {'ctx'}, dimensions={1}, use_global_device_ids=true | all-gather | bytes 589824 | tf_op jit(solution)/shard_map/all_gather | solution.py:258
  319.4 4.9 bitcast_dynamic-update-slice_fusion
  328.6 5.5 dynamic-slice_bitcast_fusion
  346.6 33.6 %all-gather.16 = bf16[1,1,1024,256]{3,2,1,0:T(8,128)(2,1)} all-gather(bf16[1,1,128,256]{3,2,1,0:T(8,128)(2,1)S(1)} %get-tuple-element.378), channel_id=18, replica_groups=mesh['section'=2,'ctx'=8,'fsdp'=2] {'ctx'}, dimensions={2}, use_global_device_ids=true | all-gather | bytes 589824 | tf_op jit(solution)/shard_map/all_gather | solution.py:372
  389.9 33.4 %all-gather.17 = bf16[1,1,1024,256]{3,2,1,0:T(8,128)(2,1)} all-gather(bf16[1,1,128,256]{3,2,1,0:T(8,128)(2,1)S(1)} %get-tuple-element.375), channel_id=19, replica_groups=mesh['section'=2,'ctx'=8,'fsdp'=2] {'ctx'}, dimensions={2}, use_global_device_ids=true | all-gather | bytes 589824 | tf_op jit(solution)/shard_map/all_gather | solution.py:373
  459.6 31.9 %all-gather.18 = bf16[1,1,1024,256]{3,2,1,0:T(8,128)(2,1)S(1)} all-gather(bf16[1,1,128,256]{3,2,1,0:T(8,128)(2,1)} %get-tuple-element.377), channel_id=20, replica_groups=mesh['section'=2,'ctx'=8,'fsdp'=2] {'ctx'}, dimensions={2}, use_global_device_ids=true | all-gather | bytes 589824 | tf_op jit(solution)/shard_map/all_gather | solution.py:372
  491.5 33.7 %all-gather.19 = bf16[1,1,1024,256]{3,2,1,0:T(8,128)(2,1)} all-gather(bf16[1,1,128,256]{3,2,1,0:T(8,128)(2,1)} %get-tuple-element.374), channel_id=21, replica_groups=mesh['section'=2,'ctx'=8,'fsdp'=2] {'ctx'}, dimensions={2}, use_global_device_ids=true | all-gather | bytes 589824 | tf_op jit(solution)/shard_map/all_gather | solution.py:373
  533.4 36.2 %reduce-scatter.16.cloned.1.call-done = f32[1,128,256]{2,1,0:T(8,128)} async-done(((f32[1,1024,256]{2,1,0:T(8,128)}), f32[1,128,256]{2,1,0:T(8,128)}) %reduce-scatter.16.cloned.1.call-update) | async-done | bytes 131088 | tf_op jit(solution)/shard_map/reduce_scatter | solution.py:410
  584.4 3.8 fusion.64
  609.3 32.2 %all-gather.20 = bf16[1,1,1024,256]{3,2,1,0:T(8,128)(2,1)S(1)} all-gather(bf16[1,1,128,256]{3,2,1,0:T(8,128)(2,1)} %get-tuple-element.376), channel_id=22, replica_groups=mesh['section'=2,'ctx'=8,'fsdp'=2] {'ctx'}, dimensions={2}, use_global_device_ids=true | all-gather | bytes 589824 | tf_op jit(solution)/shard_map/all_gather | solution.py:372
  641.6 34.0 %all-gather.21 = bf16[1,1,1024,256]{3,2,1,0:T(8,128)(2,1)} all-gather(bf16[1,1,128,256]{3,2,1,0:T(8,128)(2,1)} %get-tuple-element.373), channel_id=23, replica_groups=mesh['section'=2,'ctx'=8,'fsdp'=2] {'ctx'}, dimensions={2}, use_global_device_ids=true | all-gather | bytes 589824 | tf_op jit(solution)/shard_map/all_gather | solution.py:373
  692.0 51.9 %reduce-scatter.20.cloned.1.call-done = f32[1,128,256]{2,1,0:T(8,128)} async-done(((f32[1,1024,256]{2,1,0:T(8,128)}), f32[1,128,256]{2,1,0:T(8,128)}) %reduce-scatter.20.cloned.1.call-update) | async-done | bytes 131088 | tf_op jit(solution)/shard_map/reduce_scatter | solution.py:410
  750.7 5.5 collective-permute-done.3
  805.2 27.0 %reduce-scatter.22.cloned.1.call-done = f32[1,128,256]{2,1,0:T(8,128)} async-done(((f32[1,1024,256]{2,1,0:T(8,128)}), f32[1,128,256]{2,1,0:T(8,128)}) %reduce-scatter.22.cloned.1.call-update) | async-done | bytes 131088 | tf_op jit(solution)/shard_map/reduce_scatter | solution.py:409
  834.1 64.9 %reduce-scatter.24.cloned.1.call-done = f32[1,128,256]{2,1,0:T(8,128)} async-done(((f32[1,1024,256]{2,1,0:T(8,128)}), f32[1,128,256]{2,1,0:T(8,128)}) %reduce-scatter.24.cloned.1.call-update) | async-done | bytes 131088 | tf_op jit(solution)/shard_map/reduce_scatter | solution.py:410
  900.1 4.2 add_convert_fusion.2
  917.7 5.5 fusion.109
  923.2 7.0 add_convert_fusion
  939.5 5.6 reduce-scatter.26.cloned.1.call-done
  947.4 11.8 reduce-scatter.38.cloned.1.call-done
  962.1 11.3 reduce-scatter.36.cloned.1.call-done
  976.5 11.0 reduce-scatter.34.cloned.1.call-done
  1009.0 23.8 %all-reduce.10 = (f32[1,320]{1,0:T(1,128)}, f32[1,128]{1,0:T(1,128)}, f32[1,128]{1,0:T(1,128)}, f32[1,320]{1,0:T(1,128)}, f32[1,320]{1,0:T(1,128)}, /*index=5*/f32[1,320]{1,0:T(1,128)}) all-reduce(f32[1,320]{1,0:T(1,128)S(1)} %broadcast_in_dim.413, ...), channel_id=1, replica_groups=mesh['section'=2,'ctx'=8,'fsdp'=2] {'ctx'}, use_global_device_ids=true, to_apply=%region_87.88 | all-reduce | flops 1536 | bytes 12288 | tf_op jit(solution)/shard_map/psum | solution.py:535
  1033.9 312.7 %all-reduce.16.cloned.1.call-done = (f32[1,320,1024]{2,1,0:T(8,128)}, f32[1,320,256]{2,1,0:T(8,128)}, f32[1,320,256]{2,1,0:T(8,128)}, f32[1,512,640]{2,1,0:T(8,1...) async-done(((f32[1,320,1024]{2,1,0:T(8,128)}, f32[1,320,256]{2,1,0:T(8,128)}, f32[1,320,256]{2,1,0:T(8,128)}, ...) | async-done | bytes 11141136 | tf_op jit(solution)/shard_map/psum | solution.py:535
  (1039 shorter events, 340.4 us)
Async XLA Ops:
  7.2 17.8 %all-gather.28.cloned.1.call-start = ((), (), s32[]{:S(2)}) async-start(), calls=%async_computation.26 | async-start | bytes 1966080 | tf_op jit(solution)/shard_map/all_gather | solution.py:162
  7.9 95.3 %all-gather.30.cloned.1.call-start = ((), (), s32[]{:S(2)}) async-start(), calls=%async_computation.27 | async-start | bytes 1966080 | tf_op jit(solution)/shard_map/all_gather | solution.py:165
  8.8 102.6 %all-gather.32.cloned.1.call-start = ((), (), s32[]{:S(2)}) async-start(), calls=%async_computation.28 | async-start | bytes 3932160 | tf_op jit(solution)/shard_map/all_gather | solution.py:166
  9.5 101.8 %all-gather.34.cloned.1.call-start = ((), (), s32[]{:S(2)}) async-start(), calls=%async_computation.29 | async-start | bytes 3932160 | tf_op jit(solution)/shard_map/all_gather | solution.py:167
  10.1 109.2 %all-gather.36.cloned.1.call-start = ((), (), s32[]{:S(2)}) async-start(), calls=%async_computation.30 | async-start | bytes 3932160 | tf_op jit(solution)/shard_map/all_gather | solution.py:168
  10.7 518.3 %reduce-scatter.14.cloned.1.call-start = ((), (), s32[]{:S(2)}) async-start(), calls=%async_computation.13 | async-start | bytes 1179648 | tf_op jit(solution)/shard_map/reduce_scatter | solution.py:409
  11.1 89.4 %copy-start.209 = (s32[512]{0:T(512)}, s32[512]{0:T(512)S(1)}, u32[]{:S(2)}) copy-start(s32[512]{0:T(512)S(1)} %broadcast_bitcast_fusion.1) | copy-start | bytes 6148
  23.9 76.5 %copy-start.194 = (s32[1024]{0:T(1024)}, s32[1024]{0:T(1024)S(1)}, u32[]{:S(2)}) copy-start(s32[1024]{0:T(1024)S(1)} %add.900) | copy-start | bytes 12292
  24.8 284.5 %copy-start.54 = (f32[128,128]{1,0:T(8,128)}, f32[128,128]{1,0:T(8,128)S(1)}, u32[]{:S(2)}) copy-start(f32[128,128]{1,0:T(8,128)S(1)} %get-tuple-element.382) | copy-start | bytes 196612
  24.9 284.5 %copy-start.57 = (f32[128,128]{1,0:T(8,128)}, f32[128,128]{1,0:T(8,128)S(1)}, u32[]{:S(2)}) copy-start(f32[128,128]{1,0:T(8,128)S(1)} %get-tuple-element.383) | copy-start | bytes 196612
  122.5 9.0 collective-permute-start
  222.0 10.6 collective-permute-start.1
  438.2 131.4 %reduce-scatter.16.cloned.1.call-start = ((), (), s32[]{:S(2)}) async-start(), calls=%async_computation.14 | async-start | bytes 1179648 | tf_op jit(solution)/shard_map/reduce_scatter | solution.py:410
  451.3 236.9 %reduce-scatter.18.cloned.1.call-start = ((), (), s32[]{:S(2)}) async-start(), calls=%async_computation.15 | async-start | bytes 1179648 | tf_op jit(solution)/shard_map/reduce_scatter | solution.py:409
  458.3 68.7 %copy-start.199 = (s32[1024]{0:T(1024)S(1)}, s32[1024]{0:T(1024)}, u32[]{:S(2)}) copy-start(s32[1024]{0:T(1024)} %copy-done.194) | copy-start | bytes 12292
  458.3 68.7 %copy-start.214 = (s32[512]{0:T(512)S(1)}, s32[512]{0:T(512)}, u32[]{:S(2)}) copy-start(s32[512]{0:T(512)} %copy-done.209) | copy-start | bytes 6148
  458.3 68.7 %copy-start.248 = (f32[1,1,512]{2,1,0:T(1,128)S(1)}, f32[1,1,512]{2,1,0:T(1,128)}, u32[]{:S(2)}) copy-start(f32[1,1,512]{2,1,0:T(1,128)} %get-tuple-element.380) | copy-start | bytes 6148
  575.3 7.3 collective-permute-start.2
  601.6 142.4 %reduce-scatter.20.cloned.1.call-start = ((), (), s32[]{:S(2)}) async-start(), calls=%async_computation.16 | async-start | bytes 1179648 | tf_op jit(solution)/shard_map/reduce_scatter | solution.py:410
  680.6 151.6 %reduce-scatter.22.cloned.1.call-start = ((), (), s32[]{:S(2)}) async-start(), calls=%async_computation.17 | async-start | bytes 1179648 | tf_op jit(solution)/shard_map/reduce_scatter | solution.py:409
  749.0 7.2 collective-permute-start.3
  770.5 128.5 %reduce-scatter.24.cloned.1.call-start = ((), (), s32[]{:S(2)}) async-start(), calls=%async_computation.18 | async-start | bytes 1179648 | tf_op jit(solution)/shard_map/reduce_scatter | solution.py:410
  788.9 145.0 %reduce-scatter.32.cloned.1.call-start = ((), (), s32[]{:S(2)}) async-start(), calls=%async_computation.22 | async-start | bytes 1966080 | tf_op jit(solution)/shard_map/reduce_scatter | solution.py:489
  801.5 134.7 %reduce-scatter.30.cloned.1.call-start = ((), (), s32[]{:S(2)}) async-start(), calls=%async_computation.21 | async-start | bytes 491520 | tf_op jit(solution)/shard_map/reduce_scatter | solution.py:486
  805.2 99.0 %copy-start.128 = (bf16[128,1024]{1,0:T(8,128)(2,1)}, bf16[128,1024]{1,0:T(8,128)(2,1)S(1)}, u32[]{:S(2)}) copy-start(bf16[128,1024]{1,0:T(8,128)(2,1)S(1)} %fusion.124) | copy-start | bytes 786436
  906.5 31.3 %reduce-scatter.28.cloned.1.call-start = ((), (), s32[]{:S(2)}) async-start(), calls=%async_computation.20 | async-start | bytes 491520 | tf_op jit(solution)/shard_map/reduce_scatter | solution.py:483
  907.1 38.0 %reduce-scatter.26.cloned.1.call-start = ((), (), s32[]{:S(2)}) async-start(), calls=%async_computation.19 | async-start | bytes 1966080 | tf_op jit(solution)/shard_map/reduce_scatter | solution.py:480
  909.6 49.6 %reduce-scatter.38.cloned.1.call-start = ((), (), s32[]{:S(2)}) async-start(), calls=%async_computation.25 | async-start | bytes 3932160 | tf_op jit(solution)/shard_map/reduce_scatter | solution.py:498
  914.7 58.7 %reduce-scatter.36.cloned.1.call-start = ((), (), s32[]{:S(2)}) async-start(), calls=%async_computation.24 | async-start | bytes 3932160 | tf_op jit(solution)/shard_map/reduce_scatter | solution.py:495
  933.0 54.5 %reduce-scatter.34.cloned.1.call-start = ((), (), s32[]{:S(2)}) async-start(), calls=%async_computation.23 | async-start | bytes 3932160 | tf_op jit(solution)/shard_map/reduce_scatter | solution.py:492
  933.6 413.0 %all-reduce.16.cloned.1.call-start = ((), (), s32[]{:S(2)}) async-start(), calls=%async_computation.31 | async-start | bytes 22282240 | tf_op jit(solution)/shard_map/psum | solution.py:535
  1033.9 317.9 %copy-start.162 = (bf16[1,2,1,128,640]{4,3,2,1,0:T(8,128)(2,1)}, bf16[1,2,1,128,640]{4,3,2,1,0:T(8,128)(2,1)S(1)}, u32[]{:S(2)}) copy-start(bf16[1,2,1,128,640]{4,3,2,1,0:T(8,128)(2,1)S(1)} %bitcast_dynamic-update-slice_fusion.28) | copy-start | bytes 983044
  (279 other events, 1595.0 us)
Sparse Core Ops, SparseCore 0:
  9.6 12.1 all-gather.27
  23.3 10.8 all-gather.29
  35.7 12.5 all-gather.31
  49.7 12.5 all-gather.33
  63.6 12.5 all-gather.35
  438.3 64.3 reduce-scatter.13
  507.1 62.4 reduce-scatter.15
  601.7 63.9 reduce-scatter.17
  680.8 63.1 reduce-scatter.19
  770.7 61.5 reduce-scatter.21
  836.6 62.3 reduce-scatter.23
  901.7 7.8 reduce-scatter.31
  912.4 8.8 reduce-scatter.29
  923.4 8.8 reduce-scatter.27
  935.1 9.9 reduce-scatter.25
  947.8 11.3 reduce-scatter.37
  961.9 11.4 reduce-scatter.35
  976.1 11.4 reduce-scatter.33
  995.0 351.5 all-reduce.15
where the time goes:
time: 1380 us; the launch traced here: 1370 us
  waiting for transfers between devices  543 us (39%)
  blocking collectives  436 us (32%)
  local copies, waits for them, and re-layouts  133 us (10%)
  matrix products  118 us (9%)
  other arithmetic  105 us (8%)
  between operations  20.4 us (1%)
    psum x1, waiting for transfers between devices, on_device(): lax.psum((part_query, part_key, part_value, part_output, part_gate, part_...  313 us
    reduce_scatter x3, waiting for transfers between devices, on_device(): lax.psum_scatter(value_full, 'ctx', scatter_dimension=1, tiled=True)  153 us
    all_gather x3, blocking collectives, on_device(): lax.all_gather(layer_key_rot, 'ctx', axis=1, tiled=True)  102 us
    all_gather x3, blocking collectives, on_device(): whole_values = lax.all_gather(value_low, 'ctx', axis=1, tiled=True)  101 us
    all_gather x3, blocking collectives, on_device(): lax.all_gather(layer_value_low, 'ctx', axis=1, tiled=True)  98.5 us
    all_gather x3, blocking collectives, on_device(): whole_keys = lax.all_gather(key_rot, 'ctx', axis=1, tiled=True)  97.7 us
    unnamed x605, local copies, waits for them, and re-layouts  41.2 us
  transfers between devices with their start and end apart: 23, of which 11 were waited for; matrix products, arithmetic and copies ran while one was open for 14% of the time, Pallas kernels for 0%

commit v1 on v0

v1 whole, which is shorter than its diff:
```python
import jax
import jax.numpy as jnp
from jax import lax
from jax.sharding import PartitionSpec as P

epsilon = 1e-06
rope_base = 1000000.0
masked = -1e30
score_scale = 0.0625
f32 = jnp.float32
bf16 = jnp.bfloat16


def dot_f32(left, right):
    return jnp.dot(left, right, preferred_element_type=f32)


def dot_nt(left, right):
    return lax.dot_general(left, right, (((1,), (1,)), ((), ())), preferred_element_type=f32)


def dot_tn(left, right):
    return lax.dot_general(left, right, (((0,), (0,)), ((), ())), preferred_element_type=f32)


def norm_factor(values_in):
    return lax.rsqrt(jnp.mean(values_in * values_in, axis=-1, keepdims=True) + epsilon)


def norm_apply(values_in, gain_vec):
    return values_in * norm_factor(values_in) * gain_vec


def norm_back(values_in, gain_vec, grad_out):
    factor = norm_factor(values_in)
    scaled = grad_out * gain_vec
    grad_in = factor * (
        scaled - values_in * factor * factor * jnp.mean(scaled * values_in, axis=-1, keepdims=True)
    )
    grad_gain = jnp.sum((grad_out * values_in * factor).reshape(-1, values_in.shape[-1]), axis=0)
    return (grad_in, grad_gain)


def rotate(values_in, cos_table, sin_table):
    half_width = values_in.shape[-1] // 2
    former = values_in[..., :half_width]
    latter = values_in[..., half_width:]
    return jnp.concatenate(
        [former * cos_table - latter * sin_table, latter * cos_table + former * sin_table], axis=-1
    )


def unrotate(grad_in, cos_table, sin_table):
    return rotate(grad_in, cos_table, -sin_table)


def gelu_fn(values_in):
    return jax.nn.gelu(values_in, approximate=True)


def rotation_tables(positions, half_width):
    frequency = rope_base ** (-jnp.arange(half_width, dtype=f32) / half_width)
    angles = positions.astype(f32)[:, None] * frequency[None, :]
    return (jnp.cos(angles), jnp.sin(angles))


def xor_permute(shard, axis, mask):
    count = lax.axis_size(axis)
    return lax.ppermute(shard, axis, [(i, i ^ mask) for i in range(count)])


def small_ctx():
    return lax.axis_size("ctx") == 8


def ctx_order():
    count = lax.axis_size("ctx")
    slots = jnp.arange(count, dtype=jnp.int32)
    if small_ctx():
        return lax.axis_index("ctx") ^ slots
    return slots


def gather_ctx(shard):
    if not small_ctx():
        return lax.all_gather(shard, "ctx", axis=0)
    blocks = [None] * 8
    blocks[0] = shard
    for mask in (6, 4, 2):
        blocks[mask] = xor_permute(shard, "ctx", mask)
    for mask in (0, 2, 4, 6):
        blocks[mask + 1] = xor_permute(blocks[mask], "ctx", 1)
    return jnp.stack(blocks)


def scatter_ctx(parts):
    if not small_ctx():
        return lax.psum_scatter(parts.astype(f32), "ctx", scatter_dimension=0, tiled=False)
    sums = {}
    for mask in (6, 4, 2, 0):
        came = xor_permute(parts[mask + 1], "ctx", 1)
        sums[mask] = parts[mask].astype(f32) + came.astype(f32)
    total = sums[0]
    for mask in (6, 4, 2):
        low = lax.optimization_barrier(sums[mask].astype(bf16))
        total = total + xor_permute(low, "ctx", mask).astype(f32)
    return total


def sum_ctx(shard):
    if not small_ctx():
        return lax.psum(shard.astype(f32), "ctx")
    ctx_index = lax.axis_index("ctx")
    y_index = ctx_index & 1
    z_index = ctx_index >> 1
    half = shard.shape[0] // 2
    keep = lax.dynamic_slice_in_dim(shard, y_index * half, half, 0)
    send = lax.dynamic_slice_in_dim(shard, (1 - y_index) * half, half, 0)
    came = xor_permute(send, "ctx", 1)
    inward = [(z * 2 + y, t * 2 + y) for z, t in ((0, 1), (3, 2)) for y in (0, 1)]
    middle = [(z * 2 + y, t * 2 + y) for z, t in ((1, 2), (2, 1)) for y in (0, 1)]
    outward = [(z * 2 + y, t * 2 + y) for z, t in ((1, 0), (2, 3)) for y in (0, 1)]

    def add(left, right):
        return lax.optimization_barrier((left.astype(f32) + right.astype(f32)).astype(bf16))

    part = add(keep, came)
    part = add(part, lax.ppermute(part, "ctx", inward))
    part = add(part, lax.ppermute(part, "ctx", middle))
    back = lax.ppermute(part, "ctx", outward)
    total = jnp.where((z_index == 1) | (z_index == 2), part, back)
    other = xor_permute(total, "ctx", 1)
    first = jnp.where(y_index == 0, total, other)
    second = jnp.where(y_index == 0, other, total)
    return jnp.concatenate([first, second], axis=0).astype(f32)


def gather_fsdp(shard):
    other = xor_permute(shard, "fsdp", 1)
    is_first = lax.axis_index("fsdp") == 0
    return jnp.concatenate(
        [jnp.where(is_first, shard, other), jnp.where(is_first, other, shard)], axis=0
    )


def scatter_fsdp(terms):
    half = terms.shape[0] // 2
    fsdp_index = lax.axis_index("fsdp")
    keep = lax.dynamic_slice_in_dim(terms, fsdp_index * half, half, 0)
    send = lax.dynamic_slice_in_dim(terms, (1 - fsdp_index) * half, half, 0)
    came = xor_permute(send.astype(bf16), "fsdp", 1)
    return (keep.astype(f32) + came.astype(f32)).astype(bf16)


def on_device(
    inputs,
    out_cotangent,
    block_order,
    w_query,
    w_key,
    w_value,
    w_output,
    w_gate,
    w_up,
    w_down,
    g_input,
    g_query,
    g_key,
    g_post_attn,
    g_pre_ffw,
    g_post_ffw,
):
    section_index = lax.axis_index("section")
    ctx_index = lax.axis_index("ctx")
    micro_count, seq_local, tokens, model_width = inputs.shape
    groups = micro_count * seq_local
    rows = groups * tokens
    block_len = tokens // 2
    gains_own = jnp.concatenate(
        [g_input[0], g_post_attn[0], g_pre_ffw[0], g_post_ffw[0], g_query[0], g_key[0]]
    )
    w_kv_own = jnp.concatenate([w_key[0], w_value[0]], axis=1)
    gains_other = xor_permute(gains_own.reshape(1, -1), "fsdp", 1)
    gains_pair = jnp.stack([gains_own, gains_other[0]])
    gains_pair = jnp.where(lax.axis_index("fsdp") == 0, gains_pair, gains_pair[::-1])
    w_kv = gather_fsdp(w_kv_own)
    w_q = gather_fsdp(w_query[0])
    w_out = gather_fsdp(w_output[0])
    w_ffw_in = gather_fsdp(jnp.concatenate([w_gate[0], w_up[0]], axis=1))
    w_dn = gather_fsdp(w_down[0])
    half_model = model_width // 2
    gains = gains_pair.astype(f32)
    gain_input = gains[:, :half_model].reshape(-1)
    gain_attn = gains[:, half_model : 2 * half_model].reshape(-1)
    gain_pre = gains[:, 2 * half_model : 3 * half_model].reshape(-1)
    gain_post = gains[:, 3 * half_model : 4 * half_model].reshape(-1)
    half_head = g_query.shape[1]
    gain_query = gains[:, 4 * half_model : 4 * half_model + half_head].reshape(-1)
    gain_key = gains[:, 4 * half_model + half_head :].reshape(-1)
    head_dim = 2 * half_head
    query_cols = w_out.shape[0]
    head_count = query_cols // head_dim
    ff_width = w_dn.shape[0]
    ctx_size = lax.axis_size("ctx")
    order = ctx_order()
    slot_pairs = block_order.reshape(ctx_size, 2)
    offsets = jnp.arange(block_len, dtype=jnp.int32)

    def spread(slot_ids):
        return (slot_ids.reshape(-1)[:, None] * block_len + offsets[None, :]).reshape(-1)

    local_pos = spread(slot_pairs[ctx_index])
    key_pos = spread(slot_pairs[order])
    cos_table, sin_table = rotation_tables(local_pos, head_dim // 2)
    query_pos = jnp.tile(local_pos, head_count)
    allowed = key_pos[None, None, :] <= query_pos[None, :, None]

    def to_heads(flat):
        split = flat.reshape(groups, tokens, head_count, head_dim)
        return jnp.transpose(split, (0, 2, 1, 3)).reshape(groups, head_count * tokens, head_dim)

    def from_heads(stacked):
        split = stacked.reshape(groups, head_count, tokens, head_dim)
        return jnp.transpose(split, (0, 2, 1, 3)).reshape(rows, query_cols)

    def forward(hidden):
        normed = norm_apply(hidden, gain_input).astype(bf16)
        kv_lin = dot_f32(normed, w_kv)
        key_lin = kv_lin[:, :head_dim]
        key_rot = rotate(
            norm_apply(key_lin, gain_key).reshape(groups, tokens, head_dim), cos_table, sin_table
        ).reshape(rows, head_dim)
        kv_low = jnp.concatenate([key_rot, kv_lin[:, head_dim:]], axis=1).astype(bf16)
        kv_all = gather_ctx(kv_low.reshape(groups, tokens, 2 * head_dim))
        kv_all = jnp.transpose(kv_all, (1, 0, 2, 3)).reshape(
            groups, ctx_size * tokens, 2 * head_dim
        )
        query_lin = dot_f32(normed, w_q).reshape(groups, tokens, head_count, head_dim)
        query_rot = rotate(
            norm_apply(query_lin, gain_query), cos_table[:, None, :], sin_table[:, None, :]
        ).astype(bf16)
        query_rows = to_heads(query_rot)
        keys = kv_all[:, :, :head_dim]
        values = kv_all[:, :, head_dim:]
        scores = (
            jnp.einsum("sqd,skd->sqk", query_rows, keys, preferred_element_type=f32) * score_scale
        )
        scores = jnp.where(allowed, scores, masked)
        row_max = jnp.max(scores, axis=-1, keepdims=True)
        weights = jnp.exp(scores - row_max)
        row_total = jnp.sum(weights, axis=-1, keepdims=True)
        attn_rows = (
            jnp.einsum("sqk,skd->sqd", weights.astype(bf16), values, preferred_element_type=f32)
            / row_total
        )
        log_total = row_max + jnp.log(row_total)
        attn_low = from_heads(attn_rows).astype(bf16)
        branch = dot_f32(attn_low, w_out)
        middle = hidden + norm_apply(branch, gain_attn)
        pre_ffw = norm_apply(middle, gain_pre).astype(bf16)
        gate_up = dot_f32(pre_ffw, w_ffw_in)
        hidden_ffw = (gelu_fn(gate_up[:, :ff_width]) * gate_up[:, ff_width:]).astype(bf16)
        down_out = dot_f32(hidden_ffw, w_dn)
        result = (middle + norm_apply(down_out, gain_post)).astype(bf16)
        saved = (
            hidden,
            normed,
            query_lin,
            key_lin,
            query_rows,
            kv_all,
            attn_rows,
            log_total,
            attn_low,
            branch,
            middle,
            pre_ffw,
            gate_up,
            hidden_ffw,
            down_out,
        )
        return (result, saved)

    def backward(grad_flat, saved):
        (
            hidden,
            normed,
            query_lin,
            key_lin,
            query_rows,
            kv_all,
            attn_rows,
            log_total,
            attn_low,
            branch,
            middle,
            pre_ffw,
            gate_up,
            hidden_ffw,
            down_out,
        ) = saved
        down_part, grad_gain_post = norm_back(down_out, gain_post, grad_flat)
        down_grad = down_part.astype(bf16)
        ffw_grad = dot_nt(down_grad, w_dn)
        activated, gelu_back = jax.vjp(gelu_fn, gate_up[:, :ff_width])
        gate_grad = gelu_back(ffw_grad * gate_up[:, ff_width:])[0]
        gate_up_grad = jnp.concatenate([gate_grad, ffw_grad * activated], axis=1).astype(bf16)
        pre_grad = dot_nt(gate_up_grad, w_ffw_in)
        middle_part, grad_gain_pre = norm_back(middle, gain_pre, pre_grad)
        middle_grad = grad_flat + middle_part
        branch_part, grad_gain_attn = norm_back(branch, gain_attn, middle_grad)
        branch_grad = branch_part.astype(bf16)
        attn_grad = dot_nt(branch_grad, w_out).astype(bf16)
        grad_rows = to_heads(attn_grad)
        row_delta = jnp.sum(grad_rows.astype(f32) * attn_rows, axis=-1, keepdims=True)
        key_rows = kv_all.shape[1]
        span = tokens * min(8, ctx_size)

        def span_grads(start, query_grad):
            kv_part = lax.dynamic_slice_in_dim(kv_all, start, span, 1)
            keys = kv_part[:, :, :head_dim]
            values = kv_part[:, :, head_dim:]
            seen = lax.dynamic_slice_in_dim(key_pos, start, span, 0)[None, None, :]
            scores = (
                jnp.einsum("sqd,skd->sqk", query_rows, keys, preferred_element_type=f32)
                * score_scale
            )
            probs = jnp.exp(
                jnp.where(seen <= query_pos[None, :, None], scores - log_total, masked)
            )
            prob_grad = jnp.einsum(
                "sqd,skd->sqk", grad_rows, values, preferred_element_type=f32
            )
            score_grad = (probs * (prob_grad - row_delta)).astype(bf16)
            query_part = (
                jnp.einsum("sqk,skd->sqd", score_grad, keys, preferred_element_type=f32)
                * score_scale
            )
            key_part = (
                jnp.einsum("sqk,sqd->skd", score_grad, query_rows, preferred_element_type=f32)
                * score_scale
            )
            value_part = jnp.einsum(
                "sqk,sqd->skd", probs.astype(bf16), grad_rows, preferred_element_type=f32
            )
            both = jnp.concatenate([key_part, value_part], axis=2).astype(bf16)
            return (query_grad + query_part, both)

        query_zero = jnp.zeros(query_rows.shape, f32)
        if key_rows == span:
            query_grad, kv_parts = span_grads(0, query_zero)
        else:

            def one_span(index, state):
                query_sum, all_parts = state
                query_sum, both = span_grads(index * span, query_sum)
                return (
                    query_sum,
                    lax.dynamic_update_slice_in_dim(all_parts, both, index * span, 1),
                )

            query_grad, kv_parts = lax.fori_loop(
                0, key_rows // span, one_span, (query_zero, jnp.zeros(kv_all.shape, bf16))
            )
        kv_parts = jnp.transpose(
            kv_parts.reshape(groups, ctx_size, tokens, 2 * head_dim), (1, 0, 2, 3)
        )
        kv_grad = scatter_ctx(kv_parts).reshape(rows, 2 * head_dim)
        query_tok_grad = from_heads(query_grad).reshape(groups, tokens, head_count, head_dim)
        query_lin_grad, grad_gain_query = norm_back(
            query_lin,
            gain_query,
            unrotate(query_tok_grad, cos_table[:, None, :], sin_table[:, None, :]),
        )
        key_lin_grad, grad_gain_key = norm_back(
            key_lin,
            gain_key,
            unrotate(
                kv_grad[:, :head_dim].reshape(groups, tokens, head_dim), cos_table, sin_table
            ).reshape(rows, head_dim),
        )
        query_low = query_lin_grad.reshape(rows, query_cols).astype(bf16)
        kv_grad_low = jnp.concatenate([key_lin_grad, kv_grad[:, head_dim:]], axis=1).astype(bf16)
        normed_grad = dot_nt(query_low, w_q) + dot_nt(kv_grad_low, w_kv)
        input_part, grad_gain_input = norm_back(hidden, gain_input, normed_grad)
        input_grad = (middle_grad + input_part).astype(bf16)

        def weight_grads():
            return (
                dot_tn(hidden_ffw, down_grad),
                dot_tn(pre_ffw, gate_up_grad),
                dot_tn(attn_low, branch_grad),
                dot_tn(normed, jnp.concatenate([query_low, kv_grad_low], axis=1)),
                (
                    grad_gain_input,
                    grad_gain_attn,
                    grad_gain_pre,
                    grad_gain_post,
                    grad_gain_query,
                    grad_gain_key,
                ),
            )

        return (input_grad, weight_grads)

    own_input = inputs.reshape(rows, model_width)
    first_result, _ = forward(own_input.astype(f32))
    received = lax.ppermute(first_result, "section", [(0, 1)])
    hidden = jnp.where(section_index == 0, own_input, received)
    result, saved = forward(hidden.astype(f32))
    own_grad = out_cotangent.reshape(rows, model_width)
    first_grad, _ = backward(own_grad.astype(f32), saved)
    grad_received = lax.ppermute(first_grad, "section", [(1, 0)])
    grad_in = jnp.where(section_index == 1, own_grad, grad_received)
    input_grad, weight_grads = backward(grad_in.astype(f32), saved)
    grad_down, grad_ffw, grad_out, grad_qkv, grad_gains = weight_grads()
    sum_down = sum_ctx(scatter_fsdp(grad_down))
    sum_gate = sum_ctx(scatter_fsdp(grad_ffw[:, :ff_width]))
    sum_up = sum_ctx(scatter_fsdp(grad_ffw[:, ff_width:]))
    sum_out = sum_ctx(scatter_fsdp(grad_out))
    gain_rows = jnp.concatenate([member.reshape(2, -1) for member in grad_gains], axis=1)
    width = gain_rows.shape[1]
    pad = jnp.zeros((2, 31, width), f32)
    gain_rows = jnp.concatenate([gain_rows[:, None, :], pad], axis=1)
    tail = jnp.concatenate(
        [grad_qkv[:half_model], gain_rows[0], grad_qkv[half_model:], gain_rows[1]], axis=0
    )
    sum_tail = sum_ctx(scatter_fsdp(tail))
    sum_query = sum_tail[:half_model, :query_cols]
    sum_key = sum_tail[:half_model, query_cols : query_cols + head_dim]
    sum_value = sum_tail[:half_model, query_cols + head_dim :]
    sum_gains = sum_tail[half_model]
    cuts = [0]
    for member in grad_gains:
        cuts.append(cuts[-1] + member.shape[0] // 2)
    gain_parts = [sum_gains[cuts[i] : cuts[i + 1]] for i in range(6)]
    shape = (micro_count, seq_local, tokens, model_width)
    members = (
        sum_query,
        sum_key,
        sum_value,
        sum_out,
        sum_gate,
        sum_up,
        sum_down,
        gain_parts[0],
        gain_parts[4],
        gain_parts[5],
        gain_parts[1],
        gain_parts[2],
        gain_parts[3],
    )
    return (result.reshape(shape)[None], input_grad.reshape(shape)[None]) + tuple(
        member[None] for member in members
    )


def solution(mesh):
    weight = P("section", "fsdp", None)
    gain = P("section", "fsdp")
    in_specs = (
        (P(None, "fsdp", "ctx", None),) * 2 + (P(),) + (weight,) * 7 + (gain,) * 6
    )
    out_specs = (
        (P("section", None, "fsdp", "ctx", None),) * 2 + (weight,) * 7 + (gain,) * 6
    )
    return jax.shard_map(
        on_device, mesh=mesh, in_specs=in_specs, out_specs=out_specs, check_vma=False
    )
```

time: 1380 us -> 535 us (0.39)
  the two profiles are of different devices: /device:TPU:0 before, /device:TPU:12 now
where the time goes in v1:
time: 535 us; the launch traced here: 528 us
  waiting for transfers between devices  226 us (42%)
  starting transfers between devices  76.4 us (14%)
  local copies, waits for them, and re-layouts  76.2 us (14%)
  matrix products  73.4 us (14%)
  other arithmetic  72.9 us (14%)
    ppermute x49, waiting for transfers between devices, xor_permute(): return lax.ppermute(shard, axis, [(i, i ^ mask) for i in range(count)])  148 us
    ppermute x49, starting transfers between devices, xor_permute(): return lax.ppermute(shard, axis, [(i, i ^ mask) for i in range(count)])  42.9 us
    ppermute x5, waiting for transfers between devices, sum_ctx(): part = add(part, lax.ppermute(part, 'ctx', middle))  36.3 us
    dot_general x10, matrix products, dot_nt(): lax.dot_general(left, right, (((1,), (1,)), ((), ())), preferred_element_...  30.1 us
    unnamed x326, local copies, waits for them, and re-layouts  26.9 us
    ppermute x5, waiting for transfers between devices, sum_ctx(): back = lax.ppermute(part, 'ctx', outward)  20.7 us
    ppermute x5, starting transfers between devices, sum_ctx(): part = add(part, lax.ppermute(part, 'ctx', middle))  15.1 us
    dot_general x4, matrix products, dot_tn(): lax.dot_general(left, right, (((0,), (0,)), ((), ())), preferred_element_...  11.7 us
  transfers between devices with their start and end apart: 66, of which 36 were waited for; matrix products, arithmetic and copies ran while one was open for 19% of the time, Pallas kernels for 0%

profile of v1, /device:TPU:12, one launch (start us, length us, event | category | flops | bytes accessed | tf_op | source)
XLA Modules:
  0.0 528.4 jit_solution(3758319999007152863)
XLA Ops:
  20.0 6.4 %collective-permute-done.3 = bf16[2,128,512]{2,1,0:T(8,128)(2,1)} collective-permute-done((bf16[2,128,512]{2,1,0:T(8,128)(2,1)}, bf16[2,128,512]{2,1,0:T(8,128)(2,1)}, u32[]{:S(2)}, u32[]{:S(2)}) %collective-permute-start.3) | collective-permute-done | bytes 262176 | tf_op jit(solution)/shard_map/ppermute | solution.py:69
  37.5 10.3 %collective-permute-done.6 = bf16[2,128,512]{2,1,0:T(8,128)(2,1)} collective-permute-done((bf16[2,128,512]{2,1,0:T(8,128)(2,1)}, bf16[2,128,512]{2,1,0:T(8,128)(2,1)}, u32[]{:S(2)}, u32[]{:S(2)}) %collective-permute-start.6) | collective-permute-done | bytes 262176 | tf_op jit(solution)/shard_map/ppermute | solution.py:69
  49.2 4.1 collective-permute-done.8
  57.8 4.9 collective-permute-done.7
  82.0 3.8 collective-permute-start.13
  86.5 5.4 %collective-permute-done.13 = bf16[256,640]{1,0:T(8,128)(2,1)S(1)} collective-permute-done((bf16[256,640]{1,0:T(8,128)(2,1)S(1)}, bf16[256,640]{1,0:T(8,128)(2,1)S(1)}, u32[]{:S(2)}, u32[]{:S(2)}) %collective-permute-start.13) | collective-permute-done | bytes 327712 | tf_op jit(solution)/shard_map/ppermute | solution.py:408
  95.5 3.9 collective-permute-start.17
  109.6 6.8 %collective-permute-done.17 = bf16[2,128,512]{2,1,0:T(8,128)(2,1)} collective-permute-done((bf16[2,128,512]{2,1,0:T(8,128)(2,1)}, bf16[2,128,512]{2,1,0:T(8,128)(2,1)}, u32[]{:S(2)}, u32[]{:S(2)}) %collective-permute-start.17) | collective-permute-done | bytes 262176 | tf_op jit(solution)/shard_map/ppermute | solution.py:69
  145.2 12.9 %add_convert_fusion.5 = (bf16[256,2048]{1,0:T(8,128)(2,1)S(1)}, bf16[256,2048]{1,0:T(8,128)(2,1)S(1)}) fusion(f32[256,4096]{1,0:T(8,128)S(1)} %fusion.170, bf16[1024,640]{1,0:T(8,128)(2,1)S(1)} %copy-done.67, bf16[1024,640]{1,0:T(8,128)(2,1)S(1)} %copy-done.64, bf16[256,640]{1,0:T(8,128)(2,1)S(1)} %bitcast.334, f32[256,640]{1,0:T(8,128)S(1)} %get-tuple-element.196, ...), kind=kOutput, calls=%fused_computation.60 | convolution fusion | flops 690225152 | bytes 9900544 | tf_op jit(solution)/shard_map/dot_general | solution.py:19
  180.7 5.0 collective-permute-done.22
  185.8 5.6 %collective-permute-done.24 = bf16[2,128,512]{2,1,0:T(8,128)(2,1)S(1)} collective-permute-done((bf16[2,128,512]{2,1,0:T(8,128)(2,1)S(1)}, bf16[2,128,512]{2,1,0:T(8,128)(2,1)S(1)}, u32[]{:S(2)}, u32[]{:S(2)}) %collective-permute-start.24) | collective-permute-done | bytes 262176 | tf_op jit(solution)/shard_map/ppermute | solution.py:69
  191.4 5.6 %collective-permute-done.26 = bf16[2,128,512]{2,1,0:T(8,128)(2,1)S(1)} collective-permute-done((bf16[2,128,512]{2,1,0:T(8,128)(2,1)S(1)}, bf16[2,128,512]{2,1,0:T(8,128)(2,1)S(1)}, u32[]{:S(2)}, u32[]{:S(2)}) %collective-permute-start.26) | collective-permute-done | bytes 262176 | tf_op jit(solution)/shard_map/ppermute | solution.py:69
  205.1 6.7 %collective-permute-done.23 = bf16[2,128,512]{2,1,0:T(8,128)(2,1)} collective-permute-done((bf16[2,128,512]{2,1,0:T(8,128)(2,1)}, bf16[2,128,512]{2,1,0:T(8,128)(2,1)}, u32[]{:S(2)}, u32[]{:S(2)}) %collective-permute-start.23) | collective-permute-done | bytes 262176 | tf_op jit(solution)/shard_map/ppermute | solution.py:69
  221.4 6.0 %collective-permute-done.28 = bf16[256,640]{1,0:T(8,128)(2,1)} collective-permute-done((bf16[256,640]{1,0:T(8,128)(2,1)}, bf16[256,640]{1,0:T(8,128)(2,1)}, u32[]{:S(2)}, u32[]{:S(2)}) %collective-permute-start.28) | collective-permute-done | bytes 327712 | tf_op jit(solution)/shard_map/ppermute | solution.py:413
  231.2 6.4 %add_convert_fusion.4 = (bf16[256,2048]{1,0:T(8,128)(2,1)S(1)}, bf16[256,2048]{1,0:T(8,128)(2,1)S(1)}) fusion(f32[256,4096]{1,0:T(8,128)} %copy-done.28, bf16[256,640]{1,0:T(8,128)(2,1)S(1)} %get-tuple-element.155, bf16[1024,640]{1,0:T(8,128)(2,1)S(1)} %copy-done.68, bf16[1024,640]{1,0:T(8,128)(2,1)S(1)} %copy-done.65), kind=kOutput, calls=%fused_computation.57 | convolution fusion | flops 688914432 | bytes 9240576 | tf_op jit(solution)/shard_map/dot_general | solution.py:19
  264.9 5.5 %fusion.36 = f32[640,4096]{1,0:T(8,128)} fusion(bf16[256,2048]{1,0:T(8,128)(2,1)S(1)} %copy-done.76, bf16[256,2048]{1,0:T(8,128)(2,1)S(1)} %copy-done.74, f32[256,640]{1,0:T(8,128)S(1)} %get-tuple-element.92, f32[256]{0:T(256)S(1)} %add_rsqrt_fusion.3, f32[640]{0:T(1024)S(1)} %mul.1228), kind=kOutput, calls=%fused_computation.84 | convolution fusion | flops 1346863104 | bytes 13241856 | tf_op jit(solution)/shard_map/dot_general | solution.py:23
  286.5 4.7 fusion.182
  303.5 4.3 collective-permute-start.33
  314.2 8.1 %collective-permute-done.31 = bf16[2,128,512]{2,1,0:T(8,128)(2,1)} collective-permute-done((bf16[2,128,512]{2,1,0:T(8,128)(2,1)}, bf16[2,128,512]{2,1,0:T(8,128)(2,1)}, u32[]{:S(2)}, u32[]{:S(2)}) %collective-permute-start.31) | collective-permute-done | bytes 262176 | tf_op jit(solution)/shard_map/ppermute | solution.py:69
  339.1 8.0 %collective-permute-done.43 = bf16[256,640]{1,0:T(8,128)(2,1)S(1)} collective-permute-done((bf16[256,640]{1,0:T(8,128)(2,1)S(1)}, bf16[256,640]{1,0:T(8,128)(2,1)S(1)}, u32[]{:S(2)}, u32[]{:S(2)}) %collective-permute-start.43) | collective-permute-done | bytes 327712 | tf_op jit(solution)/shard_map/ppermute | solution.py:69
  362.8 5.4 %collective-permute-done.45 = bf16[256,640]{1,0:T(8,128)(2,1)S(1)} collective-permute-done((bf16[256,640]{1,0:T(8,128)(2,1)S(1)}, bf16[256,640]{1,0:T(8,128)(2,1)S(1)}, u32[]{:S(2)}, u32[]{:S(2)}) %collective-permute-start.45) | collective-permute-done | bytes 327712 | tf_op jit(solution)/shard_map/ppermute | solution.py:129
  371.2 11.2 %collective-permute-done.55 = bf16[160,2048]{1,0:T(8,128)(2,1)S(1)} collective-permute-done((bf16[160,2048]{1,0:T(8,128)(2,1)S(1)}, bf16[160,2048]{1,0:T(8,128)(2,1)S(1)}, u32[]{:S(2)}, u32[]{:S(2)}) %collective-permute-start.55) | collective-permute-done | bytes 655392 | tf_op jit(solution)/shard_map/ppermute | solution.py:69
  383.8 12.5 %collective-permute-done.49 = bf16[160,2048]{1,0:T(8,128)(2,1)S(1)} collective-permute-done((bf16[160,2048]{1,0:T(8,128)(2,1)S(1)}, bf16[160,2048]{1,0:T(8,128)(2,1)S(1)}, u32[]{:S(2)}, u32[]{:S(2)}) %collective-permute-start.49) | collective-permute-done | bytes 655392 | tf_op jit(solution)/shard_map/ppermute | solution.py:69
  398.6 9.3 %collective-permute-done.37 = bf16[176,1536]{1,0:T(8,128)(2,1)S(1)} collective-permute-done((bf16[176,1536]{1,0:T(8,128)(2,1)S(1)}, bf16[176,1536]{1,0:T(8,128)(2,1)S(1)}, u32[]{:S(2)}, u32[]{:S(2)}) %collective-permute-start.37) | collective-permute-done | bytes 540704 | tf_op jit(solution)/shard_map/ppermute | solution.py:69
  416.7 8.8 %collective-permute-done.38 = bf16[176,1536]{1,0:T(8,128)(2,1)S(1)} collective-permute-done((bf16[176,1536]{1,0:T(8,128)(2,1)S(1)}, bf16[176,1536]{1,0:T(8,128)(2,1)S(1)}, u32[]{:S(2)}, u32[]{:S(2)}) %collective-permute-start.38) | collective-permute-done | bytes 540704 | tf_op jit(solution)/shard_map/ppermute | solution.py:128
  435.6 10.0 %collective-permute-done.39 = bf16[176,1536]{1,0:T(8,128)(2,1)S(1)} collective-permute-done((bf16[176,1536]{1,0:T(8,128)(2,1)S(1)}, bf16[176,1536]{1,0:T(8,128)(2,1)S(1)}, u32[]{:S(2)}, u32[]{:S(2)}) %collective-permute-start.39) | collective-permute-done | bytes 540704 | tf_op jit(solution)/shard_map/ppermute | solution.py:129
  448.7 11.1 %collective-permute-done.57 = bf16[160,2048]{1,0:T(8,128)(2,1)S(1)} collective-permute-done((bf16[160,2048]{1,0:T(8,128)(2,1)S(1)}, bf16[160,2048]{1,0:T(8,128)(2,1)S(1)}, u32[]{:S(2)}, u32[]{:S(2)}) %collective-permute-start.57) | collective-permute-done | bytes 655392 | tf_op jit(solution)/shard_map/ppermute | solution.py:129
  461.3 9.7 %collective-permute-done.51 = bf16[160,2048]{1,0:T(8,128)(2,1)S(1)} collective-permute-done((bf16[160,2048]{1,0:T(8,128)(2,1)S(1)}, bf16[160,2048]{1,0:T(8,128)(2,1)S(1)}, u32[]{:S(2)}, u32[]{:S(2)}) %collective-permute-start.51) | collective-permute-done | bytes 655392 | tf_op jit(solution)/shard_map/ppermute | solution.py:129
  474.9 13.1 %collective-permute-done.58 = bf16[160,2048]{1,0:T(8,128)(2,1)S(1)} collective-permute-done((bf16[160,2048]{1,0:T(8,128)(2,1)S(1)}, bf16[160,2048]{1,0:T(8,128)(2,1)S(1)}, u32[]{:S(2)}, u32[]{:S(2)}) %collective-permute-start.58) | collective-permute-done | bytes 655392 | tf_op jit(solution)/shard_map/ppermute | solution.py:130
  488.7 7.1 %collective-permute-done.52 = bf16[160,2048]{1,0:T(8,128)(2,1)S(1)} collective-permute-done((bf16[160,2048]{1,0:T(8,128)(2,1)S(1)}, bf16[160,2048]{1,0:T(8,128)(2,1)S(1)}, u32[]{:S(2)}, u32[]{:S(2)}) %collective-permute-start.52) | collective-permute-done | bytes 655392 | tf_op jit(solution)/shard_map/ppermute | solution.py:130
  503.7 12.3 %collective-permute-done.59 = bf16[160,2048]{1,0:T(8,128)(2,1)S(1)} collective-permute-done((bf16[160,2048]{1,0:T(8,128)(2,1)S(1)}, bf16[160,2048]{1,0:T(8,128)(2,1)S(1)}, u32[]{:S(2)}, u32[]{:S(2)}) %collective-permute-start.59) | collective-permute-done | bytes 655392 | tf_op jit(solution)/shard_map/ppermute | solution.py:69
  517.9 8.5 %collective-permute-done.53 = bf16[160,2048]{1,0:T(8,128)(2,1)S(1)} collective-permute-done((bf16[160,2048]{1,0:T(8,128)(2,1)S(1)}, bf16[160,2048]{1,0:T(8,128)(2,1)S(1)}, u32[]{:S(2)}, u32[]{:S(2)}) %collective-permute-start.53) | collective-permute-done | bytes 655392 | tf_op jit(solution)/shard_map/ppermute | solution.py:69
  (676 shorter events, 281.3 us)
Async XLA Ops:
  6.5 24.6 %collective-permute-start.1 = (bf16[320,1024]{1,0:T(8,128)(2,1)}, bf16[320,1024]{1,0:T(8,128)(2,1)S(1)}, u32[]{:S(2)}, u32[]{:S(2)}) collective-permute-start(bf16[320,1024]{1,0:T(8,128)(2,1)} %bitcast.353), channel_id=1, source_target_pairs={{0,1},{1,0},{2,3},{3,2},{4,5},{5,4},{6,7},{7,6},{8,9},{9,8},{10,11... | collective-permute-start | bytes 1966088 | tf_op jit(solution)/shard_map/ppermute | solution.py:69
  6.6 48.2 %collective-permute-start.10 = (bf16[512,640]{1,0:T(8,128)(2,1)}, bf16[512,640]{1,0:T(8,128)(2,1)}, u32[]{:S(2)}, u32[]{:S(2)}) collective-permute-start(bf16[512,640]{1,0:T(8,128)(2,1)} %bitcast.354), channel_id=1, source_target_pairs={{0,1},{1,0},{2,3},{3,2},{4,5},{5,4},{6,7},{7,6},{8,9},{9,8},{10,11... | collective-permute-start | bytes 1966088 | tf_op jit(solution)/shard_map/ppermute | solution.py:69
  10.6 64.0 %collective-permute-start.11 = (bf16[320,4096]{1,0:T(8,128)(2,1)}, bf16[320,4096]{1,0:T(8,128)(2,1)}, u32[]{:S(2)}, u32[]{:S(2)}) collective-permute-start(bf16[320,4096]{1,0:T(8,128)(2,1)} %pad_maximum_fusion.2), channel_id=1, source_target_pairs={{0,1},{1,0},{2,3},{3,2},{4,5},{5,4},{6,7},{7,6},{8,9},{9,8},{10,11... | collective-permute-start | bytes 7864328 | tf_op jit(solution)/shard_map/ppermute | solution.py:69
  26.4 46.1 %collective-permute-start.12 = (bf16[1024,640]{1,0:T(8,128)(2,1)}, bf16[1024,640]{1,0:T(8,128)(2,1)}, u32[]{:S(2)}, u32[]{:S(2)}) collective-permute-start(bf16[1024,640]{1,0:T(8,128)(2,1)} %bitcast.38), channel_id=1, source_target_pairs={{0,1},{1,0},{2,3},{3,2},{4,5},{5,4},{6,7},{7,6},{8,9},{9,8},{10,11... | collective-permute-start | bytes 3932168 | tf_op jit(solution)/shard_map/ppermute | solution.py:69
  94.1 27.0 %collective-permute-start.14 = (bf16[2,128,512]{2,1,0:T(8,128)(2,1)}, bf16[2,128,512]{2,1,0:T(8,128)(2,1)}, u32[]{:S(2)}, u32[]{:S(2)}) collective-permute-start(bf16[2,128,512]{2,1,0:T(8,128)(2,1)} %pad_maximum_fusion.18), channel_id=1, source_target_pairs={{0,2},{2,0},{4,6},{6,4},{8,10},{10,8},{12,14},{14,12},{1,3},{3,1},... | collective-permute-start | bytes 786440 | tf_op jit(solution)/shard_map/ppermute | solution.py:69
  99.5 21.0 %collective-permute-start.19 = (bf16[2,128,512]{2,1,0:T(8,128)(2,1)}, bf16[2,128,512]{2,1,0:T(8,128)(2,1)}, u32[]{:S(2)}, u32[]{:S(2)}) collective-permute-start(bf16[2,128,512]{2,1,0:T(8,128)(2,1)} %pad_maximum_fusion.18), channel_id=1, source_target_pairs={{0,12},{2,14},{4,8},{6,10},{8,4},{10,6},{12,0},{14,2},{1,13},{3,15... | collective-permute-start | bytes 786440 | tf_op jit(solution)/shard_map/ppermute | solution.py:69
  179.2 25.9 %collective-permute-start.21 = (bf16[2,128,512]{2,1,0:T(8,128)(2,1)}, bf16[2,128,512]{2,1,0:T(8,128)(2,1)}, u32[]{:S(2)}, u32[]{:S(2)}) collective-permute-start(bf16[2,128,512]{2,1,0:T(8,128)(2,1)} %get-tuple-element.118), channel_id=1, source_target_pairs={{0,2},{2,0},{4,6},{6,4},{8,10},{10,8},{12,14},{14,12},{1,3},{3,1},... | collective-permute-start | bytes 786440 | tf_op jit(solution)/shard_map/ppermute | solution.py:69
  282.1 32.0 %collective-permute-start.29 = (bf16[2,128,512]{2,1,0:T(8,128)(2,1)}, bf16[2,128,512]{2,1,0:T(8,128)(2,1)}, u32[]{:S(2)}, u32[]{:S(2)}) collective-permute-start(bf16[2,128,512]{2,1,0:T(8,128)(2,1)} %get-tuple-element.111), channel_id=1, source_target_pairs={{0,2},{2,0},{4,6},{6,4},{8,10},{10,8},{12,14},{14,12},{1,3},{3,1},... | collective-permute-start | bytes 786440 | tf_op jit(solution)/shard_map/ppermute | solution.py:69
  286.5 62.3 %collective-permute-start.60 = (bf16[1024,640]{1,0:T(8,128)(2,1)}, bf16[1024,640]{1,0:T(8,128)(2,1)}, u32[]{:S(2)}, u32[]{:S(2)}) collective-permute-start(bf16[1024,640]{1,0:T(8,128)(2,1)} %dynamic-slice_convert_fusion), channel_id=1, source_target_pairs={{0,1},{1,0},{2,3},{3,2},{4,5},{5,4},{6,7},{7,6},{8,9},{9,8},{10,11... | collective-permute-start | bytes 3932168 | tf_op jit(solution)/shard_map/ppermute | solution.py:69
  300.2 22.0 %collective-permute-start.31 = (bf16[2,128,512]{2,1,0:T(8,128)(2,1)}, bf16[2,128,512]{2,1,0:T(8,128)(2,1)}, u32[]{:S(2)}, u32[]{:S(2)}) collective-permute-start(bf16[2,128,512]{2,1,0:T(8,128)(2,1)} %get-tuple-element.115), channel_id=1, source_target_pairs={{0,12},{2,14},{4,8},{6,10},{8,4},{10,6},{12,0},{14,2},{1,13},{3,15... | collective-permute-start | bytes 786440 | tf_op jit(solution)/shard_map/ppermute | solution.py:69
  303.5 22.4 %collective-permute-start.33 = (bf16[2,128,512]{2,1,0:T(8,128)(2,1)}, bf16[2,128,512]{2,1,0:T(8,128)(2,1)}, u32[]{:S(2)}, u32[]{:S(2)}) collective-permute-start(bf16[2,128,512]{2,1,0:T(8,128)(2,1)} %get-tuple-element.117), channel_id=1, source_target_pairs={{0,8},{2,10},{4,12},{6,14},{8,0},{10,2},{12,4},{14,6},{1,9},{3,11}... | collective-permute-start | bytes 786440 | tf_op jit(solution)/shard_map/ppermute | solution.py:69
  314.1 37.2 %collective-permute-start.54 = (bf16[320,2048]{1,0:T(8,128)(2,1)}, bf16[320,2048]{1,0:T(8,128)(2,1)}, u32[]{:S(2)}, u32[]{:S(2)}) collective-permute-start(bf16[320,2048]{1,0:T(8,128)(2,1)} %dynamic-slice_convert_fusion.1), channel_id=1, source_target_pairs={{0,1},{1,0},{2,3},{3,2},{4,5},{5,4},{6,7},{7,6},{8,9},{9,8},{10,11... | collective-permute-start | bytes 3932168 | tf_op jit(solution)/shard_map/ppermute | solution.py:69
  322.3 32.3 %collective-permute-start.48 = (bf16[320,2048]{1,0:T(8,128)(2,1)}, bf16[320,2048]{1,0:T(8,128)(2,1)}, u32[]{:S(2)}, u32[]{:S(2)}) collective-permute-start(bf16[320,2048]{1,0:T(8,128)(2,1)} %dynamic-slice_convert_fusion.2), channel_id=1, source_target_pairs={{0,1},{1,0},{2,3},{3,2},{4,5},{5,4},{6,7},{7,6},{8,9},{9,8},{10,11... | collective-permute-start | bytes 3932168 | tf_op jit(solution)/shard_map/ppermute | solution.py:69
  334.7 27.0 %collective-permute-start.36 = (bf16[352,1536]{1,0:T(8,128)(2,1)S(1)}, bf16[352,1536]{1,0:T(8,128)(2,1)S(1)}, u32[]{:S(2)}, u32[]{:S(2)}) collective-permute-start(bf16[352,1536]{1,0:T(8,128)(2,1)S(1)} %dynamic-slice_convert_fusion.3), channel_id=1, source_target_pairs={{0,1},{1,0},{2,3},{3,2},{4,5},{5,4},{6,7},{7,6},{8,9},{9,8},{10,11... | collective-permute-start | bytes 3244040 | tf_op jit(solution)/shard_map/ppermute | solution.py:69
  353.1 29.2 %collective-permute-start.55 = (bf16[160,2048]{1,0:T(8,128)(2,1)S(1)}, bf16[160,2048]{1,0:T(8,128)(2,1)S(1)}, u32[]{:S(2)}, u32[]{:S(2)}) collective-permute-start(bf16[160,2048]{1,0:T(8,128)(2,1)S(1)} %constant_dynamic-slice_fusion.1), channel_id=1, source_target_pairs={{0,2},{2,0},{4,6},{6,4},{8,10},{10,8},{12,14},{14,12},{1,3},{3,1},... | collective-permute-start | bytes 1966088 | tf_op jit(solution)/shard_map/ppermute | solution.py:69
  356.4 40.0 %collective-permute-start.49 = (bf16[160,2048]{1,0:T(8,128)(2,1)S(1)}, bf16[160,2048]{1,0:T(8,128)(2,1)S(1)}, u32[]{:S(2)}, u32[]{:S(2)}) collective-permute-start(bf16[160,2048]{1,0:T(8,128)(2,1)S(1)} %constant_dynamic-slice_fusion.2), channel_id=1, source_target_pairs={{0,2},{2,0},{4,6},{6,4},{8,10},{10,8},{12,14},{14,12},{1,3},{3,1},... | collective-permute-start | bytes 1966088 | tf_op jit(solution)/shard_map/ppermute | solution.py:69
  362.1 45.8 %collective-permute-start.37 = (bf16[176,1536]{1,0:T(8,128)(2,1)S(1)}, bf16[176,1536]{1,0:T(8,128)(2,1)S(1)}, u32[]{:S(2)}, u32[]{:S(2)}) collective-permute-start(bf16[176,1536]{1,0:T(8,128)(2,1)S(1)} %constant_dynamic-slice_fusion.4), channel_id=1, source_target_pairs={{0,2},{2,0},{4,6},{6,4},{8,10},{10,8},{12,14},{14,12},{1,3},{3,1},... | collective-permute-start | bytes 1622024 | tf_op jit(solution)/shard_map/ppermute | solution.py:69
  368.4 29.5 %collective-permute-start.46 = (bf16[256,640]{1,0:T(8,128)(2,1)S(1)}, bf16[256,640]{1,0:T(8,128)(2,1)S(1)}, u32[]{:S(2)}, u32[]{:S(2)}) collective-permute-start(bf16[256,640]{1,0:T(8,128)(2,1)S(1)} %add_convert_fusion.19), channel_id=1, source_target_pairs={{4,0},{6,2},{8,12},{10,14},{5,1},{7,3},{9,13},{11,15},{20,16},{22,... | collective-permute-start | bytes 983048 | tf_op jit(solution)/shard_map/ppermute | solution.py:130
  369.9 44.5 %collective-permute-start.62 = (bf16[512,640]{1,0:T(8,128)(2,1)S(1)}, bf16[512,640]{1,0:T(8,128)(2,1)S(1)}, u32[]{:S(2)}, u32[]{:S(2)}) collective-permute-start(bf16[512,640]{1,0:T(8,128)(2,1)S(1)} %add_convert_fusion.8), channel_id=1, source_target_pairs={{0,4},{2,6},{12,8},{14,10},{1,5},{3,7},{13,9},{15,11},{16,20},{18,... | collective-permute-start | bytes 1966088 | tf_op jit(solution)/shard_map/ppermute | solution.py:128
  382.5 46.8 %collective-permute-start.56 = (bf16[160,2048]{1,0:T(8,128)(2,1)S(1)}, bf16[160,2048]{1,0:T(8,128)(2,1)S(1)}, u32[]{:S(2)}, u32[]{:S(2)}) collective-permute-start(bf16[160,2048]{1,0:T(8,128)(2,1)S(1)} %add_convert_fusion.11), channel_id=1, source_target_pairs={{0,4},{2,6},{12,8},{14,10},{1,5},{3,7},{13,9},{15,11},{16,20},{18,... | collective-permute-start | bytes 1966088 | tf_op jit(solution)/shard_map/ppermute | solution.py:128
  396.6 35.2 %collective-permute-start.50 = (bf16[160,2048]{1,0:T(8,128)(2,1)S(1)}, bf16[160,2048]{1,0:T(8,128)(2,1)S(1)}, u32[]{:S(2)}, u32[]{:S(2)}) collective-permute-start(bf16[160,2048]{1,0:T(8,128)(2,1)S(1)} %add_convert_fusion.14), channel_id=1, source_target_pairs={{0,4},{2,6},{12,8},{14,10},{1,5},{3,7},{13,9},{15,11},{16,20},{18,... | collective-permute-start | bytes 1966088 | tf_op jit(solution)/shard_map/ppermute | solution.py:128
  414.5 32.6 %collective-permute-start.63 = (bf16[512,640]{1,0:T(8,128)(2,1)S(1)}, bf16[512,640]{1,0:T(8,128)(2,1)S(1)}, u32[]{:S(2)}, u32[]{:S(2)}) collective-permute-start(bf16[512,640]{1,0:T(8,128)(2,1)S(1)} %add_convert_fusion.7), channel_id=1, source_target_pairs={{4,8},{6,10},{8,4},{10,6},{5,9},{7,11},{9,5},{11,7},{20,24},{22,26... | collective-permute-start | bytes 1966088 | tf_op jit(solution)/shard_map/ppermute | solution.py:129
  429.6 30.2 %collective-permute-start.57 = (bf16[160,2048]{1,0:T(8,128)(2,1)S(1)}, bf16[160,2048]{1,0:T(8,128)(2,1)S(1)}, u32[]{:S(2)}, u32[]{:S(2)}) collective-permute-start(bf16[160,2048]{1,0:T(8,128)(2,1)S(1)} %add_convert_fusion.10), channel_id=1, source_target_pairs={{4,8},{6,10},{8,4},{10,6},{5,9},{7,11},{9,5},{11,7},{20,24},{22,26... | collective-permute-start | bytes 1966088 | tf_op jit(solution)/shard_map/ppermute | solution.py:129
  432.0 39.0 %collective-permute-start.51 = (bf16[160,2048]{1,0:T(8,128)(2,1)S(1)}, bf16[160,2048]{1,0:T(8,128)(2,1)S(1)}, u32[]{:S(2)}, u32[]{:S(2)}) collective-permute-start(bf16[160,2048]{1,0:T(8,128)(2,1)S(1)} %add_convert_fusion.13), channel_id=1, source_target_pairs={{4,8},{6,10},{8,4},{10,6},{5,9},{7,11},{9,5},{11,7},{20,24},{22,26... | collective-permute-start | bytes 1966088 | tf_op jit(solution)/shard_map/ppermute | solution.py:129
  445.8 26.7 %collective-permute-start.40 = (bf16[176,1536]{1,0:T(8,128)(2,1)S(1)}, bf16[176,1536]{1,0:T(8,128)(2,1)S(1)}, u32[]{:S(2)}, u32[]{:S(2)}) collective-permute-start(bf16[176,1536]{1,0:T(8,128)(2,1)S(1)} %add_convert_fusion.16), channel_id=1, source_target_pairs={{4,0},{6,2},{8,12},{10,14},{5,1},{7,3},{9,13},{11,15},{20,16},{22,... | collective-permute-start | bytes 1622024 | tf_op jit(solution)/shard_map/ppermute | solution.py:130
  447.3 26.5 %collective-permute-start.64 = (bf16[512,640]{1,0:T(8,128)(2,1)S(1)}, bf16[512,640]{1,0:T(8,128)(2,1)S(1)}, u32[]{:S(2)}, u32[]{:S(2)}) collective-permute-start(bf16[512,640]{1,0:T(8,128)(2,1)S(1)} %add_convert_fusion.6), channel_id=1, source_target_pairs={{4,0},{6,2},{8,12},{10,14},{5,1},{7,3},{9,13},{11,15},{20,16},{22,... | collective-permute-start | bytes 1966088 | tf_op jit(solution)/shard_map/ppermute | solution.py:130
  459.9 28.0 %collective-permute-start.58 = (bf16[160,2048]{1,0:T(8,128)(2,1)S(1)}, bf16[160,2048]{1,0:T(8,128)(2,1)S(1)}, u32[]{:S(2)}, u32[]{:S(2)}) collective-permute-start(bf16[160,2048]{1,0:T(8,128)(2,1)S(1)} %add_convert_fusion.9), channel_id=1, source_target_pairs={{4,0},{6,2},{8,12},{10,14},{5,1},{7,3},{9,13},{11,15},{20,16},{22,... | collective-permute-start | bytes 1966088 | tf_op jit(solution)/shard_map/ppermute | solution.py:130
  471.2 24.6 %collective-permute-start.52 = (bf16[160,2048]{1,0:T(8,128)(2,1)S(1)}, bf16[160,2048]{1,0:T(8,128)(2,1)S(1)}, u32[]{:S(2)}, u32[]{:S(2)}) collective-permute-start(bf16[160,2048]{1,0:T(8,128)(2,1)S(1)} %add_convert_fusion.12), channel_id=1, source_target_pairs={{4,0},{6,2},{8,12},{10,14},{5,1},{7,3},{9,13},{11,15},{20,16},{22,... | collective-permute-start | bytes 1966088 | tf_op jit(solution)/shard_map/ppermute | solution.py:130
  472.6 23.9 %collective-permute-start.41 = (bf16[176,1536]{1,0:T(8,128)(2,1)S(1)}, bf16[176,1536]{1,0:T(8,128)(2,1)S(1)}, u32[]{:S(2)}, u32[]{:S(2)}) collective-permute-start(bf16[176,1536]{1,0:T(8,128)(2,1)S(1)} %broadcast_select_fusion.11), channel_id=1, source_target_pairs={{0,2},{2,0},{4,6},{6,4},{8,10},{10,8},{12,14},{14,12},{1,3},{3,1},... | collective-permute-start | bytes 1622024 | tf_op jit(solution)/shard_map/ppermute | solution.py:69
  473.9 28.0 %collective-permute-start.65 = (bf16[512,640]{1,0:T(8,128)(2,1)S(1)}, bf16[512,640]{1,0:T(8,128)(2,1)S(1)}, u32[]{:S(2)}, u32[]{:S(2)}) collective-permute-start(bf16[512,640]{1,0:T(8,128)(2,1)S(1)} %broadcast_select_fusion.4), channel_id=1, source_target_pairs={{0,2},{2,0},{4,6},{6,4},{8,10},{10,8},{12,14},{14,12},{1,3},{3,1},... | collective-permute-start | bytes 1966088 | tf_op jit(solution)/shard_map/ppermute | solution.py:69
  488.0 28.0 %collective-permute-start.59 = (bf16[160,2048]{1,0:T(8,128)(2,1)S(1)}, bf16[160,2048]{1,0:T(8,128)(2,1)S(1)}, u32[]{:S(2)}, u32[]{:S(2)}) collective-permute-start(bf16[160,2048]{1,0:T(8,128)(2,1)S(1)} %broadcast_select_fusion.5), channel_id=1, source_target_pairs={{0,2},{2,0},{4,6},{6,4},{8,10},{10,8},{12,14},{14,12},{1,3},{3,1},... | collective-permute-start | bytes 1966088 | tf_op jit(solution)/shard_map/ppermute | solution.py:69
  495.8 30.5 %collective-permute-start.53 = (bf16[160,2048]{1,0:T(8,128)(2,1)S(1)}, bf16[160,2048]{1,0:T(8,128)(2,1)S(1)}, u32[]{:S(2)}, u32[]{:S(2)}) collective-permute-start(bf16[160,2048]{1,0:T(8,128)(2,1)S(1)} %broadcast_select_fusion.6), channel_id=1, source_target_pairs={{0,2},{2,0},{4,6},{6,4},{8,10},{10,8},{12,14},{14,12},{1,3},{3,1},... | collective-permute-start | bytes 1966088 | tf_op jit(solution)/shard_map/ppermute | solution.py:69
  (186 other events, 1613.6 us)

commit v2 on v1

v2 whole, which is shorter than its diff:
```python
import functools

import jax
import jax.numpy as jnp
from jax import lax
from jax.experimental import pallas as pl
from jax.experimental.pallas import tpu as pltpu
from jax.sharding import PartitionSpec as P

epsilon = 1e-06
rope_base = 1000000.0
masked = -1e30
score_scale = 0.0625
gelu_slope = 0.7978845608028654
gelu_cubic = 0.044715
f32 = jnp.float32
bf16 = jnp.bfloat16
vmem_bytes = 56 * 1024 * 1024


def dot_nn(left, right):
    return jnp.dot(left, right, preferred_element_type=f32)


def dot_nt(left, right):
    return lax.dot_general(left, right, (((1,), (1,)), ((), ())), preferred_element_type=f32)


def dot_tn(left, right):
    return lax.dot_general(left, right, (((0,), (0,)), ((), ())), preferred_element_type=f32)


def norm_factor(values_in):
    return lax.rsqrt(jnp.mean(values_in * values_in, axis=-1, keepdims=True) + epsilon)


def norm_apply(values_in, gain_vec):
    return values_in * norm_factor(values_in) * gain_vec


def norm_back(values_in, gain_vec, grad_out):
    factor = norm_factor(values_in)
    scaled = grad_out * gain_vec
    grad_in = factor * (
        scaled - values_in * factor * factor * jnp.mean(scaled * values_in, axis=-1, keepdims=True)
    )
    grad_gain = jnp.sum(grad_out * values_in * factor, axis=0, keepdims=True)
    return (grad_in, grad_gain)


def rotate(values_in, cos_table, sin_table):
    half_width = values_in.shape[-1] // 2
    former = values_in[..., :half_width]
    latter = values_in[..., half_width:]
    return jnp.concatenate(
        [former * cos_table - latter * sin_table, latter * cos_table + former * sin_table], axis=-1
    )


def rotation_tables(positions, half_width):
    frequency = rope_base ** (-jnp.arange(half_width, dtype=f32) / half_width)
    angles = positions.astype(f32)[:, None] * frequency[None, :]
    return (jnp.cos(angles), jnp.sin(angles))


def call_kernel(body, out_shapes, inputs, far_inputs, scratch):
    whole = pl.BlockSpec(memory_space=pltpu.VMEM)
    far = pl.BlockSpec(memory_space=pl.ANY)
    return pl.pallas_call(
        body,
        out_shape=out_shapes,
        in_specs=[whole] * len(inputs) + [far] * len(far_inputs),
        out_specs=jax.tree.map(lambda _: whole, out_shapes),
        scratch_shapes=scratch,
        compiler_params=pltpu.CompilerParams(vmem_limit_bytes=vmem_bytes),
    )(*inputs, *far_inputs)


def struct(shape, dtype):
    return jax.ShapeDtypeStruct(shape, dtype)


def start_halves(own, other, target, sems, first_sem):
    half = own.shape[0]
    fsdp_index = lax.axis_index("fsdp")
    copies = [
        pltpu.make_async_copy(
            own, target.at[pl.ds(fsdp_index * half, half)], sems.at[first_sem]
        ),
        pltpu.make_async_copy(
            other, target.at[pl.ds((1 - fsdp_index) * half, half)], sems.at[first_sem + 1]
        ),
    ]
    for copy in copies:
        copy.start()
    return copies


def wait_all(copies):
    for copy in copies:
        copy.wait()


def whole_gain(own_ref, other_ref, start, width):
    own = own_ref[:, start : start + width].astype(f32)
    other = other_ref[:, start : start + width].astype(f32)
    is_first = lax.axis_index("fsdp") == 0
    return jnp.concatenate(
        [jnp.where(is_first, own, other), jnp.where(is_first, other, own)], axis=1
    )


class Sizes:
    def __init__(self, groups, tokens, model, heads, head_dim, ff, blocks):
        self.groups, self.tokens, self.model = groups, tokens, model
        self.heads, self.head_dim, self.ff, self.blocks = heads, head_dim, ff, blocks
        self.rows = groups * tokens
        self.query_cols = heads * head_dim
        self.head_rows = heads * tokens
        self.keys = blocks * tokens
        self.span = tokens * min(8, blocks)
        self.chunk = min(256, self.head_rows)
        half = model // 2
        self.gain_at = {
            "input": (0, half),
            "attn": (half, half),
            "pre": (2 * half, half),
            "post": (3 * half, half),
            "query": (4 * half, head_dim // 2),
            "key": (4 * half + head_dim // 2, head_dim // 2),
        }


def kv_kernel(
    sz, hidden, gain_own, gain_other, cos_ref, sin_ref, k_own, k_other, v_own, v_other,
    normed, key_lin, kv_low, wk, wv, sems,
):
    k_copies = start_halves(k_own, k_other, wk, sems, 0)
    v_copies = start_halves(v_own, v_other, wv, sems, 2)
    gain_input = whole_gain(gain_own, gain_other, *sz.gain_at["input"])
    gain_key = whole_gain(gain_own, gain_other, *sz.gain_at["key"])
    low = norm_apply(hidden[...].astype(f32), gain_input).astype(bf16)
    normed[...] = low
    wait_all(k_copies)
    lin = dot_nn(low, wk[...])
    key_lin[...] = lin
    cos = jnp.concatenate([cos_ref[...]] * sz.groups, axis=0)
    sin = jnp.concatenate([sin_ref[...]] * sz.groups, axis=0)
    kv_low[:, : sz.head_dim] = rotate(norm_apply(lin, gain_key), cos, sin).astype(bf16)
    wait_all(v_copies)
    kv_low[:, sz.head_dim :] = dot_nn(low, wv[...]).astype(bf16)


def project_kv(sz, hidden, gains, tables, w_key, w_value):
    half = (sz.model, sz.head_dim)
    return call_kernel(
        functools.partial(kv_kernel, sz),
        [
            struct((sz.rows, sz.model), bf16),
            struct((sz.rows, sz.head_dim), f32),
            struct((sz.rows, 2 * sz.head_dim), bf16),
        ],
        [hidden, *gains, *tables],
        [*w_key, *w_value],
        [pltpu.VMEM(half, bf16), pltpu.VMEM(half, bf16), pltpu.SemaphoreType.DMA((4,))],
    )


def query_kernel(
    sz, normed, gain_own, gain_other, cos_ref, sin_ref, q_own, q_other,
    query_lin, query_low, wq, sems,
):
    copies = start_halves(q_own, q_other, wq, sems, 0)
    gain_query = whole_gain(gain_own, gain_other, *sz.gain_at["query"])
    cos = jnp.concatenate([cos_ref[...]] * sz.groups, axis=0)
    sin = jnp.concatenate([sin_ref[...]] * sz.groups, axis=0)
    low = normed[...]
    wait_all(copies)
    for head in range(sz.heads):
        cols = slice(head * sz.head_dim, (head + 1) * sz.head_dim)
        lin = dot_nn(low, wq[:, cols])
        query_lin[:, cols] = lin
        turned = rotate(norm_apply(lin, gain_query), cos, sin)
        turned = (turned.astype(bf16).astype(f32) * score_scale).astype(bf16)
        for group in range(sz.groups):
            query_low[group, head * sz.tokens : (head + 1) * sz.tokens, :] = turned[
                group * sz.tokens : (group + 1) * sz.tokens
            ]


def project_query(sz, normed, gains, tables, w_query):
    return call_kernel(
        functools.partial(query_kernel, sz),
        [
            struct((sz.rows, sz.query_cols), f32),
            struct((sz.groups, sz.head_rows, sz.head_dim), bf16),
        ],
        [normed, *gains, *tables],
        [*w_query],
        [pltpu.VMEM((sz.model, sz.query_cols), bf16), pltpu.SemaphoreType.DMA((2,))],
    )


def start_blocks(sz, blocks, target, sems, first_sem):
    copies = []
    for index, block in enumerate(blocks):
        copies.append(
            pltpu.make_async_copy(
                block,
                target.at[:, pl.ds(index * sz.tokens, sz.tokens)],
                sems.at[first_sem + index],
            )
        )
    for copy in copies:
        copy.start()
    return copies


def load_group(sz, stacked, group, target, sems, first_sem):
    def one(index):
        return pltpu.make_async_copy(
            stacked.at[index, group],
            target.at[0, pl.ds(index * sz.tokens, sz.tokens)],
            sems.at[first_sem + index],
        )

    def start(index, carry):
        one(index).start()
        return carry

    def wait(index, carry):
        one(index).wait()
        return carry

    lax.fori_loop(0, sz.blocks, start, 0)
    lax.fori_loop(0, sz.blocks, wait, 0)


def forward_kernel(sz, block_count, save, *refs):
    query_low, hidden, gain_own, gain_other, key_row, query_col = refs[:6]
    refs = refs[6:]
    blocks, refs = refs[:block_count], refs[block_count:]
    out_pair, gate_pair, up_pair, down_pair = (refs[2 * i : 2 * i + 2] for i in range(4))
    refs = refs[8:]
    result, refs = refs[0], refs[1:]
    if save:
        log_total, attn_low, branch_ref, middle_ref, pre_ref, gate_ref, up_ref, act_ref, down_ref = (
            refs[:9]
        )
        refs = refs[9:]
    else:
        attn_low, act_ref = refs[:2]
        refs = refs[2:]
    kv, w_out, w_gate, w_up, w_down, sems = refs
    if block_count > 1:
        kv_copies = start_blocks(sz, blocks, kv, sems, 8)
    out_copies = start_halves(*out_pair, w_out, sems, 0)
    gate_copies = start_halves(*gate_pair, w_gate, sems, 2)
    up_copies = start_halves(*up_pair, w_up, sems, 4)
    down_copies = start_halves(*down_pair, w_down, sems, 6)
    gain_attn = whole_gain(gain_own, gain_other, *sz.gain_at["attn"])
    gain_pre = whole_gain(gain_own, gain_other, *sz.gain_at["pre"])
    gain_post = whole_gain(gain_own, gain_other, *sz.gain_at["post"])
    if block_count > 1:
        wait_all(kv_copies)
    spans = sz.keys // sz.span
    for group in range(sz.groups):
        slot = group if block_count > 1 else 0
        if block_count == 1:
            load_group(sz, blocks[0], group, kv, sems, 8)
        for first in range(0, sz.head_rows, sz.chunk):
            query = query_low[group, first : first + sz.chunk, :]
            query_pos = query_col[first : first + sz.chunk, :]

            def one_span(index, state):
                row_max, row_total, row_sum = state
                at = pl.ds(index * sz.span, sz.span)
                scores = dot_nt(query, kv[slot, at, : sz.head_dim])
                scores = jnp.where(key_row[:, at] <= query_pos, scores, masked)
                new_max = jnp.maximum(row_max, jnp.max(scores, axis=1, keepdims=True))
                probs = jnp.exp(scores - new_max)
                part = dot_nn(probs.astype(bf16), kv[slot, at, sz.head_dim :])
                shrink = jnp.exp(row_max - new_max)
                return (
                    new_max,
                    row_total * shrink + jnp.sum(probs, axis=1, keepdims=True),
                    row_sum * shrink + part,
                )

            state = (
                jnp.full((sz.chunk, 1), masked, f32),
                jnp.zeros((sz.chunk, 1), f32),
                jnp.zeros((sz.chunk, sz.head_dim), f32),
            )
            if spans == 1:
                state = one_span(0, state)
            else:
                state = lax.fori_loop(0, spans, one_span, state)
            row_max, row_total, row_sum = state
            attended = (row_sum / row_total).astype(bf16)
            if save:
                log_total[group, first : first + sz.chunk, :] = row_max + jnp.log(row_total)
            for part in range(sz.chunk // sz.tokens):
                head = first // sz.tokens + part
                attn_low[
                    group * sz.tokens : (group + 1) * sz.tokens,
                    head * sz.head_dim : (head + 1) * sz.head_dim,
                ] = attended[part * sz.tokens : (part + 1) * sz.tokens]
    wait_all(out_copies)
    branch = dot_nn(attn_low[...], w_out[...])
    middle = hidden[...].astype(f32) + norm_apply(branch, gain_attn)
    pre_ffw = norm_apply(middle, gain_pre).astype(bf16)
    if save:
        branch_ref[...] = branch
        middle_ref[...] = middle
        pre_ref[...] = pre_ffw
    wait_all(gate_copies)
    wait_all(up_copies)
    step = min(512, sz.ff)
    for first in range(0, sz.ff, step):
        cols = slice(first, first + step)
        gate = dot_nn(pre_ffw, w_gate[:, cols])
        up = dot_nn(pre_ffw, w_up[:, cols])
        if save:
            gate_ref[:, cols] = gate
            up_ref[:, cols] = up
        bend = jnp.tanh(gelu_slope * (gate + gelu_cubic * gate * gate * gate))
        act_ref[:, cols] = (0.5 * gate * (1.0 + bend) * up).astype(bf16)
    wait_all(down_copies)
    down_out = dot_nn(act_ref[...], w_down[...])
    if save:
        down_ref[...] = down_out
    result[...] = (middle + norm_apply(down_out, gain_post)).astype(bf16)


def forward_layer(sz, query_low, hidden, gains, places, blocks, weights, save):
    rows, model = sz.rows, sz.model
    outs = [struct((rows, model), bf16)]
    attn = (rows, sz.query_cols)
    act = (rows, sz.ff)
    scratch = []
    if save:
        outs += [
            struct((sz.groups, sz.head_rows, 1), f32),
            struct(attn, bf16),
            struct((rows, model), f32),
            struct((rows, model), f32),
            struct((rows, model), bf16),
            struct(act, f32),
            struct(act, f32),
            struct(act, bf16),
            struct((rows, model), f32),
        ]
    else:
        scratch += [pltpu.VMEM(attn, bf16), pltpu.VMEM(act, bf16)]
    scratch += [
        pltpu.VMEM((sz.groups if len(blocks) > 1 else 1, sz.keys, 2 * sz.head_dim), bf16),
        pltpu.VMEM((sz.query_cols, model), bf16),
        pltpu.VMEM((model, sz.ff), bf16),
        pltpu.VMEM((model, sz.ff), bf16),
        pltpu.VMEM((sz.ff, model), bf16),
        pltpu.SemaphoreType.DMA((8 + sz.blocks,)),
    ]
    far = [*blocks, *weights["out"], *weights["gate"], *weights["up"], *weights["down"]]
    return call_kernel(
        functools.partial(forward_kernel, sz, len(blocks), save),
        outs,
        [query_low, hidden, *gains, places["key_row"], places["query_col"]],
        far,
        scratch,
    )


def backward_kernel(sz, block_count, *refs):
    (
        grad_ref, gain_own, gain_other, down_out, gate_ref, up_ref, middle, branch,
        query_low, log_row, key_col, query_row,
    ) = refs[:12]
    refs = refs[12:]
    blocks, refs = refs[:block_count], refs[block_count:]
    out_pair, gate_pair, up_pair, down_pair = (refs[2 * i : 2 * i + 2] for i in range(4))
    refs = refs[8:]
    (
        middle_grad, down_grad, gate_grad, up_grad, branch_grad, gain_post_grad, gain_pre_grad,
        gain_attn_grad, query_grad,
    ) = refs[:9]
    refs = refs[9:]
    parts, refs = refs[:block_count], refs[block_count:]
    kv, w_out, w_gate, w_up, w_down, key_sum, value_sum, sems = refs
    down_copies = start_halves(*down_pair, w_down, sems, 0)
    gate_copies = start_halves(*gate_pair, w_gate, sems, 2)
    up_copies = start_halves(*up_pair, w_up, sems, 4)
    out_copies = start_halves(*out_pair, w_out, sems, 6)
    if block_count > 1:
        kv_copies = start_blocks(sz, blocks, kv, sems, 8)
    gain_attn = whole_gain(gain_own, gain_other, *sz.gain_at["attn"])
    gain_pre = whole_gain(gain_own, gain_other, *sz.gain_at["pre"])
    gain_post = whole_gain(gain_own, gain_other, *sz.gain_at["post"])
    grad = grad_ref[...].astype(f32)
    down_part, gain_post_grad[...] = norm_back(down_out[...], gain_post, grad)
    down_low = down_part.astype(bf16)
    down_grad[...] = down_low
    wait_all(down_copies)
    wait_all(gate_copies)
    wait_all(up_copies)
    step = min(512, sz.ff)
    pre_grad = jnp.zeros((sz.rows, sz.model), f32)
    for first in range(0, sz.ff, step):
        cols = slice(first, first + step)
        ffw_grad = dot_nt(down_low, w_down[cols, :])
        gate = gate_ref[:, cols]
        up = up_ref[:, cols]
        square = gate * gate
        bend = jnp.tanh(gelu_slope * (gate + gelu_cubic * square * gate))
        half_open = 0.5 * (1.0 + bend)
        slope = half_open + 0.5 * gate * (1.0 - bend * bend) * gelu_slope * (
            1.0 + 3.0 * gelu_cubic * square
        )
        gate_low = (ffw_grad * up * slope).astype(bf16)
        up_low = (ffw_grad * gate * half_open).astype(bf16)
        gate_grad[:, cols] = gate_low
        up_grad[:, cols] = up_low
        pre_grad = pre_grad + dot_nt(gate_low, w_gate[:, cols]) + dot_nt(up_low, w_up[:, cols])
    middle_part, gain_pre_grad[...] = norm_back(middle[...], gain_pre, pre_grad)
    total = grad + middle_part
    middle_grad[...] = total
    branch_part, gain_attn_grad[...] = norm_back(branch[...], gain_attn, total)
    branch_low = branch_part.astype(bf16)
    branch_grad[...] = branch_low
    wait_all(out_copies)
    attn_grad = dot_nt(branch_low, w_out[...]).astype(bf16)
    if block_count > 1:
        wait_all(kv_copies)
    spans = sz.keys // sz.span
    heads_in = sz.chunk // sz.tokens
    chunks = range(0, sz.head_rows, sz.chunk)

    def probs_of(slot, group, first, at):
        query = query_low[group, first : first + sz.chunk, :]
        query_pos = query_row[:, first : first + sz.chunk]
        log_here = log_row[group, :, first : first + sz.chunk]
        scores = dot_nt(kv[slot, at, : sz.head_dim], query)
        probs = jnp.exp(jnp.where(key_col[at, :] <= query_pos, scores - log_here, masked))
        grad_rows = jnp.concatenate(
            [
                attn_grad[
                    group * sz.tokens : (group + 1) * sz.tokens,
                    (first // sz.tokens + part) * sz.head_dim : (first // sz.tokens + part + 1)
                    * sz.head_dim,
                ]
                for part in range(heads_in)
            ],
            axis=0,
        )
        return probs, dot_nt(kv[slot, at, sz.head_dim :], grad_rows), query, grad_rows

    def finish(slot, first, at, got, delta):
        probs, prob_grad, query, grad_rows = got
        score_grad = (probs * (prob_grad - delta)).astype(bf16)
        key_part = dot_nn(score_grad, query)
        value_part = dot_nn(probs.astype(bf16), grad_rows)
        if first == 0:
            key_sum[...] = key_part
            value_sum[...] = value_part
        else:
            key_sum[...] += key_part
            value_sum[...] += value_part
        return dot_tn(score_grad, kv[slot, at, : sz.head_dim])

    for group in range(sz.groups):
        if block_count > 1:
            for first in chunks:
                at = slice(0, sz.span)
                got = probs_of(group, group, first, at)
                delta = jnp.sum(got[0] * got[1], axis=0, keepdims=True)
                query_grad[group, first : first + sz.chunk, :] = finish(
                    group, first, at, got, delta
                )
            for index in range(block_count):
                at = slice(index * sz.tokens, (index + 1) * sz.tokens)
                parts[index][group, :, : sz.head_dim] = key_sum[at, :].astype(bf16)
                parts[index][group, :, sz.head_dim :] = value_sum[at, :].astype(bf16)
            continue
        load_group(sz, blocks[0], group, kv, sems, 8)
        deltas = []
        for first in chunks:

            def add_delta(index, delta, first=first):
                got = probs_of(0, group, first, pl.ds(index * sz.span, sz.span))
                return delta + jnp.sum(got[0] * got[1], axis=0, keepdims=True)

            deltas.append(lax.fori_loop(0, spans, add_delta, jnp.zeros((1, sz.chunk), f32)))
            query_grad[group, first : first + sz.chunk, :] = jnp.zeros(
                (sz.chunk, sz.head_dim), f32
            )

        def add_span(index, carry):
            at = pl.ds(index * sz.span, sz.span)
            for first, delta in zip(chunks, deltas):
                query_grad[group, first : first + sz.chunk, :] += finish(
                    0, first, at, probs_of(0, group, first, at), delta
                )
            per_span = sz.span // sz.tokens
            for step in range(per_span):
                rows = slice(step * sz.tokens, (step + 1) * sz.tokens)
                target = parts[0].at[index * per_span + step, group]
                target[:, : sz.head_dim] = key_sum[rows, :].astype(bf16)
                target[:, sz.head_dim :] = value_sum[rows, :].astype(bf16)
            return carry

        lax.fori_loop(0, spans, add_span, 0)


def backward_layer(sz, grad, gains, saved, places, blocks, weights):
    rows, model = sz.rows, sz.model
    gain = struct((1, model), f32)
    outs = [
        struct((rows, model), f32),
        struct((rows, model), bf16),
        struct((rows, sz.ff), bf16),
        struct((rows, sz.ff), bf16),
        struct((rows, model), bf16),
        gain,
        gain,
        gain,
        struct((sz.groups, sz.head_rows, sz.head_dim), f32),
    ]
    outs += [struct(block.shape, bf16) for block in blocks]
    scratch = [
        pltpu.VMEM((sz.groups if len(blocks) > 1 else 1, sz.keys, 2 * sz.head_dim), bf16),
        pltpu.VMEM((sz.query_cols, model), bf16),
        pltpu.VMEM((model, sz.ff), bf16),
        pltpu.VMEM((model, sz.ff), bf16),
        pltpu.VMEM((sz.ff, model), bf16),
        pltpu.VMEM((sz.span, sz.head_dim), f32),
        pltpu.VMEM((sz.span, sz.head_dim), f32),
        pltpu.SemaphoreType.DMA((8 + sz.blocks,)),
    ]
    inputs = [
        grad, *gains, saved["down_out"], saved["gate"], saved["up"], saved["middle"],
        saved["branch"], saved["query_low"], saved["log_row"], places["key_col"],
        places["query_row"],
    ]
    far = [*blocks, *weights["out"], *weights["gate"], *weights["up"], *weights["down"]]
    got = call_kernel(
        functools.partial(backward_kernel, sz, len(blocks)), outs, inputs, far, scratch
    )
    return got[:9], got[9:]


def query_back_kernel(
    sz, query_grad, query_lin, gain_own, gain_other, cos_ref, sin_ref, q_own, q_other,
    lin_grad, normed_grad, gain_grad, wq, sems,
):
    copies = start_halves(q_own, q_other, wq, sems, 0)
    gain_query = whole_gain(gain_own, gain_other, *sz.gain_at["query"])
    cos = jnp.concatenate([cos_ref[...]] * sz.groups, axis=0)
    sin = jnp.concatenate([sin_ref[...]] * sz.groups, axis=0)
    gain_sum = jnp.zeros((1, sz.head_dim), f32)
    for head in range(sz.heads):
        cols = slice(head * sz.head_dim, (head + 1) * sz.head_dim)
        rows = slice(head * sz.tokens, (head + 1) * sz.tokens)
        grad = jnp.concatenate([query_grad[g, rows, :] for g in range(sz.groups)], axis=0)
        turned = rotate(grad * score_scale, cos, -sin)
        part, gain_part = norm_back(query_lin[:, cols], gain_query, turned)
        lin_grad[:, cols] = part.astype(bf16)
        gain_sum = gain_sum + gain_part
    gain_grad[...] = gain_sum
    wait_all(copies)
    normed_grad[...] = dot_nt(lin_grad[...], wq[...])


def query_back(sz, query_grad, query_lin, gains, tables, w_query):
    return call_kernel(
        functools.partial(query_back_kernel, sz),
        [
            struct((sz.rows, sz.query_cols), bf16),
            struct((sz.rows, sz.model), f32),
            struct((1, sz.head_dim), f32),
        ],
        [query_grad, query_lin, *gains, *tables],
        [*w_query],
        [pltpu.VMEM((sz.model, sz.query_cols), bf16), pltpu.SemaphoreType.DMA((2,))],
    )


def input_back_kernel(sz, term_count, *refs):
    terms, refs = refs[:term_count], refs[term_count:]
    (
        key_lin, hidden, query_part, middle_grad, gain_own, gain_other, cos_ref, sin_ref,
        k_own, k_other, v_own, v_other, input_grad, kv_grad, gain_input_grad, gain_key_grad,
        wk, wv, sems,
    ) = refs
    k_copies = start_halves(k_own, k_other, wk, sems, 0)
    v_copies = start_halves(v_own, v_other, wv, sems, 2)
    gain_input = whole_gain(gain_own, gain_other, *sz.gain_at["input"])
    gain_key = whole_gain(gain_own, gain_other, *sz.gain_at["key"])
    cos = jnp.concatenate([cos_ref[...]] * sz.groups, axis=0)
    sin = jnp.concatenate([sin_ref[...]] * sz.groups, axis=0)
    total = terms[0][...].astype(f32)
    for term in terms[1:]:
        total = total + term[...].astype(f32)
    turned = rotate(total[:, : sz.head_dim], cos, -sin)
    key_part, gain_key_grad[...] = norm_back(key_lin[...], gain_key, turned)
    key_low = key_part.astype(bf16)
    value_low = total[:, sz.head_dim :].astype(bf16)
    kv_grad[:, : sz.head_dim] = key_low
    kv_grad[:, sz.head_dim :] = value_low
    wait_all(k_copies)
    wait_all(v_copies)
    normed_grad = query_part[...] + dot_nt(key_low, wk[...]) + dot_nt(value_low, wv[...])
    part, gain_input_grad[...] = norm_back(hidden[...].astype(f32), gain_input, normed_grad)
    input_grad[...] = (middle_grad[...] + part).astype(bf16)


def input_back(sz, terms, key_lin, hidden, query_part, middle_grad, gains, tables, w_key, w_value):
    half = (sz.model, sz.head_dim)
    flat = [term.reshape(sz.rows, 2 * sz.head_dim) for term in terms]
    return call_kernel(
        functools.partial(input_back_kernel, sz, len(flat)),
        [
            struct((sz.rows, sz.model), bf16),
            struct((sz.rows, 2 * sz.head_dim), bf16),
            struct((1, sz.model), f32),
            struct((1, sz.head_dim), f32),
        ],
        [*flat, key_lin, hidden, query_part, middle_grad, *gains, *tables],
        [*w_key, *w_value],
        [pltpu.VMEM(half, bf16), pltpu.VMEM(half, bf16), pltpu.SemaphoreType.DMA((4,))],
    )


def xor_permute(shard, axis, mask):
    count = lax.axis_size(axis)
    return lax.ppermute(shard, axis, [(i, i ^ mask) for i in range(count)])


def small_ctx():
    return lax.axis_size("ctx") == 8


def ctx_order():
    count = lax.axis_size("ctx")
    slots = jnp.arange(count, dtype=jnp.int32)
    if small_ctx():
        return lax.axis_index("ctx") ^ slots
    return slots


def gather_ctx(shard):
    if not small_ctx():
        return [lax.all_gather(shard, "ctx", axis=0)]
    blocks = [None] * 8
    blocks[0] = shard
    for mask in (6, 4, 2):
        blocks[mask] = xor_permute(shard, "ctx", mask)
    for mask in (0, 2, 4, 6):
        blocks[mask + 1] = xor_permute(blocks[mask], "ctx", 1)
    return blocks


def scatter_ctx(parts):
    if len(parts) == 1:
        return [lax.psum_scatter(parts[0].astype(f32), "ctx", scatter_dimension=0, tiled=False)]
    terms = []
    for mask in (6, 4, 2):
        came = xor_permute(parts[mask + 1], "ctx", 1)
        both = (parts[mask].astype(f32) + came.astype(f32)).astype(bf16)
        terms.append(xor_permute(both, "ctx", mask))
    return terms + [parts[0], xor_permute(parts[1], "ctx", 1)]


def sum_ctx(shard):
    if not small_ctx():
        return lax.psum(shard.astype(f32), "ctx")
    ctx_index = lax.axis_index("ctx")
    y_index = ctx_index & 1
    z_index = ctx_index >> 1
    half = shard.shape[0] // 2
    keep = lax.dynamic_slice_in_dim(shard, y_index * half, half, 0)
    send = lax.dynamic_slice_in_dim(shard, (1 - y_index) * half, half, 0)
    came = xor_permute(send, "ctx", 1)
    inward = [(z * 2 + y, t * 2 + y) for z, t in ((0, 1), (3, 2)) for y in (0, 1)]
    middle = [(z * 2 + y, t * 2 + y) for z, t in ((1, 2), (2, 1)) for y in (0, 1)]
    outward = [(z * 2 + y, t * 2 + y) for z, t in ((1, 0), (2, 3)) for y in (0, 1)]

    def add(left, right):
        return lax.optimization_barrier((left.astype(f32) + right.astype(f32)).astype(bf16))

    part = add(keep, came)
    part = add(part, lax.ppermute(part, "ctx", inward))
    part = add(part, lax.ppermute(part, "ctx", middle))
    back = lax.ppermute(part, "ctx", outward)
    total = jnp.where((z_index == 1) | (z_index == 2), part, back)
    other = xor_permute(total, "ctx", 1)
    first = jnp.where(y_index == 0, total, other)
    second = jnp.where(y_index == 0, other, total)
    return jnp.concatenate([first, second], axis=0).astype(f32)


def weight_term(left, right):
    half = left.shape[1] // 2
    fsdp_index = lax.axis_index("fsdp")
    keep = lax.dynamic_slice_in_dim(left, fsdp_index * half, half, 1)
    send = lax.dynamic_slice_in_dim(left, (1 - fsdp_index) * half, half, 1)
    came = xor_permute(dot_tn(send, right).astype(bf16), "fsdp", 1)
    return (dot_tn(keep, right) + came.astype(f32)).astype(bf16)


def on_device(
    inputs,
    out_cotangent,
    block_order,
    w_query,
    w_key,
    w_value,
    w_output,
    w_gate,
    w_up,
    w_down,
    g_input,
    g_query,
    g_key,
    g_post_attn,
    g_pre_ffw,
    g_post_ffw,
):
    section_index = lax.axis_index("section")
    fsdp_index = lax.axis_index("fsdp")
    ctx_index = lax.axis_index("ctx")
    ctx_size = lax.axis_size("ctx")
    micro_count, seq_local, tokens, model_width = inputs.shape
    head_dim = 2 * g_query.shape[1]
    sz = Sizes(
        micro_count * seq_local,
        tokens,
        model_width,
        w_query.shape[2] // head_dim,
        head_dim,
        w_gate.shape[2],
        ctx_size,
    )
    block_len = tokens // 2
    gains_own = jnp.concatenate([g_input, g_post_attn, g_pre_ffw, g_post_ffw, g_query, g_key], 1)
    gains = (gains_own, xor_permute(gains_own, "fsdp", 1))
    weights = {}
    for name, own in (
        ("key", w_key),
        ("value", w_value),
        ("query", w_query),
        ("out", w_output),
        ("gate", w_gate),
        ("up", w_up),
        ("down", w_down),
    ):
        weights[name] = (own[0], xor_permute(own[0], "fsdp", 1))
    slot_pairs = block_order.reshape(ctx_size, 2)
    offsets = jnp.arange(block_len, dtype=jnp.int32)

    def spread(slot_ids):
        return (slot_ids.reshape(-1)[:, None] * block_len + offsets[None, :]).reshape(-1)

    local_pos = spread(slot_pairs[ctx_index])
    key_pos = spread(slot_pairs[ctx_order()])
    tables = rotation_tables(local_pos, head_dim // 2)
    query_pos = jnp.tile(local_pos, sz.heads)
    places = {
        "key_row": key_pos.reshape(1, -1),
        "key_col": key_pos.reshape(-1, 1),
        "query_row": query_pos.reshape(1, -1),
        "query_col": query_pos.reshape(-1, 1),
    }
    block_shape = (sz.groups, tokens, 2 * head_dim)

    def forward(hidden, save):
        normed, key_lin, kv_low = project_kv(
            sz, hidden, gains, tables, weights["key"], weights["value"]
        )
        blocks = gather_ctx(kv_low.reshape(block_shape))
        query_lin, query_low = project_query(sz, normed, gains, tables, weights["query"])
        got = forward_layer(sz, query_low, hidden, gains, places, blocks, weights, save)
        if not save:
            return got[0], None
        names = (
            "log_total", "attn_low", "branch", "middle", "pre_ffw", "gate", "up", "act", "down_out"
        )
        saved = dict(zip(names, got[1:]))
        saved["log_row"] = saved["log_total"].reshape(sz.groups, 1, sz.head_rows)
        saved.update(
            hidden=hidden, normed=normed, key_lin=key_lin, query_lin=query_lin,
            query_low=query_low, blocks=blocks,
        )
        return got[0], saved

    def backward(grad, saved):
        got, parts = backward_layer(sz, grad, gains, saved, places, saved["blocks"], weights)
        middle_grad = got[0]
        query_low_grad, query_part, gain_query = query_back(
            sz, got[8], saved["query_lin"], gains, tables, weights["query"]
        )
        terms = scatter_ctx(parts)
        input_grad, kv_grad, gain_input, gain_key = input_back(
            sz, terms, saved["key_lin"], saved["hidden"], query_part, middle_grad, gains, tables,
            weights["key"], weights["value"],
        )
        return input_grad, dict(
            down=got[1], gate=got[2], up=got[3], branch=got[4], post=got[5], pre=got[6],
            attn=got[7], query_lin=query_low_grad, query=gain_query, kv=kv_grad,
            input=gain_input, key=gain_key,
        )

    own_input = inputs.reshape(sz.rows, model_width)
    first_result, _ = forward(own_input, False)
    received = lax.ppermute(first_result, "section", [(0, 1)])
    hidden = jnp.where(section_index == 0, own_input, received)
    result, saved = forward(hidden, True)
    own_grad = out_cotangent.reshape(sz.rows, model_width)
    first_grad, _ = backward(own_grad, saved)
    grad_received = lax.ppermute(first_grad, "section", [(1, 0)])
    grad_in = jnp.where(section_index == 1, own_grad, grad_received)
    input_grad, grads = backward(grad_in, saved)

    sum_down = sum_ctx(weight_term(saved["act"], grads["down"]))
    sum_gate = sum_ctx(weight_term(saved["pre_ffw"], grads["gate"]))
    sum_up = sum_ctx(weight_term(saved["pre_ffw"], grads["up"]))
    sum_out = sum_ctx(weight_term(saved["attn_low"], grads["branch"]))
    sum_query = sum_ctx(weight_term(saved["normed"], grads["query_lin"]))
    names = ("input", "attn", "pre", "post", "query", "key")
    gain_rows = jnp.concatenate([grads[name].reshape(2, -1) for name in names], axis=1)
    kv_width = 2 * head_dim
    gain_rows = gain_rows.reshape(2, -1, kv_width)
    gain_count = gain_rows.shape[1]
    gain_rows = jnp.pad(gain_rows, ((0, 0), (0, 32 - gain_count), (0, 0)))
    gain_keep = lax.dynamic_index_in_dim(gain_rows, fsdp_index, 0, keepdims=False)
    gain_send = lax.dynamic_index_in_dim(gain_rows, 1 - fsdp_index, 0, keepdims=False)
    gain_came = xor_permute(gain_send.astype(bf16), "fsdp", 1)
    gain_term = (gain_keep + gain_came.astype(f32)).astype(bf16)
    kv_term = weight_term(saved["normed"], grads["kv"])
    sum_tail = sum_ctx(jnp.concatenate([kv_term, gain_term], axis=0))
    half_model = model_width // 2
    sum_key = sum_tail[:half_model, :head_dim]
    sum_value = sum_tail[:half_model, head_dim:]
    sum_gains = sum_tail[half_model : half_model + gain_count].reshape(-1)
    gain_sums = {}
    for name in names:
        start, width = sz.gain_at[name]
        gain_sums[name] = sum_gains[start : start + width]
    shape = (micro_count, seq_local, tokens, model_width)
    members = (
        sum_query,
        sum_key,
        sum_value,
        sum_out,
        sum_gate,
        sum_up,
        sum_down,
        gain_sums["input"],
        gain_sums["query"],
        gain_sums["key"],
        gain_sums["attn"],
        gain_sums["pre"],
        gain_sums["post"],
    )
    return (result.reshape(shape)[None], input_grad.reshape(shape)[None]) + tuple(
        member[None] for member in members
    )


def solution(mesh):
    weight = P("section", "fsdp", None)
    gain = P("section", "fsdp")
    in_specs = (P(None, "fsdp", "ctx", None),) * 2 + (P(),) + (weight,) * 7 + (gain,) * 6
    out_specs = (
        (P("section", None, "fsdp", "ctx", None),) * 2 + (weight,) * 7 + (gain,) * 6
    )
    return jax.shard_map(
        on_device, mesh=mesh, in_specs=in_specs, out_specs=out_specs, check_vma=False
    )
```

time: 535 us -> 475 us (0.89)
  the two profiles are of different devices: /device:TPU:12 before, /device:TPU:0 now
where the time goes in v2:
time: 475 us; the launch traced here: 467 us
  waiting for transfers between devices  211 us (44%)
  starting transfers between devices  103 us (22%)
  Pallas kernels  88.8 us (19%)
  other arithmetic  26.1 us (5%)
  local copies, waits for them, and re-layouts  18.6 us (4%)
  matrix products  17.8 us (4%)
    ppermute x55, waiting for transfers between devices, xor_permute(): return lax.ppermute(shard, axis, [(i, i ^ mask) for i in range(count)])  124 us
    pallas_call x12, Pallas kernels, call_kernel(): pl.pallas_call(body, out_shape=out_shapes, in_specs=[whole] * len(inputs)...  88.8 us
    ppermute x55, starting transfers between devices, xor_permute(): return lax.ppermute(shard, axis, [(i, i ^ mask) for i in range(count)])  66.8 us
    ppermute x6, waiting for transfers between devices, sum_ctx(): back = lax.ppermute(part, 'ctx', outward)  45.1 us
    ppermute x6, waiting for transfers between devices, sum_ctx(): part = add(part, lax.ppermute(part, 'ctx', inward))  27.8 us
    ppermute x6, starting transfers between devices, sum_ctx(): part = add(part, lax.ppermute(part, 'ctx', inward))  18.9 us
    dot_general x12, matrix products, dot_tn(): lax.dot_general(left, right, (((0,), (0,)), ((), ())), preferred_element_...  17.8 us
  transfers between devices with their start and end apart: 75, of which 28 were waited for; matrix products, arithmetic and copies ran while one was open for 11% of the time, Pallas kernels for 5%

profile of v2, /device:TPU:0, one launch (start us, length us, event | category | flops | bytes accessed | tf_op | source)
XLA Modules:
  0.0 467.1 jit_solution(1149894931277079961)
XLA Ops:
  8.9 4.7 %collective-permute-start.9 = (bf16[2,128,512]{2,1,0:T(8,128)(2,1)}, bf16[2,128,512]{2,1,0:T(8,128)(2,1)S(1)}, u32[]{:S(2)}, u32[]{:S(2)}) collective-permute-start(bf16[2,128,512]{2,1,0:T(8,128)(2,1)} %bitcast.131), channel_id=1, source_target_pairs={{0,12},{2,14},{4,8},{6,10},{8,4},{10,6},{12,0},{14,2},{1,13},{3,15... | collective-permute-start | bytes 786440 | tf_op jit(solution)/shard_map/ppermute | solution.py:635
  15.9 5.1 %collective-permute-done.9.refs_12_ = bf16[2,128,512]{2,1,0:T(8,128)(2,1)S(1)} collective-permute-done((bf16[2,128,512]{2,1,0:T(8,128)(2,1)}, bf16[2,128,512]{2,1,0:T(8,128)(2,1)S(1)}, u32[]{:S(2)}, u32[]{:S(2)}) %collective-permute-start.9) | collective-permute-done | bytes 262176 | tf_op jit(solution)/shard_map/ppermute | solution.py:635
  21.1 6.4 %collective-permute-done.5.refs_8_ = bf16[2,128,512]{2,1,0:T(8,128)(2,1)S(1)} collective-permute-done((bf16[2,128,512]{2,1,0:T(8,128)(2,1)}, bf16[2,128,512]{2,1,0:T(8,128)(2,1)S(1)}, u32[]{:S(2)}, u32[]{:S(2)}) %collective-permute-start.5) | collective-permute-done | bytes 262176 | tf_op jit(solution)/shard_map/ppermute | solution.py:635
  27.5 9.2 %collective-permute-done.7.refs_10_ = bf16[2,128,512]{2,1,0:T(8,128)(2,1)S(1)} collective-permute-done((bf16[2,128,512]{2,1,0:T(8,128)(2,1)}, bf16[2,128,512]{2,1,0:T(8,128)(2,1)S(1)}, u32[]{:S(2)}, u32[]{:S(2)}) %collective-permute-start.7) | collective-permute-done | bytes 262176 | tf_op jit(solution)/shard_map/ppermute | solution.py:635
  42.4 5.0 %collective-permute-done.10.refs_13_ = bf16[2,128,512]{2,1,0:T(8,128)(2,1)} collective-permute-done((bf16[2,128,512]{2,1,0:T(8,128)(2,1)S(1)}, bf16[2,128,512]{2,1,0:T(8,128)(2,1)}, u32[]{:S(2)}, u32[]{:S(2)}) %collective-permute-start.10) | collective-permute-done | bytes 262176 | tf_op jit(solution)/shard_map/ppermute | solution.py:635
  58.6 9.6 %shard_map.273 = bf16[256,640]{1,0:T(8,128)(2,1)} custom-call(bf16[2,512,256]{2,1,0:T(8,128)(2,1)} %get-tuple-element.70.refs_0_, bf16[256,640]{1,0:T(8,128)(2,1)} %bitcast.111, bf16[1,1536]{1,0:T(2,128)(2,1)} %copy-done.27, bf16[1,1536]{1,0:T(2,128)(2,1)} %copy-done.28, s32[1,1024]{1,0:T(1,128)} %add.235.refs_4_, s32[512,1]{1,0:T(8,128)} %copy.33.refs_5_, ...), custom_call_target="tpu_custom_call" | custom-call | tf_op jit(solution)/shard_map/pallas_call | solution.py:69
  72.1 5.9 %collective-permute-done.15 = bf16[256,640]{1,0:T(8,128)(2,1)S(1)} collective-permute-done((bf16[256,640]{1,0:T(8,128)(2,1)}, bf16[256,640]{1,0:T(8,128)(2,1)S(1)}, u32[]{:S(2)}, u32[]{:S(2)}) %collective-permute-start.15) | collective-permute-done | bytes 327712 | tf_op jit(solution)/shard_map/ppermute | solution.py:814
  88.4 5.0 %collective-permute-done.17.refs_8_.refs_14_ = bf16[2,128,512]{2,1,0:T(8,128)(2,1)S(1)} collective-permute-done((bf16[2,128,512]{2,1,0:T(8,128)(2,1)}, bf16[2,128,512]{2,1,0:T(8,128)(2,1)S(1)}, u32[]{:S(2)}, u32[]{:S(2)}) %collective-permute-start.17) | collective-permute-done | bytes 262176 | tf_op jit(solution)/shard_map/ppermute | solution.py:635
  94.9 9.2 %collective-permute-done.19.refs_10_.refs_16_ = bf16[2,128,512]{2,1,0:T(8,128)(2,1)S(1)} collective-permute-done((bf16[2,128,512]{2,1,0:T(8,128)(2,1)}, bf16[2,128,512]{2,1,0:T(8,128)(2,1)S(1)}, u32[]{:S(2)}, u32[]{:S(2)}) %collective-permute-start.19) | collective-permute-done | bytes 262176 | tf_op jit(solution)/shard_map/ppermute | solution.py:635
  114.0 11.3 %shard_map.276 = (bf16[256,640]{1,0:T(8,128)(2,1)}, f32[2,512,1]{2,1,0:T(8,128)}, bf16[256,1024]{1,0:T(8,128)(2,1)}, f32[256,640]{1,0:T(8,128)}, f32[256,640]{1,...) custom-call(bf16[2,512,256]{2,1,0:T(8,128)(2,1)} %get-tuple-element., ...), custom_call_target="tpu_custom_call" | custom-call | tf_op jit(solution)/shard_map/pallas_call | solution.py:69
  127.2 17.5 %shard_map.277 = (f32[256,640]{1,0:T(8,128)}, bf16[256,640]{1,0:T(8,128)(2,1)}, bf16[256,2048]{1,0:T(8,128)(2,1)}, bf16[256,2048]{1,0:T(8,128)(2,1)}, bf16[256,6...) custom-call(bf16[256,640]{1,0:T(8,128)(2,1)} %bitcast.129, ...), custom_call_target="tpu_custom_call" | custom-call | tf_op jit(solution)/shard_map/pallas_call | solution.py:69
  148.8 4.8 %collective-permute-done.27 = bf16[2,128,512]{2,1,0:T(8,128)(2,1)S(1)} collective-permute-done((bf16[2,128,512]{2,1,0:T(8,128)(2,1)}, bf16[2,128,512]{2,1,0:T(8,128)(2,1)S(1)}, u32[]{:S(2)}, u32[]{:S(2)}) %collective-permute-start.27) | collective-permute-done | bytes 262176 | tf_op jit(solution)/shard_map/ppermute | solution.py:635
  158.3 5.1 %collective-permute-start.26 = (bf16[2,128,512]{2,1,0:T(8,128)(2,1)S(1)}, bf16[2,128,512]{2,1,0:T(8,128)(2,1)S(1)}, u32[]{:S(2)}, u32[]{:S(2)}) collective-permute-start(bf16[2,128,512]{2,1,0:T(8,128)(2,1)S(1)} %add_convert_fusion.20), channel_id=1, source_target_pairs={{0,8},{2,10},{4,12},{6,14},{8,0},{10,2},{12,4},{14,6},{1,9},{3,11}... | collective-permute-start | bytes 786440 | tf_op jit(solution)/shard_map/ppermute | solution.py:635
  169.8 8.5 %collective-permute-done.26 = bf16[2,128,512]{2,1,0:T(8,128)(2,1)S(1)} collective-permute-done((bf16[2,128,512]{2,1,0:T(8,128)(2,1)S(1)}, bf16[2,128,512]{2,1,0:T(8,128)(2,1)S(1)}, u32[]{:S(2)}, u32[]{:S(2)}) %collective-permute-start.26) | collective-permute-done | bytes 262176 | tf_op jit(solution)/shard_map/ppermute | solution.py:635
  179.1 4.5 shard_map.279
  185.1 7.6 %collective-permute-done.30 = bf16[256,640]{1,0:T(8,128)(2,1)S(1)} collective-permute-done((bf16[256,640]{1,0:T(8,128)(2,1)}, bf16[256,640]{1,0:T(8,128)(2,1)S(1)}, u32[]{:S(2)}, u32[]{:S(2)}) %collective-permute-start.30) | collective-permute-done | bytes 327712 | tf_op jit(solution)/shard_map/ppermute | solution.py:819
  193.5 17.5 %shard_map.280 = (f32[256,640]{1,0:T(8,128)}, bf16[256,640]{1,0:T(8,128)(2,1)}, bf16[256,2048]{1,0:T(8,128)(2,1)}, bf16[256,2048]{1,0:T(8,128)(2,1)}, bf16[256,6...) custom-call(bf16[256,640]{1,0:T(8,128)(2,1)} %broadcast_select_fusio, ...), custom_call_target="tpu_custom_call" | custom-call | tf_op jit(solution)/shard_map/pallas_call | solution.py:69
  225.8 5.3 %collective-permute-start.34 = (bf16[2,128,512]{2,1,0:T(8,128)(2,1)}, bf16[2,128,512]{2,1,0:T(8,128)(2,1)}, u32[]{:S(2)}, u32[]{:S(2)}) collective-permute-start(bf16[2,128,512]{2,1,0:T(8,128)(2,1)} %add_convert_fusion.17), channel_id=1, source_target_pairs={{0,8},{2,10},{4,12},{6,14},{8,0},{10,2},{12,4},{14,6},{1,9},{3,11}... | collective-permute-start | bytes 786440 | tf_op jit(solution)/shard_map/ppermute | solution.py:635
  241.5 8.0 %collective-permute-done.34 = bf16[2,128,512]{2,1,0:T(8,128)(2,1)} collective-permute-done((bf16[2,128,512]{2,1,0:T(8,128)(2,1)}, bf16[2,128,512]{2,1,0:T(8,128)(2,1)}, u32[]{:S(2)}, u32[]{:S(2)}) %collective-permute-start.34) | collective-permute-done | bytes 262176 | tf_op jit(solution)/shard_map/ppermute | solution.py:635
  263.7 6.4 %collective-permute-done.52 = bf16[256,640]{1,0:T(8,128)(2,1)S(1)} collective-permute-done((bf16[256,640]{1,0:T(8,128)(2,1)S(1)}, bf16[256,640]{1,0:T(8,128)(2,1)S(1)}, u32[]{:S(2)}, u32[]{:S(2)}) %collective-permute-start.52) | collective-permute-done | bytes 327712 | tf_op jit(solution)/shard_map/ppermute | solution.py:635
  271.8 8.3 %collective-permute-done.46 = bf16[176,512]{1,0:T(8,128)(2,1)S(1)} collective-permute-done((bf16[176,512]{1,0:T(8,128)(2,1)S(1)}, bf16[176,512]{1,0:T(8,128)(2,1)S(1)}, u32[]{:S(2)}, u32[]{:S(2)}) %collective-permute-start.46) | collective-permute-done | bytes 180256 | tf_op jit(solution)/shard_map/ppermute | solution.py:635
  280.1 5.2 %collective-permute-start.53 = (bf16[256,640]{1,0:T(8,128)(2,1)S(1)}, bf16[256,640]{1,0:T(8,128)(2,1)S(1)}, u32[]{:S(2)}, u32[]{:S(2)}) collective-permute-start(bf16[256,640]{1,0:T(8,128)(2,1)S(1)} %add_convert_fusion.12), channel_id=1, source_target_pairs={{0,4},{2,6},{12,8},{14,10},{1,5},{3,7},{13,9},{15,11},{16,20},{18,... | collective-permute-start | bytes 983048 | tf_op jit(solution)/shard_map/ppermute | solution.py:691
  286.9 9.1 %collective-permute-done.47 = bf16[176,512]{1,0:T(8,128)(2,1)S(1)} collective-permute-done((bf16[176,512]{1,0:T(8,128)(2,1)S(1)}, bf16[176,512]{1,0:T(8,128)(2,1)S(1)}, u32[]{:S(2)}, u32[]{:S(2)}) %collective-permute-start.47) | collective-permute-done | bytes 180256 | tf_op jit(solution)/shard_map/ppermute | solution.py:691
  314.2 7.2 %collective-permute-done.49 = bf16[176,512]{1,0:T(8,128)(2,1)S(1)} collective-permute-done((bf16[176,512]{1,0:T(8,128)(2,1)S(1)}, bf16[176,512]{1,0:T(8,128)(2,1)S(1)}, u32[]{:S(2)}, u32[]{:S(2)}) %collective-permute-start.49) | collective-permute-done | bytes 180256 | tf_op jit(solution)/shard_map/ppermute | solution.py:693
  325.5 25.9 %collective-permute-done.50 = bf16[176,512]{1,0:T(8,128)(2,1)S(1)} collective-permute-done((bf16[176,512]{1,0:T(8,128)(2,1)S(1)}, bf16[176,512]{1,0:T(8,128)(2,1)S(1)}, u32[]{:S(2)}, u32[]{:S(2)}) %collective-permute-start.50) | collective-permute-done | bytes 180256 | tf_op jit(solution)/shard_map/ppermute | solution.py:635
  357.9 5.3 %collective-permute-start.71 = (bf16[512,640]{1,0:T(8,128)(2,1)S(1)}, bf16[512,640]{1,0:T(8,128)(2,1)S(1)}, u32[]{:S(2)}, u32[]{:S(2)}) collective-permute-start(bf16[512,640]{1,0:T(8,128)(2,1)S(1)} %add_convert_fusion.3), channel_id=1, source_target_pairs={{0,4},{2,6},{12,8},{14,10},{1,5},{3,7},{13,9},{15,11},{16,20},{18,... | collective-permute-start | bytes 1966088 | tf_op jit(solution)/shard_map/ppermute | solution.py:691
  383.1 9.2 %collective-permute-done.65 = bf16[160,2048]{1,0:T(8,128)(2,1)S(1)} collective-permute-done((bf16[160,2048]{1,0:T(8,128)(2,1)S(1)}, bf16[160,2048]{1,0:T(8,128)(2,1)S(1)}, u32[]{:S(2)}, u32[]{:S(2)}) %collective-permute-start.65) | collective-permute-done | bytes 655392 | tf_op jit(solution)/shard_map/ppermute | solution.py:691
  393.2 9.5 %collective-permute-done.59 = bf16[160,2048]{1,0:T(8,128)(2,1)S(1)} collective-permute-done((bf16[160,2048]{1,0:T(8,128)(2,1)S(1)}, bf16[160,2048]{1,0:T(8,128)(2,1)S(1)}, u32[]{:S(2)}, u32[]{:S(2)}) %collective-permute-start.59) | collective-permute-done | bytes 655392 | tf_op jit(solution)/shard_map/ppermute | solution.py:691
  408.2 17.8 %collective-permute-done.73 = bf16[512,640]{1,0:T(8,128)(2,1)S(1)} collective-permute-done((bf16[512,640]{1,0:T(8,128)(2,1)S(1)}, bf16[512,640]{1,0:T(8,128)(2,1)S(1)}, u32[]{:S(2)}, u32[]{:S(2)}) %collective-permute-start.73) | collective-permute-done | bytes 655392 | tf_op jit(solution)/shard_map/ppermute | solution.py:693
  427.7 12.3 %collective-permute-done.67 = bf16[160,2048]{1,0:T(8,128)(2,1)S(1)} collective-permute-done((bf16[160,2048]{1,0:T(8,128)(2,1)S(1)}, bf16[160,2048]{1,0:T(8,128)(2,1)S(1)}, u32[]{:S(2)}, u32[]{:S(2)}) %collective-permute-start.67) | collective-permute-done | bytes 655392 | tf_op jit(solution)/shard_map/ppermute | solution.py:693
  441.7 7.8 %collective-permute-done.61 = bf16[160,2048]{1,0:T(8,128)(2,1)S(1)} collective-permute-done((bf16[160,2048]{1,0:T(8,128)(2,1)S(1)}, bf16[160,2048]{1,0:T(8,128)(2,1)S(1)}, u32[]{:S(2)}, u32[]{:S(2)}) %collective-permute-start.61) | collective-permute-done | bytes 655392 | tf_op jit(solution)/shard_map/ppermute | solution.py:693
  455.5 9.3 %collective-permute-done.62 = bf16[160,2048]{1,0:T(8,128)(2,1)S(1)} collective-permute-done((bf16[160,2048]{1,0:T(8,128)(2,1)S(1)}, bf16[160,2048]{1,0:T(8,128)(2,1)S(1)}, u32[]{:S(2)}, u32[]{:S(2)}) %collective-permute-start.62) | collective-permute-done | bytes 655392 | tf_op jit(solution)/shard_map/ppermute | solution.py:635
  (329 shorter events, 181.2 us)
Async XLA Ops:
  13.6 23.1 %collective-permute-start.7 = (bf16[2,128,512]{2,1,0:T(8,128)(2,1)}, bf16[2,128,512]{2,1,0:T(8,128)(2,1)S(1)}, u32[]{:S(2)}, u32[]{:S(2)}) collective-permute-start(bf16[2,128,512]{2,1,0:T(8,128)(2,1)} %bitcast.133), channel_id=1, source_target_pairs={{0,8},{2,10},{4,12},{6,14},{8,0},{10,2},{12,4},{14,6},{1,9},{3,11}... | collective-permute-start | bytes 786440 | tf_op jit(solution)/shard_map/ppermute | solution.py:635
  14.2 22.5 %collective-permute-start.4 = (bf16[2,128,512]{2,1,0:T(8,128)(2,1)}, bf16[2,128,512]{2,1,0:T(8,128)(2,1)S(1)}, u32[]{:S(2)}, u32[]{:S(2)}) collective-permute-start(bf16[2,128,512]{2,1,0:T(8,128)(2,1)} %bitcast.134), channel_id=1, source_target_pairs={{0,2},{2,0},{4,6},{6,4},{8,10},{10,8},{12,14},{14,12},{1,3},{3,1},... | collective-permute-start | bytes 786440 | tf_op jit(solution)/shard_map/ppermute | solution.py:635
  15.9 22.2 %collective-permute-start.3 = (bf16[320,1024]{1,0:T(8,128)(2,1)}, bf16[320,1024]{1,0:T(8,128)(2,1)}, u32[]{:S(2)}, u32[]{:S(2)}) collective-permute-start(bf16[320,1024]{1,0:T(8,128)(2,1)} %bitcast.105), channel_id=1, source_target_pairs={{0,1},{1,0},{2,3},{3,2},{4,5},{5,4},{6,7},{7,6},{8,9},{9,8},{10,11... | collective-permute-start | bytes 1966088 | tf_op jit(solution)/shard_map/ppermute | solution.py:635
  21.1 36.5 %collective-permute-start.12 = (bf16[320,2048]{1,0:T(8,128)(2,1)S(1)}, bf16[320,2048]{1,0:T(8,128)(2,1)S(1)}, u32[]{:S(2)}, u32[]{:S(2)}) collective-permute-start(bf16[320,2048]{1,0:T(8,128)(2,1)S(1)} %bitcast.89), channel_id=1, source_target_pairs={{0,1},{1,0},{2,3},{3,2},{4,5},{5,4},{6,7},{7,6},{8,9},{9,8},{10,11... | collective-permute-start | bytes 3932168 | tf_op jit(solution)/shard_map/ppermute | solution.py:635
  27.4 30.1 %collective-permute-start.13 = (bf16[320,2048]{1,0:T(8,128)(2,1)}, bf16[320,2048]{1,0:T(8,128)(2,1)}, u32[]{:S(2)}, u32[]{:S(2)}) collective-permute-start(bf16[320,2048]{1,0:T(8,128)(2,1)} %bitcast.90), channel_id=1, source_target_pairs={{0,1},{1,0},{2,3},{3,2},{4,5},{5,4},{6,7},{7,6},{8,9},{9,8},{10,11... | collective-permute-start | bytes 3932168 | tf_op jit(solution)/shard_map/ppermute | solution.py:635
  36.7 20.8 %collective-permute-start.14 = (bf16[1024,640]{1,0:T(8,128)(2,1)}, bf16[1024,640]{1,0:T(8,128)(2,1)}, u32[]{:S(2)}, u32[]{:S(2)}) collective-permute-start(bf16[1024,640]{1,0:T(8,128)(2,1)} %bitcast.95), channel_id=1, source_target_pairs={{0,1},{1,0},{2,3},{3,2},{4,5},{5,4},{6,7},{7,6},{8,9},{9,8},{10,11... | collective-permute-start | bytes 3932168 | tf_op jit(solution)/shard_map/ppermute | solution.py:635
  82.5 21.6 %collective-permute-start.19 = (bf16[2,128,512]{2,1,0:T(8,128)(2,1)}, bf16[2,128,512]{2,1,0:T(8,128)(2,1)S(1)}, u32[]{:S(2)}, u32[]{:S(2)}) collective-permute-start(bf16[2,128,512]{2,1,0:T(8,128)(2,1)} %bitcast.123), channel_id=1, source_target_pairs={{0,8},{2,10},{4,12},{6,14},{8,0},{10,2},{12,4},{14,6},{1,9},{3,11}... | collective-permute-start | bytes 786440 | tf_op jit(solution)/shard_map/ppermute | solution.py:635
  85.5 20.0 %collective-permute-start.21 = (bf16[2,128,512]{2,1,0:T(8,128)(2,1)}, bf16[2,128,512]{2,1,0:T(8,128)(2,1)S(1)}, u32[]{:S(2)}, u32[]{:S(2)}) collective-permute-start(bf16[2,128,512]{2,1,0:T(8,128)(2,1)} %bitcast.124), channel_id=1, source_target_pairs={{0,12},{2,14},{4,8},{6,10},{8,4},{10,6},{12,0},{14,2},{1,13},{3,15... | collective-permute-start | bytes 786440 | tf_op jit(solution)/shard_map/ppermute | solution.py:635
  86.9 24.6 %collective-permute-start.16 = (bf16[2,128,512]{2,1,0:T(8,128)(2,1)}, bf16[2,128,512]{2,1,0:T(8,128)(2,1)S(1)}, u32[]{:S(2)}, u32[]{:S(2)}) collective-permute-start(bf16[2,128,512]{2,1,0:T(8,128)(2,1)} %bitcast.125), channel_id=1, source_target_pairs={{0,2},{2,0},{4,6},{6,4},{8,10},{10,8},{12,14},{14,12},{1,3},{3,1},... | collective-permute-start | bytes 786440 | tf_op jit(solution)/shard_map/ppermute | solution.py:635
  148.3 21.4 %collective-permute-start.29 = (bf16[2,128,512]{2,1,0:T(8,128)(2,1)}, bf16[2,128,512]{2,1,0:T(8,128)(2,1)S(1)}, u32[]{:S(2)}, u32[]{:S(2)}) collective-permute-start(bf16[2,128,512]{2,1,0:T(8,128)(2,1)} %get-tuple-element.89), channel_id=1, source_target_pairs={{0,2},{2,0},{4,6},{6,4},{8,10},{10,8},{12,14},{14,12},{1,3},{3,1},... | collective-permute-start | bytes 786440 | tf_op jit(solution)/shard_map/ppermute | solution.py:635
  158.3 20.0 %collective-permute-start.26 = (bf16[2,128,512]{2,1,0:T(8,128)(2,1)S(1)}, bf16[2,128,512]{2,1,0:T(8,128)(2,1)S(1)}, u32[]{:S(2)}, u32[]{:S(2)}) collective-permute-start(bf16[2,128,512]{2,1,0:T(8,128)(2,1)S(1)} %add_convert_fusion.20), channel_id=1, source_target_pairs={{0,8},{2,10},{4,12},{6,14},{8,0},{10,2},{12,4},{14,6},{1,9},{3,11}... | collective-permute-start | bytes 786440 | tf_op jit(solution)/shard_map/ppermute | solution.py:635
  214.6 26.4 %collective-permute-start.37 = (bf16[2,128,512]{2,1,0:T(8,128)(2,1)}, bf16[2,128,512]{2,1,0:T(8,128)(2,1)S(1)}, u32[]{:S(2)}, u32[]{:S(2)}) collective-permute-start(bf16[2,128,512]{2,1,0:T(8,128)(2,1)} %get-tuple-element.103), channel_id=1, source_target_pairs={{0,2},{2,0},{4,6},{6,4},{8,10},{10,8},{12,14},{14,12},{1,3},{3,1},... | collective-permute-start | bytes 786440 | tf_op jit(solution)/shard_map/ppermute | solution.py:635
  221.0 36.5 %collective-permute-start.51 = (bf16[512,640]{1,0:T(8,128)(2,1)}, bf16[512,640]{1,0:T(8,128)(2,1)S(1)}, u32[]{:S(2)}, u32[]{:S(2)}) collective-permute-start(bf16[512,640]{1,0:T(8,128)(2,1)} %convolution_convert_fusion.3), channel_id=1, source_target_pairs={{0,1},{1,0},{2,3},{3,2},{4,5},{5,4},{6,7},{7,6},{8,9},{9,8},{10,11... | collective-permute-start | bytes 1966088 | tf_op jit(solution)/shard_map/ppermute | solution.py:635
  225.8 23.7 %collective-permute-start.34 = (bf16[2,128,512]{2,1,0:T(8,128)(2,1)}, bf16[2,128,512]{2,1,0:T(8,128)(2,1)}, u32[]{:S(2)}, u32[]{:S(2)}) collective-permute-start(bf16[2,128,512]{2,1,0:T(8,128)(2,1)} %add_convert_fusion.17), channel_id=1, source_target_pairs={{0,8},{2,10},{4,12},{6,14},{8,0},{10,2},{12,4},{14,6},{1,9},{3,11}... | collective-permute-start | bytes 786440 | tf_op jit(solution)/shard_map/ppermute | solution.py:635
  241.0 59.5 %collective-permute-start.69 = (bf16[1024,640]{1,0:T(8,128)(2,1)S(1)}, bf16[1024,640]{1,0:T(8,128)(2,1)}, u32[]{:S(2)}, u32[]{:S(2)}) collective-permute-start(bf16[1024,640]{1,0:T(8,128)(2,1)S(1)} %convolution_convert_fusion.2), channel_id=1, source_target_pairs={{0,1},{1,0},{2,3},{3,2},{4,5},{5,4},{6,7},{7,6},{8,9},{9,8},{10,11... | collective-permute-start | bytes 3932168 | tf_op jit(solution)/shard_map/ppermute | solution.py:635
  241.1 63.0 %collective-permute-start.63 = (bf16[320,2048]{1,0:T(8,128)(2,1)}, bf16[320,2048]{1,0:T(8,128)(2,1)}, u32[]{:S(2)}, u32[]{:S(2)}) collective-permute-start(bf16[320,2048]{1,0:T(8,128)(2,1)} %convolution_convert_fusion), channel_id=1, source_target_pairs={{0,1},{1,0},{2,3},{3,2},{4,5},{5,4},{6,7},{7,6},{8,9},{9,8},{10,11... | collective-permute-start | bytes 3932168 | tf_op jit(solution)/shard_map/ppermute | solution.py:635
  257.4 51.0 %collective-permute-start.57 = (bf16[320,2048]{1,0:T(8,128)(2,1)}, bf16[320,2048]{1,0:T(8,128)(2,1)S(1)}, u32[]{:S(2)}, u32[]{:S(2)}) collective-permute-start(bf16[320,2048]{1,0:T(8,128)(2,1)} %convolution_convert_fusion.1), channel_id=1, source_target_pairs={{0,1},{1,0},{2,3},{3,2},{4,5},{5,4},{6,7},{7,6},{8,9},{9,8},{10,11... | collective-permute-start | bytes 3932168 | tf_op jit(solution)/shard_map/ppermute | solution.py:635
  262.7 22.8 %collective-permute-start.39 = (bf16[160,1024]{1,0:T(8,128)(2,1)S(1)}, bf16[160,1024]{1,0:T(8,128)(2,1)S(1)}, u32[]{:S(2)}, u32[]{:S(2)}) collective-permute-start(bf16[160,1024]{1,0:T(8,128)(2,1)S(1)} %constant_dynamic-slice_fusion.4), channel_id=1, source_target_pairs={{0,2},{2,0},{4,6},{6,4},{8,10},{10,8},{12,14},{14,12},{1,3},{3,1},... | collective-permute-start | bytes 983048 | tf_op jit(solution)/shard_map/ppermute | solution.py:635
  280.1 30.9 %collective-permute-start.53 = (bf16[256,640]{1,0:T(8,128)(2,1)S(1)}, bf16[256,640]{1,0:T(8,128)(2,1)S(1)}, u32[]{:S(2)}, u32[]{:S(2)}) collective-permute-start(bf16[256,640]{1,0:T(8,128)(2,1)S(1)} %add_convert_fusion.12), channel_id=1, source_target_pairs={{0,4},{2,6},{12,8},{14,10},{1,5},{3,7},{13,9},{15,11},{16,20},{18,... | collective-permute-start | bytes 983048 | tf_op jit(solution)/shard_map/ppermute | solution.py:691
  304.0 52.5 %collective-permute-start.70 = (bf16[512,640]{1,0:T(8,128)(2,1)}, bf16[512,640]{1,0:T(8,128)(2,1)}, u32[]{:S(2)}, u32[]{:S(2)}) collective-permute-start(bf16[512,640]{1,0:T(8,128)(2,1)} %constant_dynamic-slice_fusion), channel_id=1, source_target_pairs={{0,2},{2,0},{4,6},{6,4},{8,10},{10,8},{12,14},{14,12},{1,3},{3,1},... | collective-permute-start | bytes 1966088 | tf_op jit(solution)/shard_map/ppermute | solution.py:635
  308.4 54.7 %collective-permute-start.64 = (bf16[160,2048]{1,0:T(8,128)(2,1)}, bf16[160,2048]{1,0:T(8,128)(2,1)}, u32[]{:S(2)}, u32[]{:S(2)}) collective-permute-start(bf16[160,2048]{1,0:T(8,128)(2,1)} %constant_dynamic-slice_fusion.1), channel_id=1, source_target_pairs={{0,2},{2,0},{4,6},{6,4},{8,10},{10,8},{12,14},{14,12},{1,3},{3,1},... | collective-permute-start | bytes 1966088 | tf_op jit(solution)/shard_map/ppermute | solution.py:635
  311.0 57.5 %collective-permute-start.58 = (bf16[160,2048]{1,0:T(8,128)(2,1)}, bf16[160,2048]{1,0:T(8,128)(2,1)}, u32[]{:S(2)}, u32[]{:S(2)}) collective-permute-start(bf16[160,2048]{1,0:T(8,128)(2,1)} %constant_dynamic-slice_fusion.2), channel_id=1, source_target_pairs={{0,2},{2,0},{4,6},{6,4},{8,10},{10,8},{12,14},{14,12},{1,3},{3,1},... | collective-permute-start | bytes 1966088 | tf_op jit(solution)/shard_map/ppermute | solution.py:635
  322.1 29.2 %collective-permute-start.50 = (bf16[176,512]{1,0:T(8,128)(2,1)S(1)}, bf16[176,512]{1,0:T(8,128)(2,1)S(1)}, u32[]{:S(2)}, u32[]{:S(2)}) collective-permute-start(bf16[176,512]{1,0:T(8,128)(2,1)S(1)} %broadcast_select_fusion.7), channel_id=1, source_target_pairs={{0,2},{2,0},{4,6},{6,4},{8,10},{10,8},{12,14},{14,12},{1,3},{3,1},... | collective-permute-start | bytes 540680 | tf_op jit(solution)/shard_map/ppermute | solution.py:635
  324.1 41.8 %collective-permute-start.55 = (bf16[256,640]{1,0:T(8,128)(2,1)}, bf16[256,640]{1,0:T(8,128)(2,1)}, u32[]{:S(2)}, u32[]{:S(2)}) collective-permute-start(bf16[256,640]{1,0:T(8,128)(2,1)} %add_convert_fusion.10), channel_id=1, source_target_pairs={{4,0},{6,2},{8,12},{10,14},{5,1},{7,3},{9,13},{11,15},{20,16},{22,... | collective-permute-start | bytes 983048 | tf_op jit(solution)/shard_map/ppermute | solution.py:693
  357.9 24.4 %collective-permute-start.71 = (bf16[512,640]{1,0:T(8,128)(2,1)S(1)}, bf16[512,640]{1,0:T(8,128)(2,1)S(1)}, u32[]{:S(2)}, u32[]{:S(2)}) collective-permute-start(bf16[512,640]{1,0:T(8,128)(2,1)S(1)} %add_convert_fusion.3), channel_id=1, source_target_pairs={{0,4},{2,6},{12,8},{14,10},{1,5},{3,7},{13,9},{15,11},{16,20},{18,... | collective-permute-start | bytes 1966088 | tf_op jit(solution)/shard_map/ppermute | solution.py:691
  364.5 27.9 %collective-permute-start.65 = (bf16[160,2048]{1,0:T(8,128)(2,1)S(1)}, bf16[160,2048]{1,0:T(8,128)(2,1)S(1)}, u32[]{:S(2)}, u32[]{:S(2)}) collective-permute-start(bf16[160,2048]{1,0:T(8,128)(2,1)S(1)} %add_convert_fusion.6), channel_id=1, source_target_pairs={{0,4},{2,6},{12,8},{14,10},{1,5},{3,7},{13,9},{15,11},{16,20},{18,... | collective-permute-start | bytes 1966088 | tf_op jit(solution)/shard_map/ppermute | solution.py:691
  369.8 33.0 %collective-permute-start.59 = (bf16[160,2048]{1,0:T(8,128)(2,1)S(1)}, bf16[160,2048]{1,0:T(8,128)(2,1)S(1)}, u32[]{:S(2)}, u32[]{:S(2)}) collective-permute-start(bf16[160,2048]{1,0:T(8,128)(2,1)S(1)} %add_convert_fusion.9), channel_id=1, source_target_pairs={{0,4},{2,6},{12,8},{14,10},{1,5},{3,7},{13,9},{15,11},{16,20},{18,... | collective-permute-start | bytes 1966088 | tf_op jit(solution)/shard_map/ppermute | solution.py:691
  382.4 21.2 %collective-permute-start.72 = (bf16[512,640]{1,0:T(8,128)(2,1)S(1)}, bf16[512,640]{1,0:T(8,128)(2,1)S(1)}, u32[]{:S(2)}, u32[]{:S(2)}) collective-permute-start(bf16[512,640]{1,0:T(8,128)(2,1)S(1)} %add_convert_fusion.2), channel_id=1, source_target_pairs={{4,8},{6,10},{8,4},{10,6},{5,9},{7,11},{9,5},{11,7},{20,24},{22,26... | collective-permute-start | bytes 1966088 | tf_op jit(solution)/shard_map/ppermute | solution.py:692
  403.9 22.1 %collective-permute-start.73 = (bf16[512,640]{1,0:T(8,128)(2,1)S(1)}, bf16[512,640]{1,0:T(8,128)(2,1)S(1)}, u32[]{:S(2)}, u32[]{:S(2)}) collective-permute-start(bf16[512,640]{1,0:T(8,128)(2,1)S(1)} %add_convert_fusion.1), channel_id=1, source_target_pairs={{4,0},{6,2},{8,12},{10,14},{5,1},{7,3},{9,13},{11,15},{20,16},{22,... | collective-permute-start | bytes 1966088 | tf_op jit(solution)/shard_map/ppermute | solution.py:693
  405.4 34.6 %collective-permute-start.67 = (bf16[160,2048]{1,0:T(8,128)(2,1)S(1)}, bf16[160,2048]{1,0:T(8,128)(2,1)S(1)}, u32[]{:S(2)}, u32[]{:S(2)}) collective-permute-start(bf16[160,2048]{1,0:T(8,128)(2,1)S(1)} %add_convert_fusion.4), channel_id=1, source_target_pairs={{4,0},{6,2},{8,12},{10,14},{5,1},{7,3},{9,13},{11,15},{20,16},{22,... | collective-permute-start | bytes 1966088 | tf_op jit(solution)/shard_map/ppermute | solution.py:693
  406.9 42.6 %collective-permute-start.61 = (bf16[160,2048]{1,0:T(8,128)(2,1)S(1)}, bf16[160,2048]{1,0:T(8,128)(2,1)S(1)}, u32[]{:S(2)}, u32[]{:S(2)}) collective-permute-start(bf16[160,2048]{1,0:T(8,128)(2,1)S(1)} %add_convert_fusion.7), channel_id=1, source_target_pairs={{4,0},{6,2},{8,12},{10,14},{5,1},{7,3},{9,13},{11,15},{20,16},{22,... | collective-permute-start | bytes 1966088 | tf_op jit(solution)/shard_map/ppermute | solution.py:693
  426.0 25.2 %collective-permute-start.74 = (bf16[512,640]{1,0:T(8,128)(2,1)S(1)}, bf16[512,640]{1,0:T(8,128)(2,1)S(1)}, u32[]{:S(2)}, u32[]{:S(2)}) collective-permute-start(bf16[512,640]{1,0:T(8,128)(2,1)S(1)} %broadcast_select_fusion), channel_id=1, source_target_pairs={{0,2},{2,0},{4,6},{6,4},{8,10},{10,8},{12,14},{14,12},{1,3},{3,1},... | collective-permute-start | bytes 1966088 | tf_op jit(solution)/shard_map/ppermute | solution.py:635
  (91 other events, 833.5 us)

commit v3 on v2

--- a/solution.py
+++ b/solution.py
@@ -371,28 +371,20 @@
     )
 
 
-def backward_kernel(sz, block_count, *refs):
-    (
-        grad_ref, gain_own, gain_other, down_out, gate_ref, up_ref, middle, branch,
-        query_low, log_row, key_col, query_row,
-    ) = refs[:12]
-    refs = refs[12:]
-    blocks, refs = refs[:block_count], refs[block_count:]
+def ffw_back_kernel(sz, *refs):
+    grad_ref, gain_own, gain_other, down_out, gate_ref, up_ref, middle, branch = refs[:8]
+    refs = refs[8:]
     out_pair, gate_pair, up_pair, down_pair = (refs[2 * i : 2 * i + 2] for i in range(4))
     refs = refs[8:]
     (
         middle_grad, down_grad, gate_grad, up_grad, branch_grad, gain_post_grad, gain_pre_grad,
-        gain_attn_grad, query_grad,
+        gain_attn_grad, attn_grad,
     ) = refs[:9]
-    refs = refs[9:]
-    parts, refs = refs[:block_count], refs[block_count:]
-    kv, w_out, w_gate, w_up, w_down, key_sum, value_sum, sems = refs
+    w_out, w_gate, w_up, w_down, sems = refs[9:]
     down_copies = start_halves(*down_pair, w_down, sems, 0)
     gate_copies = start_halves(*gate_pair, w_gate, sems, 2)
     up_copies = start_halves(*up_pair, w_up, sems, 4)
     out_copies = start_halves(*out_pair, w_out, sems, 6)
-    if block_count > 1:
-        kv_copies = start_blocks(sz, blocks, kv, sems, 8)
     gain_attn = whole_gain(gain_own, gain_other, *sz.gain_at["attn"])
     gain_pre = whole_gain(gain_own, gain_other, *sz.gain_at["pre"])
     gain_post = whole_gain(gain_own, gain_other, *sz.gain_at["post"])
@@ -428,9 +420,18 @@
     branch_low = branch_part.astype(bf16)
     branch_grad[...] = branch_low
     wait_all(out_copies)
-    attn_grad = dot_nt(branch_low, w_out[...]).astype(bf16)
+    attn_grad[...] = dot_nt(branch_low, w_out[...]).astype(bf16)
+
+
+def attn_back_kernel(sz, block_count, *refs):
+    attn_grad, query_low, log_row, key_col, query_row = refs[:5]
+    refs = refs[5:]
+    blocks, refs = refs[:block_count], refs[block_count:]
+    query_grad, refs = refs[0], refs[1:]
+    parts, refs = refs[:block_count], refs[block_count:]
+    kv, key_sum, value_sum, sems = refs
     if block_count > 1:
-        wait_all(kv_copies)
+        wait_all(start_blocks(sz, blocks, kv, sems, 0))
     spans = sz.keys // sz.span
     heads_in = sz.chunk // sz.tokens
     chunks = range(0, sz.head_rows, sz.chunk)
@@ -481,7 +482,7 @@
                 parts[index][group, :, : sz.head_dim] = key_sum[at, :].astype(bf16)
                 parts[index][group, :, sz.head_dim :] = value_sum[at, :].astype(bf16)
             continue
-        load_group(sz, blocks[0], group, kv, sems, 8)
+        load_group(sz, blocks[0], group, kv, sems, 0)
         deltas = []
         for first in chunks:
 
@@ -511,7 +512,7 @@
         lax.fori_loop(0, spans, add_span, 0)
 
 
-def backward_layer(sz, grad, gains, saved, places, blocks, weights):
+def ffw_back(sz, grad, gains, saved, weights):
     rows, model = sz.rows, sz.model
     gain = struct((1, model), f32)
     outs = [
@@ -523,29 +524,71 @@
         gain,
         gain,
         gain,
-        struct((sz.groups, sz.head_rows, sz.head_dim), f32),
+        struct((rows, sz.query_cols), bf16),
     ]
-    outs += [struct(block.shape, bf16) for block in blocks]
     scratch = [
-        pltpu.VMEM((sz.groups if len(blocks) > 1 else 1, sz.keys, 2 * sz.head_dim), bf16),
         pltpu.VMEM((sz.query_cols, model), bf16),
         pltpu.VMEM((model, sz.ff), bf16),
         pltpu.VMEM((model, sz.ff), bf16),
         pltpu.VMEM((sz.ff, model), bf16),
-        pltpu.VMEM((sz.span, sz.head_dim), f32),
-        pltpu.VMEM((sz.span, sz.head_dim), f32),
-        pltpu.SemaphoreType.DMA((8 + sz.blocks,)),
+        pltpu.SemaphoreType.DMA((8,)),
     ]
     inputs = [
         grad, *gains, saved["down_out"], saved["gate"], saved["up"], saved["middle"],
-        saved["branch"], saved["query_low"], saved["log_row"], places["key_col"],
-        places["query_row"],
+        saved["branch"],
     ]
-    far = [*blocks, *weights["out"], *weights["gate"], *weights["up"], *weights["down"]]
+    far = [*weights["out"], *weights["gate"], *weights["up"], *weights["down"]]
+    return call_kernel(functools.partial(ffw_back_kernel, sz), outs, inputs, far, scratch)
+
+
+def attn_back(sz, attn_grad, saved, places):
+    blocks = saved["blocks"]
+    outs = [struct((sz.groups, sz.head_rows, sz.head_dim), f32)]
+    outs += [struct(block.shape, bf16) for block in blocks]
+    scratch = [
+        pltpu.VMEM((sz.groups if len(blocks) > 1 else 1, sz.keys, 2 * sz.head_dim), bf16),
+        pltpu.VMEM((sz.span, sz.head_dim), f32),
+        pltpu.VMEM((sz.span, sz.head_dim), f32),
+        pltpu.SemaphoreType.DMA((sz.blocks,)),
+    ]
+    inputs = [
+        attn_grad, saved["query_low"], saved["log_row"], places["key_col"], places["query_row"]
+    ]
     got = call_kernel(
-        functools.partial(backward_kernel, sz, len(blocks)), outs, inputs, far, scratch
-    )
-    return got[:9], got[9:]
+        functools.partial(attn_back_kernel, sz, len(blocks)), outs, inputs, blocks, scratch
+    )
+    return got[0], got[1:]
+
+
+def weight_kernel(sz, cuts, left, right, *refs):
+    outs, turned = refs[:-1], refs[-1]
+    turned[...] = left[...].T
+    half = left.shape[1] // 2
+    fsdp_index = lax.axis_index("fsdp")
+    y_index = lax.axis_index("ctx") & 1
+    for side, owner in ((0, 1 - fsdp_index), (1, fsdp_index)):
+        for part, y_half in ((0, y_index), (1, 1 - y_index)):
+            first = pl.multiple_of(owner * half + y_half * (half // 2), 16)
+            rows = turned[pl.ds(first, half // 2), :]
+            for index, (start, stop) in enumerate(cuts):
+                outs[2 * index + side][part * (half // 2) : (part + 1) * (half // 2), :] = dot_nn(
+                    rows, right[:, start:stop]
+                ).astype(bf16)
+
+
+def weight_terms(sz, left, right, pieces):
+    half = left.shape[1] // 2
+    width = right.shape[1] // pieces
+    cuts = [(index * width, (index + 1) * width) for index in range(pieces)]
+    outs = [struct((half, width), bf16)] * (2 * pieces)
+    got = call_kernel(
+        functools.partial(weight_kernel, sz, cuts),
+        outs,
+        [left, right],
+        [],
+        [pltpu.VMEM((left.shape[1], left.shape[0]), bf16)],
+    )
+    return [(got[2 * index], got[2 * index + 1]) for index in range(pieces)]
 
 
 def query_back_kernel(
@@ -647,64 +690,118 @@
     return slots
 
 
-def gather_ctx(shard):
+def after(value, *earlier):
+    return lax.optimization_barrier((value, earlier))[0]
+
+
+def gather_ctx(shard, meanwhile):
     if not small_ctx():
         return [lax.all_gather(shard, "ctx", axis=0)]
     blocks = [None] * 8
     blocks[0] = shard
     for mask in (6, 4, 2):
         blocks[mask] = xor_permute(shard, "ctx", mask)
-    for mask in (0, 2, 4, 6):
+    blocks[1] = xor_permute(shard, "ctx", 1)
+    for mask in (2, 4, 6):
+        blocks[mask] = after(blocks[mask], meanwhile)
         blocks[mask + 1] = xor_permute(blocks[mask], "ctx", 1)
     return blocks
 
 
-def scatter_ctx(parts):
-    if len(parts) == 1:
-        return [lax.psum_scatter(parts[0].astype(f32), "ctx", scatter_dimension=0, tiled=False)]
-    terms = []
-    for mask in (6, 4, 2):
-        came = xor_permute(parts[mask + 1], "ctx", 1)
-        both = (parts[mask].astype(f32) + came.astype(f32)).astype(bf16)
-        terms.append(xor_permute(both, "ctx", mask))
-    return terms + [parts[0], xor_permute(parts[1], "ctx", 1)]
-
-
-def sum_ctx(shard):
-    if not small_ctx():
-        return lax.psum(shard.astype(f32), "ctx")
+def add_low(*terms):
+    total = terms[0].astype(f32)
+    for term in terms[1:]:
+        total = total + term.astype(f32)
+    return lax.optimization_barrier(total.astype(bf16))
+
+
+def xor_pairs(count, mask):
+    return [(i, i ^ mask) for i in range(count)]
+
+
+def scatter_stages(parts):
+    y_swap = xor_pairs(8, 1)
+    came = yield [(parts[mask + 1], "ctx", y_swap) for mask in (6, 4, 2, 0)]
+    sums = [add_low(parts[mask], got) for mask, got in zip((6, 4, 2), came)]
+    got = yield [(low, "ctx", xor_pairs(8, mask)) for low, mask in zip(sums, (6, 4, 2))]
+    return list(got) + [parts[0], came[3]]
+
+
+def sum_stages(make):
+    send, keep = make()
     ctx_index = lax.axis_index("ctx")
     y_index = ctx_index & 1
     z_index = ctx_index >> 1
-    half = shard.shape[0] // 2
-    keep = lax.dynamic_slice_in_dim(shard, y_index * half, half, 0)
-    send = lax.dynamic_slice_in_dim(shard, (1 - y_index) * half, half, 0)
-    came = xor_permute(send, "ctx", 1)
+    half = send.shape[0] // 2
+    y_swap = xor_pairs(8, 1)
     inward = [(z * 2 + y, t * 2 + y) for z, t in ((0, 1), (3, 2)) for y in (0, 1)]
     middle = [(z * 2 + y, t * 2 + y) for z, t in ((1, 2), (2, 1)) for y in (0, 1)]
     outward = [(z * 2 + y, t * 2 + y) for z, t in ((1, 0), (2, 3)) for y in (0, 1)]
-
-    def add(left, right):
-        return lax.optimization_barrier((left.astype(f32) + right.astype(f32)).astype(bf16))
-
-    part = add(keep, came)
-    part = add(part, lax.ppermute(part, "ctx", inward))
-    part = add(part, lax.ppermute(part, "ctx", middle))
-    back = lax.ppermute(part, "ctx", outward)
-    total = jnp.where((z_index == 1) | (z_index == 2), part, back)
-    other = xor_permute(total, "ctx", 1)
+    (core,) = yield [(send, "fsdp", [(0, 1), (1, 0)])]
+    (came,) = yield [(add_low(keep[half:], core[half:]), "ctx", y_swap)]
+    part = add_low(keep[:half], core[:half], came)
+    (came,) = yield [(part, "ctx", inward)]
+    part = add_low(part, came)
+    (came,) = yield [(part, "ctx", middle)]
+    part = add_low(part, came)
+    (came,) = yield [(part, "ctx", outward)]
+    total = jnp.where((z_index == 1) | (z_index == 2), part, came)
+    (other,) = yield [(total, "ctx", y_swap)]
     first = jnp.where(y_index == 0, total, other)
     second = jnp.where(y_index == 0, other, total)
     return jnp.concatenate([first, second], axis=0).astype(f32)
 
 
-def weight_term(left, right):
-    half = left.shape[1] // 2
-    fsdp_index = lax.axis_index("fsdp")
-    keep = lax.dynamic_slice_in_dim(left, fsdp_index * half, half, 1)
-    send = lax.dynamic_slice_in_dim(left, (1 - fsdp_index) * half, half, 1)
-    came = xor_permute(dot_tn(send, right).astype(bf16), "fsdp", 1)
-    return (dot_tn(keep, right) + came.astype(f32)).astype(bf16)
+def sum_plain(send, keep):
+    half = send.shape[0] // 2
+    y_index = lax.axis_index("ctx") & 1
+    came = xor_permute(send, "fsdp", 1)
+    both = add_low(keep, came)
+    first = jnp.where(y_index == 0, both[:half], both[half:])
+    second = jnp.where(y_index == 0, both[half:], both[:half])
+    return lax.psum(jnp.concatenate([first, second], axis=0).astype(f32), "ctx")
+
+
+def run_staggered(sets):
+    results = {}
+    states = [dict(entries=list(one), active=[], turn=0, landed=None) for one in sets]
+    turn = 0
+    while any(st["active"] or st["turn"] < len(st["entries"]) for st in states):
+        state = states[turn % len(states)]
+        turn += 1
+        going = []
+        for (name, stage, _), landed in zip(state["active"], state["landed"] or []):
+            try:
+                going.append((name, stage, stage.send(landed)))
+            except StopIteration as end:
+                results[name] = end.value
+        if state["turn"] < len(state["entries"]):
+            for name, make_stage in state["entries"][state["turn"]]:
+                stage = make_stage(results)
+                going.append((name, stage, next(stage)))
+        state["turn"] += 1
+        state["active"] = going
+        state["landed"] = None
+        if not going:
+            continue
+        operands = [[move[0] for move in moves] for _, _, moves in going]
+        for other in states:
+            if other is not state and other["landed"] is not None:
+                other["landed"] = after(other["landed"], operands)
+        state["landed"] = [
+            [lax.ppermute(value, axis, pairs) for value, axis, pairs in moves]
+            for _, _, moves in going
+        ]
+    return results
+
+
+def run_alone(stage):
+    moves = next(stage)
+    while True:
+        try:
+            moves = stage.send([lax.ppermute(value, axis, pairs) for value, axis, pairs in moves])
+        except StopIteration as end:
+            return end.value
 
 
 def on_device(
@@ -776,8 +873,8 @@
         normed, key_lin, kv_low = project_kv(
             sz, hidden, gains, tables, weights["key"], weights["value"]
         )
-        blocks = gather_ctx(kv_low.reshape(block_shape))
         query_lin, query_low = project_query(sz, normed, gains, tables, weights["query"])
+        blocks = gather_ctx(kv_low.reshape(block_shape), query_low)
         got = forward_layer(sz, query_low, hidden, gains, places, blocks, weights, save)
         if not save:
             return got[0], None
@@ -792,58 +889,139 @@
         )
         return got[0], saved
 
-    def backward(grad, saved):
-        got, parts = backward_layer(sz, grad, gains, saved, places, saved["blocks"], weights)
-        middle_grad = got[0]
-        query_low_grad, query_part, gain_query = query_back(
-            sz, got[8], saved["query_lin"], gains, tables, weights["query"]
-        )
-        terms = scatter_ctx(parts)
-        input_grad, kv_grad, gain_input, gain_key = input_back(
+    def input_part(terms, middle_grad, query_part, saved):
+        return input_back(
             sz, terms, saved["key_lin"], saved["hidden"], query_part, middle_grad, gains, tables,
             weights["key"], weights["value"],
         )
-        return input_grad, dict(
-            down=got[1], gate=got[2], up=got[3], branch=got[4], post=got[5], pre=got[6],
-            attn=got[7], query_lin=query_low_grad, query=gain_query, kv=kv_grad,
-            input=gain_input, key=gain_key,
-        )
+
+    def queries_back(query_grad, saved):
+        return query_back(
+            sz, query_grad, saved["query_lin"], gains, tables, weights["query"]
+        )
+
+    def scatter_plain(parts):
+        return [lax.psum_scatter(parts[0].astype(f32), "ctx", scatter_dimension=0, tiled=False)]
 
     own_input = inputs.reshape(sz.rows, model_width)
     first_result, _ = forward(own_input, False)
     received = lax.ppermute(first_result, "section", [(0, 1)])
     hidden = jnp.where(section_index == 0, own_input, received)
     result, saved = forward(hidden, True)
+
     own_grad = out_cotangent.reshape(sz.rows, model_width)
-    first_grad, _ = backward(own_grad, saved)
+    got = ffw_back(sz, own_grad, gains, saved, weights)
+    query_grad, parts = attn_back(sz, got[8], saved, places)
+    _, query_part, _ = queries_back(query_grad, saved)
+    terms = run_alone(scatter_stages(parts)) if small_ctx() else scatter_plain(parts)
+    first_grad = input_part(terms, got[0], query_part, saved)[0]
     grad_received = lax.ppermute(first_grad, "section", [(1, 0)])
     grad_in = jnp.where(section_index == 1, own_grad, grad_received)
-    input_grad, grads = backward(grad_in, saved)
-
-    sum_down = sum_ctx(weight_term(saved["act"], grads["down"]))
-    sum_gate = sum_ctx(weight_term(saved["pre_ffw"], grads["gate"]))
-    sum_up = sum_ctx(weight_term(saved["pre_ffw"], grads["up"]))
-    sum_out = sum_ctx(weight_term(saved["attn_low"], grads["branch"]))
-    sum_query = sum_ctx(weight_term(saved["normed"], grads["query_lin"]))
-    names = ("input", "attn", "pre", "post", "query", "key")
-    gain_rows = jnp.concatenate([grads[name].reshape(2, -1) for name in names], axis=1)
+
+    got = ffw_back(sz, grad_in, gains, saved, weights)
+    middle_grad, down_low, gate_low, up_low, branch_low, gain_post, gain_pre, gain_attn = got[:8]
+    down_terms = weight_terms(sz, saved["act"], down_low, 1)
+    gate_terms = weight_terms(sz, saved["pre_ffw"], gate_low, 2)
+    up_terms = weight_terms(sz, saved["pre_ffw"], up_low, 2)
+    out_terms = weight_terms(sz, saved["attn_low"], branch_low, 1)
+    query_grad, parts = attn_back(sz, got[8], saved, places)
+    query_lin_low, query_part, gain_query = queries_back(query_grad, saved)
+    query_terms = weight_terms(sz, saved["normed"], query_lin_low, 1)
+    half_down = down_terms[0][0].shape[0] // 2
+    cut = half_down // 2
+
+    def down_piece(index):
+        rows = [slice(first + index * cut, first + (index + 1) * cut) for first in (0, half_down)]
+        return tuple(
+            jnp.concatenate([term[rows[0]], term[rows[1]]], axis=0) for term in down_terms[0]
+        )
+
+    ends = {}
     kv_width = 2 * head_dim
-    gain_rows = gain_rows.reshape(2, -1, kv_width)
-    gain_count = gain_rows.shape[1]
-    gain_rows = jnp.pad(gain_rows, ((0, 0), (0, 32 - gain_count), (0, 0)))
-    gain_keep = lax.dynamic_index_in_dim(gain_rows, fsdp_index, 0, keepdims=False)
-    gain_send = lax.dynamic_index_in_dim(gain_rows, 1 - fsdp_index, 0, keepdims=False)
-    gain_came = xor_permute(gain_send.astype(bf16), "fsdp", 1)
-    gain_term = (gain_keep + gain_came.astype(f32)).astype(bf16)
-    kv_term = weight_term(saved["normed"], grads["kv"])
-    sum_tail = sum_ctx(jnp.concatenate([kv_term, gain_term], axis=0))
+    gain_count = gains_own.shape[1] // kv_width
     half_model = model_width // 2
-    sum_key = sum_tail[:half_model, :head_dim]
-    sum_value = sum_tail[:half_model, head_dim:]
-    sum_gains = sum_tail[half_model : half_model + gain_count].reshape(-1)
+
+    def tail_terms(terms):
+        input_grad, kv_grad, gain_input, gain_key = input_part(
+            terms, middle_grad, query_part, saved
+        )
+        ends["input_grad"] = input_grad
+        send, keep = weight_terms(sz, saved["normed"], kv_grad, 1)[0]
+        gain_grads = (gain_input, gain_attn, gain_pre, gain_post, gain_query, gain_key)
+        gain_rows = jnp.concatenate([grad.reshape(2, -1) for grad in gain_grads], axis=1)
+        gain_rows = gain_rows.reshape(2, gain_count, kv_width).astype(bf16)
+        gain_rows = jnp.pad(gain_rows, ((0, 0), (0, 16 - gain_count), (0, 0)))
+        zeros = jnp.zeros_like(gain_rows[0])
+        is_lower = (ctx_index & 1) == 0
+        pairs = []
+        for term, owner in ((send, 1 - fsdp_index), (keep, fsdp_index)):
+            here = lax.dynamic_index_in_dim(gain_rows, owner, 0, keepdims=False)
+            half = term.shape[0] // 2
+            pairs.append(
+                jnp.concatenate(
+                    [
+                        term[:half],
+                        jnp.where(is_lower, here, zeros),
+                        term[half:],
+                        jnp.where(is_lower, zeros, here),
+                    ],
+                    axis=0,
+                )
+            )
+        return tuple(pairs)
+
+    if small_ctx():
+
+        def chunk(make):
+            return lambda results: sum_stages(make)
+
+        sets = [
+            [
+                [("down0", chunk(lambda: down_piece(0)))],
+                [("gate0", chunk(lambda: gate_terms[0]))],
+                [("up0", chunk(lambda: up_terms[0])), ("kv", lambda results: scatter_stages(parts))],
+                [("out", chunk(lambda: out_terms[0]))],
+                [],
+                [("tail", lambda results: sum_stages(lambda: tail_terms(results["kv"])))],
+            ],
+            [
+                [("down1", chunk(lambda: down_piece(1)))],
+                [("gate1", chunk(lambda: gate_terms[1]))],
+                [("up1", chunk(lambda: up_terms[1]))],
+                [("query", chunk(lambda: query_terms[0]))],
+            ],
+        ]
+        sums = run_staggered(sets)
+    else:
+        sums = {}
+        for index in range(2):
+            sums["down%d" % index] = sum_plain(*down_piece(index))
+            sums["gate%d" % index] = sum_plain(*gate_terms[index])
+            sums["up%d" % index] = sum_plain(*up_terms[index])
+        sums["out"] = sum_plain(*out_terms[0])
+        sums["query"] = sum_plain(*query_terms[0])
+        sums["tail"] = sum_plain(*tail_terms(scatter_plain(parts)))
+    input_grad = ends["input_grad"]
+    sum_down = jnp.concatenate(
+        [
+            sums["down0"][:cut], sums["down1"][:cut], sums["down0"][cut:], sums["down1"][cut:],
+        ],
+        axis=0,
+    )
+    sum_gate = jnp.concatenate([sums["gate0"], sums["gate1"]], axis=1)
+    sum_up = jnp.concatenate([sums["up0"], sums["up1"]], axis=1)
+    sum_out = sums["out"]
+    sum_query = sums["query"]
+    sum_tail = sums["tail"]
+    quarter = half_model // 2
+    sum_kv = jnp.concatenate(
+        [sum_tail[:quarter], sum_tail[quarter + 16 : quarter + 16 + quarter]], axis=0
+    )
+    sum_key = sum_kv[:, :head_dim]
+    sum_value = sum_kv[:, head_dim:]
+    sum_gains = sum_tail[quarter : quarter + gain_count].reshape(-1)
     gain_sums = {}
-    for name in names:
-        start, width = sz.gain_at[name]
+    for name, (start, width) in sz.gain_at.items():
         gain_sums[name] = sum_gains[start : start + width]
     shape = (micro_count, seq_local, tokens, model_width)
     members = (

time: 475 us -> 452 us (0.952)
  waiting for transfers between devices: 211 us -> 137 us
  starting transfers between devices: 103 us -> 139 us
  Pallas kernels: 88.8 us -> 114 us
  matrix products: 17.8 us -> 0 us
  other arithmetic: 26.1 us -> 33.7 us
    ppermute x18 -> x68, starting transfers between devices: 30.7 us -> 111 us  [the longest x61 94.3 us: run_staggered(): lax.ppermute(value, axis, pairs)]
    ppermute x55 -> x22, waiting for transfers between devices: 124 us -> 49.1 us  [xor_permute(): return lax.ppermute(shard, axis, [(i, i ^ mask) for i in range(count)])]
    ppermute x55 -> x22, starting transfers between devices: 66.8 us -> 23.2 us  [xor_permute(): return lax.ppermute(shard, axis, [(i, i ^ mask) for i in range(count)])]
    pallas_call x12 -> x20, Pallas kernels: 88.8 us -> 114 us  [call_kernel(): pl.pallas_call(body, out_shape=out_shapes, in_specs=[whole] * len(inputs)...]
    dot_general x12 -> x0, matrix products: 17.8 us -> none  [dot_tn(): lax.dot_general(left, right, (((0,), (0,)), ((), ())), preferred_element_...]
    broadcast_in_dim x0 -> x4, other arithmetic: none -> 6.14 us  [on_device(): member[None]]
    convert_element_type x31 -> x47, other arithmetic: 18.6 us -> 16.8 us  [the longest x42 14.2 us: add_low(): return lax.optimization_barrier(total.astype(bf16))]
    ppermute x18 -> x68, waiting for transfers between devices: 72.9 us -> 74.1 us  [the longest x61 67.5 us: run_staggered(): lax.ppermute(value, axis, pairs)]
  transfers between devices with their start and end apart: 75 -> 92, of which waited for: 28 -> 34; matrix products, arithmetic and copies ran while one was open for 11% -> 8% of each run, Pallas kernels for 5% -> 11%
where the time goes in v3:
time: 452 us; the launch traced here: 444 us
  starting transfers between devices  139 us (31%)
  waiting for transfers between devices  137 us (30%)
  Pallas kernels  114 us (25%)
  other arithmetic  33.7 us (7%)
  local copies, waits for them, and re-layouts  17.4 us (4%)
    pallas_call x20, Pallas kernels, call_kernel(): pl.pallas_call(body, out_shape=out_shapes, in_specs=[whole] * len(inputs)...  114 us
    ppermute x61, starting transfers between devices, run_staggered(): lax.ppermute(value, axis, pairs)  94.3 us
    ppermute x61, waiting for transfers between devices, run_staggered(): lax.ppermute(value, axis, pairs)  67.5 us
    ppermute x22, waiting for transfers between devices, xor_permute(): return lax.ppermute(shard, axis, [(i, i ^ mask) for i in range(count)])  49.1 us
    ppermute x22, starting transfers between devices, xor_permute(): return lax.ppermute(shard, axis, [(i, i ^ mask) for i in range(count)])  23.2 us
    ppermute x7, starting transfers between devices, run_alone(): lax.ppermute(value, axis, pairs)  16.8 us
    convert_element_type x42, other arithmetic, add_low(): return lax.optimization_barrier(total.astype(bf16))  14.2 us
  transfers between devices with their start and end apart: 92, of which 34 were waited for; matrix products, arithmetic and copies ran while one was open for 8% of the time, Pallas kernels for 11%

profile of v3, /device:TPU:0, one launch (start us, length us, event | category | flops | bytes accessed | tf_op | source)
XLA Modules:
  0.0 444.0 jit_solution(321373619287612878)
XLA Ops:
  18.7 7.0 %collective-permute-done.5.refs_8_ = bf16[2,128,512]{2,1,0:T(8,128)(2,1)} collective-permute-done((bf16[2,128,512]{2,1,0:T(8,128)(2,1)}, bf16[2,128,512]{2,1,0:T(8,128)(2,1)}, u32[]{:S(2)}, u32[]{:S(2)}) %collective-permute-start.5) | collective-permute-done | bytes 262176 | tf_op jit(solution)/shard_map/ppermute | solution.py:678
  31.2 4.1 shard_map.272
  35.3 4.4 collective-permute-done.9.refs_12_
  42.4 6.8 %collective-permute-done.6.refs_9_ = bf16[2,128,512]{2,1,0:T(8,128)(2,1)} collective-permute-done((bf16[2,128,512]{2,1,0:T(8,128)(2,1)}, bf16[2,128,512]{2,1,0:T(8,128)(2,1)}, u32[]{:S(2)}, u32[]{:S(2)}) %collective-permute-start.6) | collective-permute-done | bytes 262176 | tf_op jit(solution)/shard_map/ppermute | solution.py:678
  54.8 4.3 collective-permute-done.10.refs_13_
  60.2 9.6 %shard_map.273 = bf16[256,640]{1,0:T(8,128)(2,1)} custom-call(bf16[2,512,256]{2,1,0:T(8,128)(2,1)} %get-tuple-element.153.refs_0_, bf16[256,640]{1,0:T(8,128)(2,1)} %bitcast.99, bf16[1,1536]{1,0:T(2,128)(2,1)} %copy-done.15, bf16[1,1536]{1,0:T(2,128)(2,1)} %copy-done.16, s32[1,1024]{1,0:T(1,128)} %add.243.refs_4_, s32[512,1]{1,0:T(8,128)} %copy.33.refs_5_, ...), custom_call_target="tpu_custom_call" | custom-call | tf_op jit(solution)/shard_map/pallas_call | solution.py:69
  73.4 6.0 %collective-permute-done.15 = bf16[256,640]{1,0:T(8,128)(2,1)S(1)} collective-permute-done((bf16[256,640]{1,0:T(8,128)(2,1)}, bf16[256,640]{1,0:T(8,128)(2,1)S(1)}, u32[]{:S(2)}, u32[]{:S(2)}) %collective-permute-start.15) | collective-permute-done | bytes 327712 | tf_op jit(solution)/shard_map/ppermute | solution.py:908
  83.8 4.3 collective-permute-start.17
  91.1 4.0 shard_map.275
  97.1 11.5 %collective-permute-done.19.refs_10_.refs_9_ = bf16[2,128,512]{2,1,0:T(8,128)(2,1)S(1)} collective-permute-done((bf16[2,128,512]{2,1,0:T(8,128)(2,1)}, bf16[2,128,512]{2,1,0:T(8,128)(2,1)S(1)}, u32[]{:S(2)}, u32[]{:S(2)}) %collective-permute-start.19) | collective-permute-done | bytes 262176 | tf_op jit(solution)/shard_map/ppermute | solution.py:678
  118.6 11.3 %shard_map.276 = (bf16[256,640]{1,0:T(8,128)(2,1)}, f32[2,512,1]{2,1,0:T(8,128)}, bf16[256,1024]{1,0:T(8,128)(2,1)}, f32[256,640]{1,0:T(8,128)}, f32[256,640]{1,...) custom-call(bf16[2,512,256]{2,1,0:T(8,128)(2,1)} %get-tuple-element., ...), custom_call_target="tpu_custom_call" | custom-call | tf_op jit(solution)/shard_map/pallas_call | solution.py:69
  131.8 12.5 %shard_map.277 = (f32[256,640]{1,0:T(8,128)}, bf16[256,640]{1,0:T(8,128)(2,1)}, bf16[256,2048]{1,0:T(8,128)(2,1)}, bf16[256,2048]{1,0:T(8,128)(2,1)}, bf16[256,6...) custom-call(bf16[256,640]{1,0:T(8,128)(2,1)} %bitcast.117, ...), custom_call_target="tpu_custom_call" | custom-call | tf_op jit(solution)/shard_map/pallas_call | solution.py:69
  144.3 8.4 %shard_map.278 = (f32[2,512,256]{2,1,0:T(8,128)}, bf16[2,128,512]{2,1,0:T(8,128)(2,1)}, bf16[2,128,512]{2,1,0:T(8,128)(2,1)}, bf16[2,128,512]{2,1,0:T(8,128)(2,1...) custom-call(bf16[256,1024]{1,0:T(8,128)(2,1)} %get-tuple-element.171, ...), custom_call_target="tpu_custom_call" | custom-call | tf_op jit(solution)/shard_map/pallas_call | solution.py:69
  164.2 7.3 %collective-permute-start.26 = (bf16[2,128,512]{2,1,0:T(8,128)(2,1)S(1)}, bf16[2,128,512]{2,1,0:T(8,128)(2,1)S(1)}, u32[]{:S(2)}, u32[]{:S(2)}) collective-permute-start(bf16[2,128,512]{2,1,0:T(8,128)(2,1)S(1)} %add_convert_fusion.36), channel_id=1, source_target_pairs={{0,8},{2,10},{4,12},{6,14},{8,0},{10,2},{12,4},{14,6},{1,9},{3,11}... | collective-permute-start | bytes 786440 | tf_op jit(solution)/shard_map/ppermute | solution.py:802
  171.5 4.0 collective-permute-start.28
  175.5 4.3 shard_map.279
  183.4 4.4 shard_map.280
  189.3 7.7 %collective-permute-done.30 = bf16[256,640]{1,0:T(8,128)(2,1)S(1)} collective-permute-done((bf16[256,640]{1,0:T(8,128)(2,1)}, bf16[256,640]{1,0:T(8,128)(2,1)S(1)}, u32[]{:S(2)}, u32[]{:S(2)}) %collective-permute-start.30) | collective-permute-done | bytes 327712 | tf_op jit(solution)/shard_map/ppermute | solution.py:918
  197.8 12.2 %shard_map.281 = (f32[256,640]{1,0:T(8,128)}, bf16[256,640]{1,0:T(8,128)(2,1)}, bf16[256,2048]{1,0:T(8,128)(2,1)}, bf16[256,2048]{1,0:T(8,128)(2,1)}, bf16[256,6...) custom-call(bf16[256,640]{1,0:T(8,128)(2,1)} %broadcast_select_fusion, ...), custom_call_target="tpu_custom_call" | custom-call | tf_op jit(solution)/shard_map/pallas_call | solution.py:69
  224.8 8.6 %shard_map.285 = (f32[2,512,256]{2,1,0:T(8,128)}, bf16[2,128,512]{2,1,0:T(8,128)(2,1)}, bf16[2,128,512]{2,1,0:T(8,128)(2,1)}, bf16[2,128,512]{2,1,0:T(8,128)(2,1...) custom-call(bf16[256,1024]{1,0:T(8,128)(2,1)} %get-tuple-element.201, ...), custom_call_target="tpu_custom_call" | custom-call | tf_op jit(solution)/shard_map/pallas_call | solution.py:69
  234.1 4.3 shard_map.287
  249.4 6.6 %collective-permute-done.32 = bf16[256,640]{1,0:T(8,128)(2,1)S(1)} collective-permute-done((bf16[256,640]{1,0:T(8,128)(2,1)S(1)}, bf16[256,640]{1,0:T(8,128)(2,1)S(1)}, u32[]{:S(2)}, u32[]{:S(2)}) %collective-permute-start.32) | collective-permute-done | bytes 327712 | tf_op jit(solution)/shard_map/ppermute | solution.py:792
  259.4 9.3 %collective-permute-done.42 = bf16[256,640]{1,0:T(8,128)(2,1)S(1)} collective-permute-done((bf16[256,640]{1,0:T(8,128)(2,1)S(1)}, bf16[256,640]{1,0:T(8,128)(2,1)S(1)}, u32[]{:S(2)}, u32[]{:S(2)}) %collective-permute-start.42) | collective-permute-done | bytes 327712 | tf_op jit(solution)/shard_map/ppermute | solution.py:792
  274.3 5.6 %collective-permute-done.41 = bf16[2,128,512]{2,1,0:T(8,128)(2,1)S(1)} collective-permute-done((bf16[2,128,512]{2,1,0:T(8,128)(2,1)S(1)}, bf16[2,128,512]{2,1,0:T(8,128)(2,1)S(1)}, u32[]{:S(2)}, u32[]{:S(2)}) %collective-permute-start.41) | collective-permute-done | bytes 262176 | tf_op jit(solution)/shard_map/ppermute | solution.py:792
  301.9 14.3 %collective-permute-done.48 = bf16[2,128,512]{2,1,0:T(8,128)(2,1)S(1)} collective-permute-done((bf16[2,128,512]{2,1,0:T(8,128)(2,1)S(1)}, bf16[2,128,512]{2,1,0:T(8,128)(2,1)S(1)}, u32[]{:S(2)}, u32[]{:S(2)}) %collective-permute-start.48) | collective-permute-done | bytes 262176 | tf_op jit(solution)/shard_map/ppermute | solution.py:792
  316.9 4.0 collective-permute-start.55
  327.3 7.0 %collective-permute-start.64 = (bf16[160,1024]{1,0:T(8,128)(2,1)S(1)}, bf16[160,1024]{1,0:T(8,128)(2,1)}, u32[]{:S(2)}, u32[]{:S(2)}) collective-permute-start(bf16[160,1024]{1,0:T(8,128)(2,1)S(1)} %add_convert_fusion.17), channel_id=1, source_target_pairs={{0,4},{2,6},{12,8},{14,10},{1,5},{3,7},{13,9},{15,11},{16,20},{18,... | collective-permute-start | bytes 983048 | tf_op jit(solution)/shard_map/ppermute | solution.py:792
  337.5 4.4 shard_map.289
  347.8 8.1 %collective-permute-start.60 = (bf16[160,1024]{1,0:T(8,128)(2,1)S(1)}, bf16[160,1024]{1,0:T(8,128)(2,1)S(1)}, u32[]{:S(2)}, u32[]{:S(2)}) collective-permute-start(bf16[160,1024]{1,0:T(8,128)(2,1)S(1)} %add_convert_fusion.13), channel_id=1, source_target_pairs={{0,4},{2,6},{12,8},{14,10},{1,5},{3,7},{13,9},{15,11},{16,20},{18,... | collective-permute-start | bytes 983048 | tf_op jit(solution)/shard_map/ppermute | solution.py:792
  364.5 6.2 %collective-permute-start.73 = (bf16[256,640]{1,0:T(8,128)(2,1)S(1)}, bf16[256,640]{1,0:T(8,128)(2,1)S(1)}, u32[]{:S(2)}, u32[]{:S(2)}) collective-permute-start(bf16[256,640]{1,0:T(8,128)(2,1)S(1)} %add_convert_fusion.9), channel_id=1, source_target_pairs={{0,4},{2,6},{12,8},{14,10},{1,5},{3,7},{13,9},{15,11},{16,20},{18,... | collective-permute-start | bytes 983048 | tf_op jit(solution)/shard_map/ppermute | solution.py:792
  375.7 7.4 %collective-permute-start.69 = (bf16[160,1024]{1,0:T(8,128)(2,1)S(1)}, bf16[160,1024]{1,0:T(8,128)(2,1)S(1)}, u32[]{:S(2)}, u32[]{:S(2)}) collective-permute-start(bf16[160,1024]{1,0:T(8,128)(2,1)S(1)} %add_convert_fusion.8), channel_id=1, source_target_pairs={{0,4},{2,6},{12,8},{14,10},{1,5},{3,7},{13,9},{15,11},{16,20},{18,... | collective-permute-start | bytes 983048 | tf_op jit(solution)/shard_map/ppermute | solution.py:792
  391.8 6.2 %collective-permute-done.81 = bf16[176,512]{1,0:T(8,128)(2,1)S(1)} collective-permute-done((bf16[176,512]{1,0:T(8,128)(2,1)S(1)}, bf16[176,512]{1,0:T(8,128)(2,1)S(1)}, u32[]{:S(2)}, u32[]{:S(2)}) %collective-permute-start.81) | collective-permute-done | bytes 180256 | tf_op jit(solution)/shard_map/ppermute | solution.py:792
  (406 shorter events, 214.8 us)
Async XLA Ops:
  2.6 26.1 %collective-permute-start.3 = (bf16[320,1024]{1,0:T(8,128)(2,1)}, bf16[320,1024]{1,0:T(8,128)(2,1)}, u32[]{:S(2)}, u32[]{:S(2)}) collective-permute-start(bf16[320,1024]{1,0:T(8,128)(2,1)} %bitcast.93), channel_id=1, source_target_pairs={{0,1},{1,0},{2,3},{3,2},{4,5},{5,4},{6,7},{7,6},{8,9},{9,8},{10,11... | collective-permute-start | bytes 1966088 | tf_op jit(solution)/shard_map/ppermute | solution.py:678
  16.1 43.0 %collective-permute-start.12 = (bf16[320,2048]{1,0:T(8,128)(2,1)S(1)}, bf16[320,2048]{1,0:T(8,128)(2,1)S(1)}, u32[]{:S(2)}, u32[]{:S(2)}) collective-permute-start(bf16[320,2048]{1,0:T(8,128)(2,1)S(1)} %bitcast.77), channel_id=1, source_target_pairs={{0,1},{1,0},{2,3},{3,2},{4,5},{5,4},{6,7},{7,6},{8,9},{9,8},{10,11... | collective-permute-start | bytes 3932168 | tf_op jit(solution)/shard_map/ppermute | solution.py:678
  18.7 40.4 %collective-permute-start.13 = (bf16[320,2048]{1,0:T(8,128)(2,1)}, bf16[320,2048]{1,0:T(8,128)(2,1)}, u32[]{:S(2)}, u32[]{:S(2)}) collective-permute-start(bf16[320,2048]{1,0:T(8,128)(2,1)} %bitcast.78), channel_id=1, source_target_pairs={{0,1},{1,0},{2,3},{3,2},{4,5},{5,4},{6,7},{7,6},{8,9},{9,8},{10,11... | collective-permute-start | bytes 3932168 | tf_op jit(solution)/shard_map/ppermute | solution.py:678
  25.8 33.4 %collective-permute-start.14 = (bf16[1024,640]{1,0:T(8,128)(2,1)}, bf16[1024,640]{1,0:T(8,128)(2,1)}, u32[]{:S(2)}, u32[]{:S(2)}) collective-permute-start(bf16[1024,640]{1,0:T(8,128)(2,1)} %bitcast.83), channel_id=1, source_target_pairs={{0,1},{1,0},{2,3},{3,2},{4,5},{5,4},{6,7},{7,6},{8,9},{9,8},{10,11... | collective-permute-start | bytes 3932168 | tf_op jit(solution)/shard_map/ppermute | solution.py:678
  88.1 20.5 %collective-permute-start.19 = (bf16[2,128,512]{2,1,0:T(8,128)(2,1)}, bf16[2,128,512]{2,1,0:T(8,128)(2,1)S(1)}, u32[]{:S(2)}, u32[]{:S(2)}) collective-permute-start(bf16[2,128,512]{2,1,0:T(8,128)(2,1)} %bitcast.111), channel_id=1, source_target_pairs={{0,8},{2,10},{4,12},{6,14},{8,0},{10,2},{12,4},{14,6},{1,9},{3,11}... | collective-permute-start | bytes 786440 | tf_op jit(solution)/shard_map/ppermute | solution.py:678
  88.1 21.0 %collective-permute-start.21 = (bf16[2,128,512]{2,1,0:T(8,128)(2,1)}, bf16[2,128,512]{2,1,0:T(8,128)(2,1)S(1)}, u32[]{:S(2)}, u32[]{:S(2)}) collective-permute-start(bf16[2,128,512]{2,1,0:T(8,128)(2,1)} %bitcast.112), channel_id=1, source_target_pairs={{0,12},{2,14},{4,8},{6,10},{8,4},{10,6},{12,0},{14,2},{1,13},{3,15... | collective-permute-start | bytes 786440 | tf_op jit(solution)/shard_map/ppermute | solution.py:678
  90.6 21.4 %collective-permute-start.16 = (bf16[2,128,512]{2,1,0:T(8,128)(2,1)}, bf16[2,128,512]{2,1,0:T(8,128)(2,1)S(1)}, u32[]{:S(2)}, u32[]{:S(2)}) collective-permute-start(bf16[2,128,512]{2,1,0:T(8,128)(2,1)} %bitcast.113), channel_id=1, source_target_pairs={{0,2},{2,0},{4,6},{6,4},{8,10},{10,8},{12,14},{14,12},{1,3},{3,1},... | collective-permute-start | bytes 786440 | tf_op jit(solution)/shard_map/ppermute | solution.py:678
  154.8 16.6 %collective-permute-start.27 = (bf16[2,128,512]{2,1,0:T(8,128)(2,1)}, bf16[2,128,512]{2,1,0:T(8,128)(2,1)S(1)}, u32[]{:S(2)}, u32[]{:S(2)}) collective-permute-start(bf16[2,128,512]{2,1,0:T(8,128)(2,1)} %get-tuple-element.178), channel_id=1, source_target_pairs={{0,2},{2,0},{4,6},{6,4},{8,10},{10,8},{12,14},{14,12},{1,3},{3,1},... | collective-permute-start | bytes 786440 | tf_op jit(solution)/shard_map/ppermute | solution.py:802
  155.4 24.5 %collective-permute-start.29 = (bf16[2,128,512]{2,1,0:T(8,128)(2,1)}, bf16[2,128,512]{2,1,0:T(8,128)(2,1)S(1)}, u32[]{:S(2)}, u32[]{:S(2)}) collective-permute-start(bf16[2,128,512]{2,1,0:T(8,128)(2,1)} %get-tuple-element.180), channel_id=1, source_target_pairs={{0,2},{2,0},{4,6},{6,4},{8,10},{10,8},{12,14},{14,12},{1,3},{3,1},... | collective-permute-start | bytes 786440 | tf_op jit(solution)/shard_map/ppermute | solution.py:802
  161.4 18.5 %collective-permute-start.24 = (bf16[2,128,512]{2,1,0:T(8,128)(2,1)S(1)}, bf16[2,128,512]{2,1,0:T(8,128)(2,1)S(1)}, u32[]{:S(2)}, u32[]{:S(2)}) collective-permute-start(bf16[2,128,512]{2,1,0:T(8,128)(2,1)S(1)} %add_convert_fusion.37), channel_id=1, source_target_pairs={{0,12},{2,14},{4,8},{6,10},{8,4},{10,6},{12,0},{14,2},{1,13},{3,15... | collective-permute-start | bytes 786440 | tf_op jit(solution)/shard_map/ppermute | solution.py:802
  164.2 18.1 %collective-permute-start.26 = (bf16[2,128,512]{2,1,0:T(8,128)(2,1)S(1)}, bf16[2,128,512]{2,1,0:T(8,128)(2,1)S(1)}, u32[]{:S(2)}, u32[]{:S(2)}) collective-permute-start(bf16[2,128,512]{2,1,0:T(8,128)(2,1)S(1)} %add_convert_fusion.36), channel_id=1, source_target_pairs={{0,8},{2,10},{4,12},{6,14},{8,0},{10,2},{12,4},{14,6},{1,9},{3,11}... | collective-permute-start | bytes 786440 | tf_op jit(solution)/shard_map/ppermute | solution.py:802
  215.9 28.4 %collective-permute-start.31 = (bf16[512,640]{1,0:T(8,128)(2,1)}, bf16[512,640]{1,0:T(8,128)(2,1)}, u32[]{:S(2)}, u32[]{:S(2)}) collective-permute-start(bf16[512,640]{1,0:T(8,128)(2,1)} %pad_maximum_fusion), channel_id=1, source_target_pairs={{0,1},{1,0},{2,3},{3,2},{4,5},{5,4},{6,7},{7,6},{8,9},{9,8},{10,11... | collective-permute-start | bytes 1966088 | tf_op jit(solution)/shard_map/ppermute | solution.py:792
  216.8 30.8 %collective-permute-start.34 = (bf16[512,640]{1,0:T(8,128)(2,1)}, bf16[512,640]{1,0:T(8,128)(2,1)}, u32[]{:S(2)}, u32[]{:S(2)}) collective-permute-start(bf16[512,640]{1,0:T(8,128)(2,1)} %pad_maximum_fusion.1), channel_id=1, source_target_pairs={{0,1},{1,0},{2,3},{3,2},{4,5},{5,4},{6,7},{7,6},{8,9},{9,8},{10,11... | collective-permute-start | bytes 1966088 | tf_op jit(solution)/shard_map/ppermute | solution.py:792
  220.8 28.0 %collective-permute-start.33 = (bf16[320,1024]{1,0:T(8,128)(2,1)}, bf16[320,1024]{1,0:T(8,128)(2,1)S(1)}, u32[]{:S(2)}, u32[]{:S(2)}) collective-permute-start(bf16[320,1024]{1,0:T(8,128)(2,1)} %get-tuple-element.193), channel_id=1, source_target_pairs={{0,1},{1,0},{2,3},{3,2},{4,5},{5,4},{6,7},{7,6},{8,9},{9,8},{10,11... | collective-permute-start | bytes 1966088 | tf_op jit(solution)/shard_map/ppermute | solution.py:792
  224.3 55.6 %collective-permute-start.37 = (bf16[320,1024]{1,0:T(8,128)(2,1)}, bf16[320,1024]{1,0:T(8,128)(2,1)S(1)}, u32[]{:S(2)}, u32[]{:S(2)}) collective-permute-start(bf16[320,1024]{1,0:T(8,128)(2,1)} %get-tuple-element.200), channel_id=1, source_target_pairs={{0,1},{1,0},{2,3},{3,2},{4,5},{5,4},{6,7},{7,6},{8,9},{9,8},{10,11... | collective-permute-start | bytes 1966088 | tf_op jit(solution)/shard_map/ppermute | solution.py:792
  233.4 36.7 %collective-permute-start.38 = (bf16[2,128,512]{2,1,0:T(8,128)(2,1)}, bf16[2,128,512]{2,1,0:T(8,128)(2,1)S(1)}, u32[]{:S(2)}, u32[]{:S(2)}) collective-permute-start(bf16[2,128,512]{2,1,0:T(8,128)(2,1)} %get-tuple-element.202), channel_id=1, source_target_pairs={{0,2},{2,0},{4,6},{6,4},{8,10},{10,8},{12,14},{14,12},{1,3},{3,1},... | collective-permute-start | bytes 786440 | tf_op jit(solution)/shard_map/ppermute | solution.py:792
  248.8 22.9 %collective-permute-start.39 = (bf16[2,128,512]{2,1,0:T(8,128)(2,1)S(1)}, bf16[2,128,512]{2,1,0:T(8,128)(2,1)S(1)}, u32[]{:S(2)}, u32[]{:S(2)}) collective-permute-start(bf16[2,128,512]{2,1,0:T(8,128)(2,1)S(1)} %copy-done.56), channel_id=1, source_target_pairs={{0,2},{2,0},{4,6},{6,4},{8,10},{10,8},{12,14},{14,12},{1,3},{3,1},... | collective-permute-start | bytes 786440 | tf_op jit(solution)/shard_map/ppermute | solution.py:792
  274.3 21.5 %collective-permute-start.50 = (bf16[512,640]{1,0:T(8,128)(2,1)S(1)}, bf16[512,640]{1,0:T(8,128)(2,1)S(1)}, u32[]{:S(2)}, u32[]{:S(2)}) collective-permute-start(bf16[512,640]{1,0:T(8,128)(2,1)S(1)} %copy-done.52), channel_id=1, source_target_pairs={{0,1},{1,0},{2,3},{3,2},{4,5},{5,4},{6,7},{7,6},{8,9},{9,8},{10,11... | collective-permute-start | bytes 1966088 | tf_op jit(solution)/shard_map/ppermute | solution.py:792
  290.1 26.8 %collective-permute-start.44 = (bf16[256,640]{1,0:T(8,128)(2,1)S(1)}, bf16[256,640]{1,0:T(8,128)(2,1)S(1)}, u32[]{:S(2)}, u32[]{:S(2)}) collective-permute-start(bf16[256,640]{1,0:T(8,128)(2,1)S(1)} %add_convert_fusion.25), channel_id=1, source_target_pairs={{4,8},{6,10},{8,4},{10,6},{5,9},{7,11},{9,5},{11,7},{20,24},{22,26... | collective-permute-start | bytes 983048 | tf_op jit(solution)/shard_map/ppermute | solution.py:792
  291.0 30.0 %collective-permute-start.45 = (bf16[160,1024]{1,0:T(8,128)(2,1)S(1)}, bf16[160,1024]{1,0:T(8,128)(2,1)S(1)}, u32[]{:S(2)}, u32[]{:S(2)}) collective-permute-start(bf16[160,1024]{1,0:T(8,128)(2,1)S(1)} %add_convert_fusion.24), channel_id=1, source_target_pairs={{0,4},{2,6},{12,8},{14,10},{1,5},{3,7},{13,9},{15,11},{16,20},{18,... | collective-permute-start | bytes 983048 | tf_op jit(solution)/shard_map/ppermute | solution.py:792
  294.0 28.5 %collective-permute-start.46 = (bf16[160,1024]{1,0:T(8,128)(2,1)S(1)}, bf16[160,1024]{1,0:T(8,128)(2,1)S(1)}, u32[]{:S(2)}, u32[]{:S(2)}) collective-permute-start(bf16[160,1024]{1,0:T(8,128)(2,1)S(1)} %add_convert_fusion.23), channel_id=1, source_target_pairs={{0,2},{2,0},{4,6},{6,4},{8,10},{10,8},{12,14},{14,12},{1,3},{3,1},... | collective-permute-start | bytes 983048 | tf_op jit(solution)/shard_map/ppermute | solution.py:792
  295.8 20.4 %collective-permute-start.48 = (bf16[2,128,512]{2,1,0:T(8,128)(2,1)S(1)}, bf16[2,128,512]{2,1,0:T(8,128)(2,1)S(1)}, u32[]{:S(2)}, u32[]{:S(2)}) collective-permute-start(bf16[2,128,512]{2,1,0:T(8,128)(2,1)S(1)} %add_convert_fusion.33), channel_id=1, source_target_pairs={{0,8},{2,10},{4,12},{6,14},{8,0},{10,2},{12,4},{14,6},{1,9},{3,11}... | collective-permute-start | bytes 786440 | tf_op jit(solution)/shard_map/ppermute | solution.py:792
  298.4 17.8 %collective-permute-start.49 = (bf16[2,128,512]{2,1,0:T(8,128)(2,1)S(1)}, bf16[2,128,512]{2,1,0:T(8,128)(2,1)S(1)}, u32[]{:S(2)}, u32[]{:S(2)}) collective-permute-start(bf16[2,128,512]{2,1,0:T(8,128)(2,1)S(1)} %add_convert_fusion.32), channel_id=1, source_target_pairs={{0,4},{2,6},{4,0},{6,2},{8,12},{10,14},{12,8},{14,10},{1,5},{3,7},... | collective-permute-start | bytes 786440 | tf_op jit(solution)/shard_map/ppermute | solution.py:792
  316.9 17.4 %collective-permute-start.55 = (bf16[160,1024]{1,0:T(8,128)(2,1)S(1)}, bf16[160,1024]{1,0:T(8,128)(2,1)S(1)}, u32[]{:S(2)}, u32[]{:S(2)}) collective-permute-start(bf16[160,1024]{1,0:T(8,128)(2,1)S(1)} %add_convert_fusion.21), channel_id=1, source_target_pairs={{0,4},{2,6},{12,8},{14,10},{1,5},{3,7},{13,9},{15,11},{16,20},{18,... | collective-permute-start | bytes 983048 | tf_op jit(solution)/shard_map/ppermute | solution.py:792
  324.6 22.4 %collective-permute-start.62 = (bf16[256,640]{1,0:T(8,128)(2,1)S(1)}, bf16[256,640]{1,0:T(8,128)(2,1)}, u32[]{:S(2)}, u32[]{:S(2)}) collective-permute-start(bf16[256,640]{1,0:T(8,128)(2,1)S(1)} %add_convert_fusion.19), channel_id=1, source_target_pairs={{4,0},{6,2},{8,12},{10,14},{5,1},{7,3},{9,13},{11,15},{20,16},{22,... | collective-permute-start | bytes 983048 | tf_op jit(solution)/shard_map/ppermute | solution.py:792
  325.9 21.9 %collective-permute-start.63 = (bf16[160,1024]{1,0:T(8,128)(2,1)S(1)}, bf16[160,1024]{1,0:T(8,128)(2,1)}, u32[]{:S(2)}, u32[]{:S(2)}) collective-permute-start(bf16[160,1024]{1,0:T(8,128)(2,1)S(1)} %add_convert_fusion.18), channel_id=1, source_target_pairs={{4,8},{6,10},{8,4},{10,6},{5,9},{7,11},{9,5},{11,7},{20,24},{22,26... | collective-permute-start | bytes 983048 | tf_op jit(solution)/shard_map/ppermute | solution.py:792
  327.3 28.6 %collective-permute-start.64 = (bf16[160,1024]{1,0:T(8,128)(2,1)S(1)}, bf16[160,1024]{1,0:T(8,128)(2,1)}, u32[]{:S(2)}, u32[]{:S(2)}) collective-permute-start(bf16[160,1024]{1,0:T(8,128)(2,1)S(1)} %add_convert_fusion.17), channel_id=1, source_target_pairs={{0,4},{2,6},{12,8},{14,10},{1,5},{3,7},{13,9},{15,11},{16,20},{18,... | collective-permute-start | bytes 983048 | tf_op jit(solution)/shard_map/ppermute | solution.py:792
  334.3 23.2 %collective-permute-start.65 = (bf16[256,640]{1,0:T(8,128)(2,1)}, bf16[256,640]{1,0:T(8,128)(2,1)}, u32[]{:S(2)}, u32[]{:S(2)}) collective-permute-start(bf16[256,640]{1,0:T(8,128)(2,1)} %add_convert_fusion.16), channel_id=1, source_target_pairs={{0,2},{2,0},{4,6},{6,4},{8,10},{10,8},{12,14},{14,12},{1,3},{3,1},... | collective-permute-start | bytes 983048 | tf_op jit(solution)/shard_map/ppermute | solution.py:792
  334.9 27.0 %collective-permute-start.58 = (bf16[256,640]{1,0:T(8,128)(2,1)S(1)}, bf16[256,640]{1,0:T(8,128)(2,1)}, u32[]{:S(2)}, u32[]{:S(2)}) collective-permute-start(bf16[256,640]{1,0:T(8,128)(2,1)S(1)} %add_convert_fusion.15), channel_id=1, source_target_pairs={{4,0},{6,2},{8,12},{10,14},{5,1},{7,3},{9,13},{11,15},{20,16},{22,... | collective-permute-start | bytes 983048 | tf_op jit(solution)/shard_map/ppermute | solution.py:792
  364.5 18.7 %collective-permute-start.73 = (bf16[256,640]{1,0:T(8,128)(2,1)S(1)}, bf16[256,640]{1,0:T(8,128)(2,1)S(1)}, u32[]{:S(2)}, u32[]{:S(2)}) collective-permute-start(bf16[256,640]{1,0:T(8,128)(2,1)S(1)} %add_convert_fusion.9), channel_id=1, source_target_pairs={{0,4},{2,6},{12,8},{14,10},{1,5},{3,7},{13,9},{15,11},{16,20},{18,... | collective-permute-start | bytes 983048 | tf_op jit(solution)/shard_map/ppermute | solution.py:792
  384.0 16.0 %collective-permute-start.79 = (bf16[160,1024]{1,0:T(8,128)(2,1)S(1)}, bf16[160,1024]{1,0:T(8,128)(2,1)S(1)}, u32[]{:S(2)}, u32[]{:S(2)}) collective-permute-start(bf16[160,1024]{1,0:T(8,128)(2,1)S(1)} %add_convert_fusion.5), channel_id=1, source_target_pairs={{4,0},{6,2},{8,12},{10,14},{5,1},{7,3},{9,13},{11,15},{20,16},{22,... | collective-permute-start | bytes 983048 | tf_op jit(solution)/shard_map/ppermute | solution.py:792
  388.8 16.2 %collective-permute-start.75 = (bf16[160,1024]{1,0:T(8,128)(2,1)S(1)}, bf16[160,1024]{1,0:T(8,128)(2,1)S(1)}, u32[]{:S(2)}, u32[]{:S(2)}) collective-permute-start(bf16[160,1024]{1,0:T(8,128)(2,1)S(1)} %broadcast_select_fusion.10), channel_id=1, source_target_pairs={{0,2},{2,0},{4,6},{6,4},{8,10},{10,8},{12,14},{14,12},{1,3},{3,1},... | collective-permute-start | bytes 983048 | tf_op jit(solution)/shard_map/ppermute | solution.py:792
  (117 other events, 1252.6 us)

commit v4 on v3

--- a/solution.py
+++ b/solution.py
@@ -63,7 +63,10 @@
     return (jnp.cos(angles), jnp.sin(angles))
 
 
-def call_kernel(body, out_shapes, inputs, far_inputs, scratch):
+def call_kernel(body, out_shapes, inputs, far_inputs, scratch, mega_macs=0):
+    moved = 0
+    for array in [*inputs, *far_inputs, *out_shapes]:
+        moved += array.size * jnp.dtype(array.dtype).itemsize
     whole = pl.BlockSpec(memory_space=pltpu.VMEM)
     far = pl.BlockSpec(memory_space=pl.ANY)
     return pl.pallas_call(
@@ -73,6 +76,9 @@
         out_specs=jax.tree.map(lambda _: whole, out_shapes),
         scratch_shapes=scratch,
         compiler_params=pltpu.CompilerParams(vmem_limit_bytes=vmem_bytes),
+        cost_estimate=pl.CostEstimate(
+            flops=2 * mega_macs * 10**6, bytes_accessed=moved * 3, transcendentals=0
+        ),
     )(*inputs, *far_inputs)
 
 
@@ -423,12 +429,11 @@
     attn_grad[...] = dot_nt(branch_low, w_out[...]).astype(bf16)
 
 
-def attn_back_kernel(sz, block_count, *refs):
+def attn_back_kernel(sz, block_count, paired, *refs):
     attn_grad, query_low, log_row, key_col, query_row = refs[:5]
     refs = refs[5:]
     blocks, refs = refs[:block_count], refs[block_count:]
-    query_grad, refs = refs[0], refs[1:]
-    parts, refs = refs[:block_count], refs[block_count:]
+    query_grad, parts, refs = refs[0], refs[1:-4], refs[-4:]
     kv, key_sum, value_sum, sems = refs
     if block_count > 1:
         wait_all(start_blocks(sz, blocks, kv, sems, 0))
@@ -479,8 +484,12 @@
                 )
             for index in range(block_count):
                 at = slice(index * sz.tokens, (index + 1) * sz.tokens)
-                parts[index][group, :, : sz.head_dim] = key_sum[at, :].astype(bf16)
-                parts[index][group, :, sz.head_dim :] = value_sum[at, :].astype(bf16)
+                if paired:
+                    target = parts[index // 2].at[index % 2, group]
+                else:
+                    target = parts[index].at[group]
+                target[:, : sz.head_dim] = key_sum[at, :].astype(bf16)
+                target[:, sz.head_dim :] = value_sum[at, :].astype(bf16)
             continue
         load_group(sz, blocks[0], group, kv, sems, 0)
         deltas = []
@@ -541,10 +550,13 @@
     return call_kernel(functools.partial(ffw_back_kernel, sz), outs, inputs, far, scratch)
 
 
-def attn_back(sz, attn_grad, saved, places):
+def attn_back(sz, attn_grad, saved, places, paired):
     blocks = saved["blocks"]
     outs = [struct((sz.groups, sz.head_rows, sz.head_dim), f32)]
-    outs += [struct(block.shape, bf16) for block in blocks]
+    if paired and len(blocks) > 1:
+        outs += [struct((2,) + block.shape, bf16) for block in blocks[::2]]
+    else:
+        outs += [struct(block.shape, bf16) for block in blocks]
     scratch = [
         pltpu.VMEM((sz.groups if len(blocks) > 1 else 1, sz.keys, 2 * sz.head_dim), bf16),
         pltpu.VMEM((sz.span, sz.head_dim), f32),
@@ -555,12 +567,17 @@
         attn_grad, saved["query_low"], saved["log_row"], places["key_col"], places["query_row"]
     ]
     got = call_kernel(
-        functools.partial(attn_back_kernel, sz, len(blocks)), outs, inputs, blocks, scratch
+        functools.partial(attn_back_kernel, sz, len(blocks), paired), outs, inputs, blocks, scratch
     )
     return got[0], got[1:]
 
 
-def weight_kernel(sz, cuts, left, right, *refs):
+gain_names = ("input", "attn", "pre", "post", "query", "key")
+gain_pad = 16
+
+
+def weight_kernel(sz, cuts, gain_count, left, right, *refs):
+    gains, refs = refs[:gain_count], refs[gain_count:]
     outs, turned = refs[:-1], refs[-1]
     turned[...] = left[...].T
     half = left.shape[1] // 2
@@ -568,27 +585,69 @@
     y_index = lax.axis_index("ctx") & 1
     for side, owner in ((0, 1 - fsdp_index), (1, fsdp_index)):
         for part, y_half in ((0, y_index), (1, 1 - y_index)):
-            first = pl.multiple_of(owner * half + y_half * (half // 2), 16)
-            rows = turned[pl.ds(first, half // 2), :]
-            for index, (start, stop) in enumerate(cuts):
-                outs[2 * index + side][part * (half // 2) : (part + 1) * (half // 2), :] = dot_nn(
-                    rows, right[:, start:stop]
+            base = owner * half + y_half * (half // 2)
+            for index, (first_row, count, first_col, cols) in enumerate(cuts):
+                out = outs[2 * index + side]
+                rows = turned[pl.ds(pl.multiple_of(base + first_row, 16), count), :]
+                first_out = part * (out.shape[0] // 2)
+                out[first_out : first_out + count, :] = dot_nn(
+                    rows, right[:, first_col : first_col + cols]
                 ).astype(bf16)
-
-
-def weight_terms(sz, left, right, pieces):
-    half = left.shape[1] // 2
-    width = right.shape[1] // pieces
-    cuts = [(index * width, (index + 1) * width) for index in range(pieces)]
-    outs = [struct((half, width), bf16)] * (2 * pieces)
+                if gain_count:
+                    out[first_out + count : first_out + count + gain_pad, :] = gain_rows(
+                        sz, gains, owner, y_half, cols
+                    )
+
+
+def gain_rows(sz, gains, owner, y_half, cols):
+    halves = []
+    for gain in gains:
+        half = gain.shape[1] // 2
+        halves.append(jnp.where(owner == 0, gain[:, :half], gain[:, half:]))
+    flat = jnp.where(y_half == 0, jnp.concatenate(halves, axis=1), 0.0)
+    rows = [flat[:, first : first + cols] for first in range(0, flat.shape[1], cols)]
+    rows.append(jnp.zeros((gain_pad - len(rows), cols), f32))
+    return jnp.concatenate(rows, axis=0).astype(bf16)
+
+
+def tail_kernel(sz, count, mine, other, key, value, *gains):
+    y_index = lax.axis_index("ctx") & 1
+    for source, y_half in ((mine, y_index), (other, 1 - y_index)):
+        rows = pl.ds(pl.multiple_of(y_half * count, 16), count)
+        key[rows, :] = source[:count, : sz.head_dim].astype(f32)
+        value[rows, :] = source[:count, sz.head_dim :].astype(f32)
+    row_count = sum(gain.shape[1] for gain in gains) // mine.shape[1]
+    here = mine[count : count + gain_pad, :].astype(f32)
+    there = other[count : count + gain_pad, :].astype(f32)
+    lower = jnp.where(y_index == 0, here, there)
+    flat = jnp.concatenate([lower[row : row + 1, :] for row in range(row_count)], axis=1)
+    start = 0
+    for gain in gains:
+        gain[...] = flat[:, start : start + gain.shape[1]]
+        start += gain.shape[1]
+
+
+def finish_tail(sz, mine, other):
+    half = sz.model // 2
+    outs = [struct((half, sz.head_dim), f32)] * 2
+    outs += [struct((1, sz.gain_at[name][1]), f32) for name in gain_names]
+    return call_kernel(
+        functools.partial(tail_kernel, sz, half // 2), outs, [mine, other], [], []
+    )
+
+
+def weight_terms(sz, left, right, cuts, gains=()):
+    outs = []
+    for _, count, _, cols in cuts:
+        outs += [struct((2 * (count + (gain_pad if gains else 0)), cols), bf16)] * 2
     got = call_kernel(
-        functools.partial(weight_kernel, sz, cuts),
+        functools.partial(weight_kernel, sz, cuts, len(gains)),
         outs,
-        [left, right],
+        [left, right, *gains],
         [],
         [pltpu.VMEM((left.shape[1], left.shape[0]), bf16)],
     )
-    return [(got[2 * index], got[2 * index + 1]) for index in range(pieces)]
+    return [(got[2 * index], got[2 * index + 1]) for index in range(len(cuts))]
 
 
 def query_back_kernel(
@@ -727,6 +786,17 @@
     return list(got) + [parts[0], came[3]]
 
 
+def scatter_pairs(pairs):
+    came = yield [(pairs[mask // 2], "ctx", xor_pairs(8, mask)) for mask in (6, 4, 2)]
+    total = pairs[0].astype(f32)
+    for term in came:
+        total = total + term.astype(f32)
+    other = lax.optimization_barrier(total[1].astype(bf16))
+    own = lax.optimization_barrier(total[0])
+    (got,) = yield [(other, "ctx", xor_pairs(8, 1))]
+    return [own, got]
+
+
 def sum_stages(make):
     send, keep = make()
     ctx_index = lax.axis_index("ctx")
@@ -747,8 +817,13 @@
     (came,) = yield [(part, "ctx", outward)]
     total = jnp.where((z_index == 1) | (z_index == 2), part, came)
     (other,) = yield [(total, "ctx", y_swap)]
-    first = jnp.where(y_index == 0, total, other)
-    second = jnp.where(y_index == 0, other, total)
+    return (total, other)
+
+
+def join_halves(mine, other):
+    y_index = lax.axis_index("ctx") & 1
+    first = jnp.where(y_index == 0, mine, other)
+    second = jnp.where(y_index == 0, other, mine)
     return jnp.concatenate([first, second], axis=0).astype(f32)
 
 
@@ -759,16 +834,23 @@
     both = add_low(keep, came)
     first = jnp.where(y_index == 0, both[:half], both[half:])
     second = jnp.where(y_index == 0, both[half:], both[:half])
-    return lax.psum(jnp.concatenate([first, second], axis=0).astype(f32), "ctx")
-
-
-def run_staggered(sets):
+    whole = lax.psum(jnp.concatenate([first, second], axis=0).astype(f32), "ctx")
+    first, second = whole[:half], whole[half:]
+    return (jnp.where(y_index == 0, first, second), jnp.where(y_index == 0, second, first))
+
+
+def run_turns(sets, turns, held):
     results = {}
-    states = [dict(entries=list(one), active=[], turn=0, landed=None) for one in sets]
-    turn = 0
-    while any(st["active"] or st["turn"] < len(st["entries"]) for st in states):
-        state = states[turn % len(states)]
-        turn += 1
+    states = {
+        name: dict(entries=list(one), active=[], turn=0, landed=None)
+        for name, one in sets.items()
+    }
+    latest = [None, ()]
+
+    def alive(state):
+        return state["active"] or state["turn"] < len(state["entries"])
+
+    def step(state):
         going = []
         for (name, stage, _), landed in zip(state["active"], state["landed"] or []):
             try:
@@ -777,21 +859,35 @@
                 results[name] = end.value
         if state["turn"] < len(state["entries"]):
             for name, make_stage in state["entries"][state["turn"]]:
-                stage = make_stage(results)
+                stage = make_stage()
                 going.append((name, stage, next(stage)))
         state["turn"] += 1
         state["active"] = going
         state["landed"] = None
         if not going:
-            continue
+            return
         operands = [[move[0] for move in moves] for _, _, moves in going]
-        for other in states:
+        for other in states.values():
             if other is not state and other["landed"] is not None:
                 other["landed"] = after(other["landed"], operands)
         state["landed"] = [
             [lax.ppermute(value, axis, pairs) for value, axis, pairs in moves]
             for _, _, moves in going
         ]
+        latest[:] = [state, operands]
+
+    for turn in turns:
+        if callable(turn):
+            state, operands = latest
+            got = turn(results, lambda value: after(value, operands))
+            got, state["landed"] = lax.optimization_barrier((got, state["landed"]))
+            held.update(got)
+        else:
+            step(states[turn])
+    while any(alive(state) for state in states.values()):
+        for state in states.values():
+            if alive(state):
+                step(state)
     return results
 
 
@@ -874,6 +970,8 @@
             sz, hidden, gains, tables, weights["key"], weights["value"]
         )
         query_lin, query_low = project_query(sz, normed, gains, tables, weights["query"])
+        if not save:
+            kv_low = after(kv_low, weights)
         blocks = gather_ctx(kv_low.reshape(block_shape), query_low)
         got = forward_layer(sz, query_low, hidden, gains, places, blocks, weights, save)
         if not save:
@@ -911,7 +1009,7 @@
 
     own_grad = out_cotangent.reshape(sz.rows, model_width)
     got = ffw_back(sz, own_grad, gains, saved, weights)
-    query_grad, parts = attn_back(sz, got[8], saved, places)
+    query_grad, parts = attn_back(sz, got[8], saved, places, False)
     _, query_part, _ = queries_back(query_grad, saved)
     terms = run_alone(scatter_stages(parts)) if small_ctx() else scatter_plain(parts)
     first_grad = input_part(terms, got[0], query_part, saved)[0]
@@ -920,109 +1018,72 @@
 
     got = ffw_back(sz, grad_in, gains, saved, weights)
     middle_grad, down_low, gate_low, up_low, branch_low, gain_post, gain_pre, gain_attn = got[:8]
-    down_terms = weight_terms(sz, saved["act"], down_low, 1)
-    gate_terms = weight_terms(sz, saved["pre_ffw"], gate_low, 2)
-    up_terms = weight_terms(sz, saved["pre_ffw"], up_low, 2)
-    out_terms = weight_terms(sz, saved["attn_low"], branch_low, 1)
-    query_grad, parts = attn_back(sz, got[8], saved, places)
-    query_lin_low, query_part, gain_query = queries_back(query_grad, saved)
-    query_terms = weight_terms(sz, saved["normed"], query_lin_low, 1)
-    half_down = down_terms[0][0].shape[0] // 2
-    cut = half_down // 2
-
-    def down_piece(index):
-        rows = [slice(first + index * cut, first + (index + 1) * cut) for first in (0, half_down)]
-        return tuple(
-            jnp.concatenate([term[rows[0]], term[rows[1]]], axis=0) for term in down_terms[0]
+    model_quarter = model_width // 4
+    kv_width = 2 * head_dim
+    down_cuts = [(0, sz.ff // 4, 0, model_width)]
+    wide_cuts = [(0, model_quarter, 0, sz.ff)]
+    out_cuts = [(0, sz.query_cols // 4, 0, model_width)]
+    query_cuts = [(0, model_quarter, 0, sz.query_cols)]
+    kv_cuts = [(0, model_quarter, 0, kv_width)]
+    at = {"down": weight_terms(sz, saved["act"], down_low, down_cuts)}
+
+    def do_gate(results, later):
+        return {"gate": weight_terms(sz, saved["pre_ffw"], later(gate_low), wide_cuts)}
+
+    def do_up(results, later):
+        return {"up": weight_terms(sz, saved["pre_ffw"], later(up_low), wide_cuts)}
+
+    def do_attention(results, later):
+        query_grad, parts = attn_back(sz, later(got[8]), saved, places, True)
+        return {"query_grad": query_grad, "parts": parts}
+
+    def do_queries(results, later):
+        low, query_part, gain_query = queries_back(later(at["query_grad"]), saved)
+        terms = weight_terms(sz, saved["normed"], low, query_cuts)
+        return {"query": terms, "query_part": query_part, "gain_query": gain_query}
+
+    def do_out(results, later):
+        return {"out": weight_terms(sz, saved["attn_low"], later(branch_low), out_cuts)}
+
+    def do_tail(results, later):
+        terms = results["kv"] if small_ctx() else scatter_plain(at["parts"])
+        input_grad, kv_grad, gain_input, gain_key = input_part(
+            later(terms), middle_grad, at["query_part"], saved
         )
-
-    ends = {}
-    kv_width = 2 * head_dim
-    gain_count = gains_own.shape[1] // kv_width
-    half_model = model_width // 2
-
-    def tail_terms(terms):
-        input_grad, kv_grad, gain_input, gain_key = input_part(
-            terms, middle_grad, query_part, saved
+        gain_grads = (gain_input, gain_attn, gain_pre, gain_post, at["gain_query"], gain_key)
+        terms = weight_terms(sz, saved["normed"], kv_grad, kv_cuts, gain_grads)
+        return {"tail": terms, "input_grad": input_grad}
+
+    if small_ctx():
+
+        def chunk(name, index):
+            return (name + str(index), lambda: sum_stages(lambda: at[name][index]))
+
+        sets = {
+            "a": [[chunk("down", 0)], [], [chunk("up", 0)], [], [], [chunk("tail", 0)]],
+            "b": [[chunk("gate", 0)], [chunk("out", 0)], [chunk("query", 0)]],
+            "kv": [[("kv", lambda: scatter_pairs(at["parts"]))]],
+        }
+        turns = (
+            ["a", "a", do_gate, "b", do_up, do_out, "b", do_attention, "a", do_queries, "b"]
+            + ["a", "kv", "b", "a", "kv", "b", "kv", do_tail]
         )
-        ends["input_grad"] = input_grad
-        send, keep = weight_terms(sz, saved["normed"], kv_grad, 1)[0]
-        gain_grads = (gain_input, gain_attn, gain_pre, gain_post, gain_query, gain_key)
-        gain_rows = jnp.concatenate([grad.reshape(2, -1) for grad in gain_grads], axis=1)
-        gain_rows = gain_rows.reshape(2, gain_count, kv_width).astype(bf16)
-        gain_rows = jnp.pad(gain_rows, ((0, 0), (0, 16 - gain_count), (0, 0)))
-        zeros = jnp.zeros_like(gain_rows[0])
-        is_lower = (ctx_index & 1) == 0
-        pairs = []
-        for term, owner in ((send, 1 - fsdp_index), (keep, fsdp_index)):
-            here = lax.dynamic_index_in_dim(gain_rows, owner, 0, keepdims=False)
-            half = term.shape[0] // 2
-            pairs.append(
-                jnp.concatenate(
-                    [
-                        term[:half],
-                        jnp.where(is_lower, here, zeros),
-                        term[half:],
-                        jnp.where(is_lower, zeros, here),
-                    ],
-                    axis=0,
-                )
-            )
-        return tuple(pairs)
-
-    if small_ctx():
-
-        def chunk(make):
-            return lambda results: sum_stages(make)
-
-        sets = [
-            [
-                [("down0", chunk(lambda: down_piece(0)))],
-                [("gate0", chunk(lambda: gate_terms[0]))],
-                [("up0", chunk(lambda: up_terms[0])), ("kv", lambda results: scatter_stages(parts))],
-                [("out", chunk(lambda: out_terms[0]))],
-                [],
-                [("tail", lambda results: sum_stages(lambda: tail_terms(results["kv"])))],
-            ],
-            [
-                [("down1", chunk(lambda: down_piece(1)))],
-                [("gate1", chunk(lambda: gate_terms[1]))],
-                [("up1", chunk(lambda: up_terms[1]))],
-                [("query", chunk(lambda: query_terms[0]))],
-            ],
-        ]
-        sums = run_staggered(sets)
+        sums = run_turns(sets, turns, at)
     else:
+        for work in (do_gate, do_up, do_attention, do_queries, do_out, do_tail):
+            at.update(work({}, lambda value: value))
         sums = {}
-        for index in range(2):
-            sums["down%d" % index] = sum_plain(*down_piece(index))
-            sums["gate%d" % index] = sum_plain(*gate_terms[index])
-            sums["up%d" % index] = sum_plain(*up_terms[index])
-        sums["out"] = sum_plain(*out_terms[0])
-        sums["query"] = sum_plain(*query_terms[0])
-        sums["tail"] = sum_plain(*tail_terms(scatter_plain(parts)))
-    input_grad = ends["input_grad"]
-    sum_down = jnp.concatenate(
-        [
-            sums["down0"][:cut], sums["down1"][:cut], sums["down0"][cut:], sums["down1"][cut:],
-        ],
-        axis=0,
-    )
-    sum_gate = jnp.concatenate([sums["gate0"], sums["gate1"]], axis=1)
-    sum_up = jnp.concatenate([sums["up0"], sums["up1"]], axis=1)
-    sum_out = sums["out"]
-    sum_query = sums["query"]
-    sum_tail = sums["tail"]
-    quarter = half_model // 2
-    sum_kv = jnp.concatenate(
-        [sum_tail[:quarter], sum_tail[quarter + 16 : quarter + 16 + quarter]], axis=0
-    )
-    sum_key = sum_kv[:, :head_dim]
-    sum_value = sum_kv[:, head_dim:]
-    sum_gains = sum_tail[quarter : quarter + gain_count].reshape(-1)
-    gain_sums = {}
-    for name, (start, width) in sz.gain_at.items():
-        gain_sums[name] = sum_gains[start : start + width]
+        for name in ("down", "gate", "up", "out", "query", "tail"):
+            for index, pair in enumerate(at[name]):
+                sums[name + str(index)] = sum_plain(*pair)
+    input_grad = at["input_grad"]
+    sum_down = join_halves(*sums["down0"])
+    sum_gate = join_halves(*sums["gate0"])
+    sum_up = join_halves(*sums["up0"])
+    sum_out = join_halves(*sums["out0"])
+    sum_query = join_halves(*sums["query0"])
+    sum_key, sum_value, *gain_parts = finish_tail(sz, *sums["tail0"])
+    gain_sums = {name: part[0] for name, part in zip(gain_names, gain_parts)}
     shape = (micro_count, seq_local, tokens, model_width)
     members = (
         sum_query,

time: 452 us -> 417 us (0.923)
  starting transfers between devices: 139 us -> 106 us
  waiting for transfers between devices: 137 us -> 147 us
  other arithmetic: 33.7 us -> 26.6 us
  local copies, waits for them, and re-layouts: 17.4 us -> 11.4 us
    ppermute x61 -> x40, starting transfers between devices: 94.3 us -> 60.5 us  [step(): lax.ppermute(value, axis, pairs)]
    ppermute x61 -> x40, waiting for transfers between devices: 67.5 us -> 88.5 us  [step(): lax.ppermute(value, axis, pairs)]
    ppermute x22, waiting for transfers between devices: 49.1 us -> 38.8 us  [xor_permute(): return lax.ppermute(shard, axis, [(i, i ^ mask) for i in range(count)])]
    broadcast_in_dim x4 -> x0, other arithmetic: 6.14 us -> none  [on_device(): member[None]]
    convert_element_type x42 -> x27, other arithmetic: 14.2 us -> 12.4 us  [add_low(): return lax.optimization_barrier(total.astype(bf16))]
    pallas_call x20 -> x21, Pallas kernels: 114 us -> 115 us  [call_kernel(): pl.pallas_call(body, out_shape=out_shapes, in_specs=[whole] * len(inputs)...]
  transfers between devices with their start and end apart: 92 -> 71, of which waited for: 34 -> 31; matrix products, arithmetic and copies ran while one was open for 8% -> 6% of each run, Pallas kernels for 11% -> 12%
where the time goes in v4:
time: 417 us; the launch traced here: 409 us
  waiting for transfers between devices  147 us (35%)
  Pallas kernels  115 us (28%)
  starting transfers between devices  106 us (25%)
  other arithmetic  26.6 us (6%)
  local copies, waits for them, and re-layouts  11.4 us (3%)
    pallas_call x21, Pallas kernels, call_kernel(): pl.pallas_call(body, out_shape=out_shapes, in_specs=[whole] * len(inputs)...  115 us
    ppermute x40, waiting for transfers between devices, step(): lax.ppermute(value, axis, pairs)  88.5 us
    ppermute x40, starting transfers between devices, step(): lax.ppermute(value, axis, pairs)  60.5 us
    ppermute x22, waiting for transfers between devices, xor_permute(): return lax.ppermute(shard, axis, [(i, i ^ mask) for i in range(count)])  38.8 us
    ppermute x22, starting transfers between devices, xor_permute(): return lax.ppermute(shard, axis, [(i, i ^ mask) for i in range(count)])  24 us
    ppermute x7, starting transfers between devices, run_alone(): lax.ppermute(value, axis, pairs)  16.4 us
    convert_element_type x27, other arithmetic, add_low(): return lax.optimization_barrier(total.astype(bf16))  12.4 us
  transfers between devices with their start and end apart: 71, of which 31 were waited for; matrix products, arithmetic and copies ran while one was open for 6% of the time, Pallas kernels for 12%

profile of v4, /device:TPU:0, one launch (start us, length us, event | category | flops | bytes accessed | tf_op | source)
XLA Modules:
  0.0 408.8 jit_solution(14726935078257574409)
XLA Ops:
  20.9 4.1 %shard_map.272 = (f32[256,1024]{1,0:T(8,128)}, bf16[2,512,256]{2,1,0:T(8,128)(2,1)}) custom-call(bf16[256,640]{1,0:T(8,128)(2,1)} %get-tuple-element.178.normed, bf16[1,1536]{1,0:T(2,128)(2,1)} %copy-done.18, bf16[1,1536]{1,0:T(2,128)(2,1)} %copy-done.19, f32[128,128]{1,0:T(8,128)} %get-tuple-element.382.cos_ref.refs_11_.refs_8_, ...), custom_call_target="tpu_custom_call" | custom-call | bytes 10045440 | tf_op jit(solution)/shard_map/pallas_call | solution.py:72
  31.4 8.0 %collective-permute-done.11.refs_10_ = bf16[2,128,512]{2,1,0:T(8,128)(2,1)} collective-permute-done((bf16[2,128,512]{2,1,0:T(8,128)(2,1)}, bf16[2,128,512]{2,1,0:T(8,128)(2,1)}, u32[]{:S(2)}, u32[]{:S(2)}) %collective-permute-start.11) | collective-permute-done | bytes 262176 | tf_op jit(solution)/shard_map/ppermute | solution.py:737
  43.1 3.9 collective-permute-done.12.refs_11_
  49.9 9.6 %shard_map.273 = bf16[256,640]{1,0:T(8,128)(2,1)} custom-call(bf16[2,512,256]{2,1,0:T(8,128)(2,1)} %get-tuple-element.179.refs_0_, bf16[256,640]{1,0:T(8,128)(2,1)} %bitcast.84, bf16[1,1536]{1,0:T(2,128)(2,1)} %copy-done.18, bf16[1,1536]{1,0:T(2,128)(2,1)} %copy-done.19, s32[1,1024]{1,0:T(1,128)} %add.188.refs_4_, s32[512,1]{1,0:T(8,128)} %copy.33.refs_5_, ...), custom_call_target="tpu_custom_call" | custom-call | bytes 37392384 | tf_op jit(solution)/shard_map/pallas_call | solution.py:72
  63.1 4.7 %collective-permute-done.15 = bf16[256,640]{1,0:T(8,128)(2,1)S(1)} collective-permute-done((bf16[256,640]{1,0:T(8,128)(2,1)}, bf16[256,640]{1,0:T(8,128)(2,1)S(1)}, u32[]{:S(2)}, u32[]{:S(2)}) %collective-permute-start.15) | collective-permute-done | bytes 327712 | tf_op jit(solution)/shard_map/ppermute | solution.py:1006
  80.1 4.1 shard_map.275
  85.0 11.5 %collective-permute-done.19.refs_10_.refs_9_ = bf16[2,128,512]{2,1,0:T(8,128)(2,1)S(1)} collective-permute-done((bf16[2,128,512]{2,1,0:T(8,128)(2,1)}, bf16[2,128,512]{2,1,0:T(8,128)(2,1)S(1)}, u32[]{:S(2)}, u32[]{:S(2)}) %collective-permute-start.19) | collective-permute-done | bytes 262176 | tf_op jit(solution)/shard_map/ppermute | solution.py:737
  106.4 11.3 %shard_map.276 = (bf16[256,640]{1,0:T(8,128)(2,1)}, f32[2,512,1]{2,1,0:T(8,128)}, bf16[256,1024]{1,0:T(8,128)(2,1)}, f32[256,640]{1,0:T(8,128)}, f32[256,640]{1,...) custom-call(bf16[2,512,256]{2,1,0:T(8,128)(2,1)} %get-tuple-element., ...), custom_call_target="tpu_custom_call" | custom-call | bytes 61587456 | tf_op jit(solution)/shard_map/pallas_call | solution.py:72
  119.6 12.4 %shard_map.277 = (f32[256,640]{1,0:T(8,128)}, bf16[256,640]{1,0:T(8,128)(2,1)}, bf16[256,2048]{1,0:T(8,128)(2,1)}, bf16[256,2048]{1,0:T(8,128)(2,1)}, bf16[256,6...) custom-call(bf16[256,640]{1,0:T(8,128)(2,1)} %bitcast.103, ...), custom_call_target="tpu_custom_call" | custom-call | bytes 58827264 | tf_op jit(solution)/shard_map/pallas_call | solution.py:72
  131.9 8.4 %shard_map.278 = (f32[2,512,256]{2,1,0:T(8,128)}, bf16[2,128,512]{2,1,0:T(8,128)(2,1)}, bf16[2,128,512]{2,1,0:T(8,128)(2,1)}, bf16[2,128,512]{2,1,0:T(8,128)(2,1...) custom-call(bf16[256,1024]{1,0:T(8,128)(2,1)} %get-tuple-element.197, ...), custom_call_target="tpu_custom_call" | custom-call | bytes 18905088 | tf_op jit(solution)/shard_map/pallas_call | solution.py:72
  144.5 3.6 collective-permute-done.23
  153.1 6.0 %collective-permute-start.26 = (bf16[2,128,512]{2,1,0:T(8,128)(2,1)S(1)}, bf16[2,128,512]{2,1,0:T(8,128)(2,1)S(1)}, u32[]{:S(2)}, u32[]{:S(2)}) collective-permute-start(bf16[2,128,512]{2,1,0:T(8,128)(2,1)S(1)} %add_convert_fusion.21), channel_id=1, source_target_pairs={{0,8},{2,10},{4,12},{6,14},{8,0},{10,2},{12,4},{14,6},{1,9},{3,11}... | collective-permute-start | bytes 786440 | tf_op jit(solution)/shard_map/ppermute | solution.py:898
  162.6 4.4 %shard_map.279 = (bf16[256,1024]{1,0:T(8,128)(2,1)}, f32[256,640]{1,0:T(8,128)}, f32[1,256]{1,0:T(1,128)}) custom-call(f32[2,512,256]{2,1,0:T(8,128)} %get-tuple-element.208.query_grad, f32[256,1024]{1,0:T(8,128)} %get-tuple-element.209.query_lin, bf16[1,1536]{1,0:T(2,128)(2,1)} %copy-done.18, bf16[1,1536]{1,0:T(2,128)(2,1)} %copy-done.19, ...), custom_call_target="tpu_custom_call" | custom-call | bytes 14177280 | tf_op jit(solution)/shard_map/pallas_call | solution.py:72
  167.0 4.2 %collective-permute-done.26 = bf16[2,128,512]{2,1,0:T(8,128)(2,1)S(1)} collective-permute-done((bf16[2,128,512]{2,1,0:T(8,128)(2,1)S(1)}, bf16[2,128,512]{2,1,0:T(8,128)(2,1)S(1)}, u32[]{:S(2)}, u32[]{:S(2)}) %collective-permute-start.26) | collective-permute-done | bytes 262176 | tf_op jit(solution)/shard_map/ppermute | solution.py:898
  172.0 4.4 %shard_map.280 = (bf16[256,640]{1,0:T(8,128)(2,1)}, bf16[256,512]{1,0:T(8,128)(2,1)}, f32[1,640]{1,0:T(1,128)}, f32[1,256]{1,0:T(1,128)}) custom-call(bf16[256,512]{1,0:T(8,128)(2,1)} %bitcast.111, bf16[256,512]{1,0:T(8,128)(2,1)} %bitcast.112, bf16[256,512]{1,0:T(8,128)(2,1)} %bitcast.113, bf16[256,512]{1,0:T(8,128)(2,1)} %bitcast.109, ...), custom_call_target="tpu_custom_call" | custom-call | bytes 13791744 | tf_op jit(solution)/shard_map/pallas_call | solution.py:72
  178.2 7.5 %collective-permute-done.30 = bf16[256,640]{1,0:T(8,128)(2,1)S(1)} collective-permute-done((bf16[256,640]{1,0:T(8,128)(2,1)}, bf16[256,640]{1,0:T(8,128)(2,1)S(1)}, u32[]{:S(2)}, u32[]{:S(2)}) %collective-permute-start.30) | collective-permute-done | bytes 327712 | tf_op jit(solution)/shard_map/ppermute | solution.py:1016
  186.5 12.2 %shard_map.281 = (f32[256,640]{1,0:T(8,128)}, bf16[256,640]{1,0:T(8,128)(2,1)}, bf16[256,2048]{1,0:T(8,128)(2,1)}, bf16[256,2048]{1,0:T(8,128)(2,1)}, bf16[256,6...) custom-call(bf16[256,640]{1,0:T(8,128)(2,1)} %broadcast_select_fusion, ...), custom_call_target="tpu_custom_call" | custom-call | bytes 58827264 | tf_op jit(solution)/shard_map/pallas_call | solution.py:72
  212.8 11.8 %collective-permute-done.32 = bf16[512,640]{1,0:T(8,128)(2,1)S(1)} collective-permute-done((bf16[512,640]{1,0:T(8,128)(2,1)S(1)}, bf16[512,640]{1,0:T(8,128)(2,1)S(1)}, u32[]{:S(2)}, u32[]{:S(2)}) %collective-permute-start.32) | collective-permute-done | bytes 655392 | tf_op jit(solution)/shard_map/ppermute | solution.py:874
  238.4 8.5 %shard_map.286 = (f32[2,512,256]{2,1,0:T(8,128)}, bf16[2,2,128,512]{3,2,1,0:T(8,128)(2,1)}, bf16[2,2,128,512]{3,2,1,0:T(8,128)(2,1)}, bf16[2,2,128,512]{3,2,1,0:T(8,128)(2,1)}, bf16[2,2,128,512]{3,2,1,0:T(8,128)(2,1)}) custom-call(bf16[256,1024]{1,0:T(8,128)(2,1)} %get-tuple-element.237.refs_0_, bf16[2,512,256]{2,1,0:T(8,128)(2,1)} %get-tuple-element.186.refs_0_.refs_1_, ...), custom_call_target="tpu_custom_call" | custom-call | bytes 18905088 | tf_op jit(solution)/shard_map/pallas_call | solution.py:72
  251.7 5.3 %collective-permute-start.39 = (bf16[160,2048]{1,0:T(8,128)(2,1)S(1)}, bf16[160,2048]{1,0:T(8,128)(2,1)S(1)}, u32[]{:S(2)}, u32[]{:S(2)}) collective-permute-start(bf16[160,2048]{1,0:T(8,128)(2,1)S(1)} %add_convert_fusion.8), channel_id=1, source_target_pairs={{0,4},{2,6},{12,8},{14,10},{1,5},{3,7},{13,9},{15,11},{16,20},{18,... | collective-permute-start | bytes 1966088 | tf_op jit(solution)/shard_map/ppermute | solution.py:874
  258.1 4.3 %shard_map.287 = (bf16[256,1024]{1,0:T(8,128)(2,1)}, f32[256,640]{1,0:T(8,128)}, f32[1,256]{1,0:T(1,128)}) custom-call(f32[2,512,256]{2,1,0:T(8,128)} %get-tuple-element.257.query_grad, f32[256,1024]{1,0:T(8,128)} %get-tuple-element.209.query_lin, bf16[1,1536]{1,0:T(2,128)(2,1)} %copy-done.18, bf16[1,1536]{1,0:T(2,128)(2,1)} %copy-done.19, ...), custom_call_target="tpu_custom_call" | custom-call | bytes 14177280 | tf_op jit(solution)/shard_map/pallas_call | solution.py:72
  268.2 5.5 %collective-permute-done.40 = bf16[256,640]{1,0:T(8,128)(2,1)S(1)} collective-permute-done((bf16[256,640]{1,0:T(8,128)(2,1)S(1)}, bf16[256,640]{1,0:T(8,128)(2,1)S(1)}, u32[]{:S(2)}, u32[]{:S(2)}) %collective-permute-start.40) | collective-permute-done | bytes 327712 | tf_op jit(solution)/shard_map/ppermute | solution.py:874
  273.7 16.1 %collective-permute-done.39 = bf16[160,2048]{1,0:T(8,128)(2,1)S(1)} collective-permute-done((bf16[160,2048]{1,0:T(8,128)(2,1)S(1)}, bf16[160,2048]{1,0:T(8,128)(2,1)S(1)}, u32[]{:S(2)}, u32[]{:S(2)}) %collective-permute-start.39) | collective-permute-done | bytes 655392 | tf_op jit(solution)/shard_map/ppermute | solution.py:874
  296.1 6.5 %collective-permute-start.48 = (bf16[256,640]{1,0:T(8,128)(2,1)S(1)}, bf16[256,640]{1,0:T(8,128)(2,1)S(1)}, u32[]{:S(2)}, u32[]{:S(2)}) collective-permute-start(bf16[256,640]{1,0:T(8,128)(2,1)S(1)} %add_convert_fusion.18), channel_id=1, source_target_pairs={{0,4},{2,6},{12,8},{14,10},{1,5},{3,7},{13,9},{15,11},{16,20},{18,... | collective-permute-start | bytes 983048 | tf_op jit(solution)/shard_map/ppermute | solution.py:874
  303.7 4.6 %collective-permute-done.45 = bf16[160,2048]{1,0:T(8,128)(2,1)S(1)} collective-permute-done((bf16[160,2048]{1,0:T(8,128)(2,1)S(1)}, bf16[160,2048]{1,0:T(8,128)(2,1)S(1)}, u32[]{:S(2)}, u32[]{:S(2)}) %collective-permute-start.45) | collective-permute-done | bytes 655392 | tf_op jit(solution)/shard_map/ppermute | solution.py:874
  310.0 7.0 %collective-permute-start.54 = (bf16[160,2048]{1,0:T(8,128)(2,1)S(1)}, bf16[160,2048]{1,0:T(8,128)(2,1)S(1)}, u32[]{:S(2)}, u32[]{:S(2)}) collective-permute-start(bf16[160,2048]{1,0:T(8,128)(2,1)S(1)} %add_convert_fusion.3), channel_id=1, source_target_pairs={{0,4},{2,6},{12,8},{14,10},{1,5},{3,7},{13,9},{15,11},{16,20},{18,... | collective-permute-start | bytes 1966088 | tf_op jit(solution)/shard_map/ppermute | solution.py:874
  325.7 6.0 %collective-permute-start.52 = (bf16[160,1024]{1,0:T(8,128)(2,1)S(1)}, bf16[160,1024]{1,0:T(8,128)(2,1)S(1)}, u32[]{:S(2)}, u32[]{:S(2)}) collective-permute-start(bf16[160,1024]{1,0:T(8,128)(2,1)S(1)} %add_convert_fusion.15), channel_id=1, source_target_pairs={{0,4},{2,6},{12,8},{14,10},{1,5},{3,7},{13,9},{15,11},{16,20},{18,... | collective-permute-start | bytes 983048 | tf_op jit(solution)/shard_map/ppermute | solution.py:874
  334.5 4.2 %shard_map.289 = (bf16[256,640]{1,0:T(8,128)(2,1)}, bf16[256,512]{1,0:T(8,128)(2,1)}, f32[1,640]{1,0:T(1,128)}, f32[1,256]{1,0:T(1,128)}) custom-call(f32[256,512]{1,0:T(8,128)} %bitcast.102, bf16[256,512]{1,0:T(8,128)(2,1)} %bitcast.114, f32[256,256]{1,0:T(8,128)} %get-tuple-element.207.refs_5_.refs_2_, ...), custom_call_target="tpu_custom_call" | custom-call | bytes 12218880 | tf_op jit(solution)/shard_map/pallas_call | solution.py:72
  343.5 6.1 %collective-permute-done.58 = bf16[512,640]{1,0:T(8,128)(2,1)S(1)} collective-permute-done((bf16[512,640]{1,0:T(8,128)(2,1)S(1)}, bf16[512,640]{1,0:T(8,128)(2,1)S(1)}, u32[]{:S(2)}, u32[]{:S(2)}) %collective-permute-start.58) | collective-permute-done | bytes 655392 | tf_op jit(solution)/shard_map/ppermute | solution.py:874
  355.4 8.2 %collective-permute-done.55 = bf16[160,2048]{1,0:T(8,128)(2,1)S(1)} collective-permute-done((bf16[160,2048]{1,0:T(8,128)(2,1)S(1)}, bf16[160,2048]{1,0:T(8,128)(2,1)S(1)}, u32[]{:S(2)}, u32[]{:S(2)}) %collective-permute-start.55) | collective-permute-done | bytes 655392 | tf_op jit(solution)/shard_map/ppermute | solution.py:874
  377.7 10.8 %collective-permute-done.66 = bf16[160,2048]{1,0:T(8,128)(2,1)S(1)} collective-permute-done((bf16[160,2048]{1,0:T(8,128)(2,1)S(1)}, bf16[160,2048]{1,0:T(8,128)(2,1)S(1)}, u32[]{:S(2)}, u32[]{:S(2)}) %collective-permute-start.66) | collective-permute-done | bytes 655392 | tf_op jit(solution)/shard_map/ppermute | solution.py:874
  389.3 3.7 collective-permute-done.65
  (272 shorter events, 178.2 us)
Async XLA Ops:
  17.7 21.6 %collective-permute-start.11 = (bf16[2,128,512]{2,1,0:T(8,128)(2,1)}, bf16[2,128,512]{2,1,0:T(8,128)(2,1)}, u32[]{:S(2)}, u32[]{:S(2)}) collective-permute-start(bf16[2,128,512]{2,1,0:T(8,128)(2,1)} %bitcast.105), channel_id=1, source_target_pairs={{0,8},{2,10},{4,12},{6,14},{8,0},{10,2},{12,4},{14,6},{1,9},{3,11}... | collective-permute-start | bytes 786440 | tf_op jit(solution)/shard_map/ppermute | solution.py:737
  20.3 20.6 %collective-permute-start.13 = (bf16[2,128,512]{2,1,0:T(8,128)(2,1)}, bf16[2,128,512]{2,1,0:T(8,128)(2,1)}, u32[]{:S(2)}, u32[]{:S(2)}) collective-permute-start(bf16[2,128,512]{2,1,0:T(8,128)(2,1)} %bitcast.106), channel_id=1, source_target_pairs={{0,12},{2,14},{4,8},{6,10},{8,4},{10,6},{12,0},{14,2},{1,13},{3,15... | collective-permute-start | bytes 786440 | tf_op jit(solution)/shard_map/ppermute | solution.py:737
  25.0 18.1 %collective-permute-start.8 = (bf16[2,128,512]{2,1,0:T(8,128)(2,1)S(1)}, bf16[2,128,512]{2,1,0:T(8,128)(2,1)}, u32[]{:S(2)}, u32[]{:S(2)}) collective-permute-start(bf16[2,128,512]{2,1,0:T(8,128)(2,1)S(1)} %bitcast.108), channel_id=1, source_target_pairs={{0,2},{2,0},{4,6},{6,4},{8,10},{10,8},{12,14},{14,12},{1,3},{3,1},... | collective-permute-start | bytes 786440 | tf_op jit(solution)/shard_map/ppermute | solution.py:737
  76.1 20.3 %collective-permute-start.19 = (bf16[2,128,512]{2,1,0:T(8,128)(2,1)}, bf16[2,128,512]{2,1,0:T(8,128)(2,1)S(1)}, u32[]{:S(2)}, u32[]{:S(2)}) collective-permute-start(bf16[2,128,512]{2,1,0:T(8,128)(2,1)} %bitcast.96), channel_id=1, source_target_pairs={{0,8},{2,10},{4,12},{6,14},{8,0},{10,2},{12,4},{14,6},{1,9},{3,11}... | collective-permute-start | bytes 786440 | tf_op jit(solution)/shard_map/ppermute | solution.py:737
  77.9 20.1 %collective-permute-start.21 = (bf16[2,128,512]{2,1,0:T(8,128)(2,1)}, bf16[2,128,512]{2,1,0:T(8,128)(2,1)S(1)}, u32[]{:S(2)}, u32[]{:S(2)}) collective-permute-start(bf16[2,128,512]{2,1,0:T(8,128)(2,1)} %bitcast.97), channel_id=1, source_target_pairs={{0,12},{2,14},{4,8},{6,10},{8,4},{10,6},{12,0},{14,2},{1,13},{3,15... | collective-permute-start | bytes 786440 | tf_op jit(solution)/shard_map/ppermute | solution.py:737
  78.5 21.2 %collective-permute-start.16 = (bf16[2,128,512]{2,1,0:T(8,128)(2,1)}, bf16[2,128,512]{2,1,0:T(8,128)(2,1)S(1)}, u32[]{:S(2)}, u32[]{:S(2)}) collective-permute-start(bf16[2,128,512]{2,1,0:T(8,128)(2,1)} %bitcast.98), channel_id=1, source_target_pairs={{0,2},{2,0},{4,6},{6,4},{8,10},{10,8},{12,14},{14,12},{1,3},{3,1},... | collective-permute-start | bytes 786440 | tf_op jit(solution)/shard_map/ppermute | solution.py:737
  144.0 22.9 %collective-permute-start.29 = (bf16[2,128,512]{2,1,0:T(8,128)(2,1)}, bf16[2,128,512]{2,1,0:T(8,128)(2,1)S(1)}, u32[]{:S(2)}, u32[]{:S(2)}) collective-permute-start(bf16[2,128,512]{2,1,0:T(8,128)(2,1)} %get-tuple-element.206), channel_id=1, source_target_pairs={{0,2},{2,0},{4,6},{6,4},{8,10},{10,8},{12,14},{14,12},{1,3},{3,1},... | collective-permute-start | bytes 786440 | tf_op jit(solution)/shard_map/ppermute | solution.py:898
  149.2 17.8 %collective-permute-start.24 = (bf16[2,128,512]{2,1,0:T(8,128)(2,1)S(1)}, bf16[2,128,512]{2,1,0:T(8,128)(2,1)S(1)}, u32[]{:S(2)}, u32[]{:S(2)}) collective-permute-start(bf16[2,128,512]{2,1,0:T(8,128)(2,1)S(1)} %add_convert_fusion.22), channel_id=1, source_target_pairs={{0,12},{2,14},{4,8},{6,10},{8,4},{10,6},{12,0},{14,2},{1,13},{3,15... | collective-permute-start | bytes 786440 | tf_op jit(solution)/shard_map/ppermute | solution.py:898
  153.1 18.1 %collective-permute-start.26 = (bf16[2,128,512]{2,1,0:T(8,128)(2,1)S(1)}, bf16[2,128,512]{2,1,0:T(8,128)(2,1)S(1)}, u32[]{:S(2)}, u32[]{:S(2)}) collective-permute-start(bf16[2,128,512]{2,1,0:T(8,128)(2,1)S(1)} %add_convert_fusion.21), channel_id=1, source_target_pairs={{0,8},{2,10},{4,12},{6,14},{8,0},{10,2},{12,4},{14,6},{1,9},{3,11}... | collective-permute-start | bytes 786440 | tf_op jit(solution)/shard_map/ppermute | solution.py:898
  207.8 16.8 %collective-permute-start.32 = (bf16[512,640]{1,0:T(8,128)(2,1)S(1)}, bf16[512,640]{1,0:T(8,128)(2,1)S(1)}, u32[]{:S(2)}, u32[]{:S(2)}) collective-permute-start(bf16[512,640]{1,0:T(8,128)(2,1)S(1)} %add_convert_fusion.11), channel_id=1, source_target_pairs={{0,2},{2,0},{4,6},{6,4},{8,10},{10,8},{12,14},{14,12},{1,3},{3,1},... | collective-permute-start | bytes 1966088 | tf_op jit(solution)/shard_map/ppermute | solution.py:874
  233.0 17.4 %collective-permute-start.34 = (bf16[160,2048]{1,0:T(8,128)(2,1)}, bf16[160,2048]{1,0:T(8,128)(2,1)S(1)}, u32[]{:S(2)}, u32[]{:S(2)}) collective-permute-start(bf16[160,2048]{1,0:T(8,128)(2,1)} %add_convert_fusion.10), channel_id=1, source_target_pairs={{0,2},{2,0},{4,6},{6,4},{8,10},{10,8},{12,14},{14,12},{1,3},{3,1},... | collective-permute-start | bytes 1966088 | tf_op jit(solution)/shard_map/ppermute | solution.py:874
  234.7 32.0 %collective-permute-start.42 = (bf16[320,2048]{1,0:T(8,128)(2,1)}, bf16[320,2048]{1,0:T(8,128)(2,1)S(1)}, u32[]{:S(2)}, u32[]{:S(2)}) collective-permute-start(bf16[320,2048]{1,0:T(8,128)(2,1)} %get-tuple-element.252), channel_id=1, source_target_pairs={{0,1},{1,0},{2,3},{3,2},{4,5},{5,4},{6,7},{7,6},{8,9},{9,8},{10,11... | collective-permute-start | bytes 3932168 | tf_op jit(solution)/shard_map/ppermute | solution.py:874
  236.8 28.4 %collective-permute-start.41 = (bf16[512,640]{1,0:T(8,128)(2,1)S(1)}, bf16[512,640]{1,0:T(8,128)(2,1)S(1)}, u32[]{:S(2)}, u32[]{:S(2)}) collective-permute-start(bf16[512,640]{1,0:T(8,128)(2,1)S(1)} %add_convert_fusion.9), channel_id=1, source_target_pairs={{0,4},{2,6},{12,8},{14,10},{1,5},{3,7},{13,9},{15,11},{16,20},{18,... | collective-permute-start | bytes 1966088 | tf_op jit(solution)/shard_map/ppermute | solution.py:874
  250.4 42.6 %collective-permute-start.36 = (bf16[2,2,128,512]{3,2,1,0:T(8,128)(2,1)}, bf16[2,2,128,512]{3,2,1,0:T(8,128)(2,1)}, u32[]{:S(2)}, u32[]{:S(2)}) collective-permute-start(bf16[2,2,128,512]{3,2,1,0:T(8,128)(2,1)} %get-tuple-element.244), channel_id=1, source_target_pairs={{0,12},{2,14},{4,8},{6,10},{8,4},{10,6},{12,0},{14,2},{1,13},{3,15... | collective-permute-start | bytes 1572872 | tf_op jit(solution)/shard_map/ppermute | solution.py:874
  251.4 44.7 %collective-permute-start.37 = (bf16[2,2,128,512]{3,2,1,0:T(8,128)(2,1)}, bf16[2,2,128,512]{3,2,1,0:T(8,128)(2,1)}, u32[]{:S(2)}, u32[]{:S(2)}) collective-permute-start(bf16[2,2,128,512]{3,2,1,0:T(8,128)(2,1)} %get-tuple-element.245), channel_id=1, source_target_pairs={{0,8},{2,10},{4,12},{6,14},{8,0},{10,2},{12,4},{14,6},{1,9},{3,11}... | collective-permute-start | bytes 1572872 | tf_op jit(solution)/shard_map/ppermute | solution.py:874
  251.7 38.1 %collective-permute-start.39 = (bf16[160,2048]{1,0:T(8,128)(2,1)S(1)}, bf16[160,2048]{1,0:T(8,128)(2,1)S(1)}, u32[]{:S(2)}, u32[]{:S(2)}) collective-permute-start(bf16[160,2048]{1,0:T(8,128)(2,1)S(1)} %add_convert_fusion.8), channel_id=1, source_target_pairs={{0,4},{2,6},{12,8},{14,10},{1,5},{3,7},{13,9},{15,11},{16,20},{18,... | collective-permute-start | bytes 1966088 | tf_op jit(solution)/shard_map/ppermute | solution.py:874
  266.7 23.8 %collective-permute-start.43 = (bf16[320,1024]{1,0:T(8,128)(2,1)}, bf16[320,1024]{1,0:T(8,128)(2,1)S(1)}, u32[]{:S(2)}, u32[]{:S(2)}) collective-permute-start(bf16[320,1024]{1,0:T(8,128)(2,1)} %get-tuple-element.263), channel_id=1, source_target_pairs={{0,1},{1,0},{2,3},{3,2},{4,5},{5,4},{6,7},{7,6},{8,9},{9,8},{10,11... | collective-permute-start | bytes 1966088 | tf_op jit(solution)/shard_map/ppermute | solution.py:874
  273.7 28.9 %collective-permute-start.38 = (bf16[2,2,128,512]{3,2,1,0:T(8,128)(2,1)S(1)}, bf16[2,2,128,512]{3,2,1,0:T(8,128)(2,1)S(1)}, u32[]{:S(2)}, u32[]{:S(2)}) collective-permute-start(bf16[2,2,128,512]{3,2,1,0:T(8,128)(2,1)S(1)} %copy-done.36), channel_id=1, source_target_pairs={{0,4},{2,6},{4,0},{6,2},{8,12},{10,14},{12,8},{14,10},{1,5},{3,7},... | collective-permute-start | bytes 1572872 | tf_op jit(solution)/shard_map/ppermute | solution.py:874
  290.5 17.7 %collective-permute-start.45 = (bf16[160,2048]{1,0:T(8,128)(2,1)S(1)}, bf16[160,2048]{1,0:T(8,128)(2,1)S(1)}, u32[]{:S(2)}, u32[]{:S(2)}) collective-permute-start(bf16[160,2048]{1,0:T(8,128)(2,1)S(1)} %add_convert_fusion.6), channel_id=1, source_target_pairs={{0,2},{2,0},{4,6},{6,4},{8,10},{10,8},{12,14},{14,12},{1,3},{3,1},... | collective-permute-start | bytes 1966088 | tf_op jit(solution)/shard_map/ppermute | solution.py:874
  293.0 27.8 %collective-permute-start.47 = (bf16[160,2048]{1,0:T(8,128)(2,1)S(1)}, bf16[160,2048]{1,0:T(8,128)(2,1)S(1)}, u32[]{:S(2)}, u32[]{:S(2)}) collective-permute-start(bf16[160,2048]{1,0:T(8,128)(2,1)S(1)} %add_convert_fusion.5), channel_id=1, source_target_pairs={{4,8},{6,10},{8,4},{10,6},{5,9},{7,11},{9,5},{11,7},{20,24},{22,26... | collective-permute-start | bytes 1966088 | tf_op jit(solution)/shard_map/ppermute | solution.py:874
  296.1 23.3 %collective-permute-start.48 = (bf16[256,640]{1,0:T(8,128)(2,1)S(1)}, bf16[256,640]{1,0:T(8,128)(2,1)S(1)}, u32[]{:S(2)}, u32[]{:S(2)}) collective-permute-start(bf16[256,640]{1,0:T(8,128)(2,1)S(1)} %add_convert_fusion.18), channel_id=1, source_target_pairs={{0,4},{2,6},{12,8},{14,10},{1,5},{3,7},{13,9},{15,11},{16,20},{18,... | collective-permute-start | bytes 983048 | tf_op jit(solution)/shard_map/ppermute | solution.py:874
  302.6 18.2 %collective-permute-start.49 = (bf16[160,1024]{1,0:T(8,128)(2,1)S(1)}, bf16[160,1024]{1,0:T(8,128)(2,1)S(1)}, u32[]{:S(2)}, u32[]{:S(2)}) collective-permute-start(bf16[160,1024]{1,0:T(8,128)(2,1)S(1)} %add_convert_fusion.17), channel_id=1, source_target_pairs={{0,2},{2,0},{4,6},{6,4},{8,10},{10,8},{12,14},{14,12},{1,3},{3,1},... | collective-permute-start | bytes 983048 | tf_op jit(solution)/shard_map/ppermute | solution.py:874
  308.7 17.0 %collective-permute-start.53 = (bf16[512,640]{1,0:T(8,128)(2,1)S(1)}, bf16[512,640]{1,0:T(8,128)(2,1)S(1)}, u32[]{:S(2)}, u32[]{:S(2)}) collective-permute-start(bf16[512,640]{1,0:T(8,128)(2,1)S(1)} %add_convert_fusion.4), channel_id=1, source_target_pairs={{4,0},{6,2},{8,12},{10,14},{5,1},{7,3},{9,13},{11,15},{20,16},{22,... | collective-permute-start | bytes 1966088 | tf_op jit(solution)/shard_map/ppermute | solution.py:874
  310.0 21.7 %collective-permute-start.54 = (bf16[160,2048]{1,0:T(8,128)(2,1)S(1)}, bf16[160,2048]{1,0:T(8,128)(2,1)S(1)}, u32[]{:S(2)}, u32[]{:S(2)}) collective-permute-start(bf16[160,2048]{1,0:T(8,128)(2,1)S(1)} %add_convert_fusion.3), channel_id=1, source_target_pairs={{0,4},{2,6},{12,8},{14,10},{1,5},{3,7},{13,9},{15,11},{16,20},{18,... | collective-permute-start | bytes 1966088 | tf_op jit(solution)/shard_map/ppermute | solution.py:874
  321.3 19.8 %collective-permute-start.50 = (bf16[160,2048]{1,0:T(8,128)(2,1)S(1)}, bf16[160,2048]{1,0:T(8,128)(2,1)S(1)}, u32[]{:S(2)}, u32[]{:S(2)}) collective-permute-start(bf16[160,2048]{1,0:T(8,128)(2,1)S(1)} %add_convert_fusion.2), channel_id=1, source_target_pairs={{4,0},{6,2},{8,12},{10,14},{5,1},{7,3},{9,13},{11,15},{20,16},{22,... | collective-permute-start | bytes 1966088 | tf_op jit(solution)/shard_map/ppermute | solution.py:874
  322.6 18.5 %collective-permute-start.51 = (bf16[256,640]{1,0:T(8,128)(2,1)S(1)}, bf16[256,640]{1,0:T(8,128)(2,1)S(1)}, u32[]{:S(2)}, u32[]{:S(2)}) collective-permute-start(bf16[256,640]{1,0:T(8,128)(2,1)S(1)} %add_convert_fusion.16), channel_id=1, source_target_pairs={{4,8},{6,10},{8,4},{10,6},{5,9},{7,11},{9,5},{11,7},{20,24},{22,26... | collective-permute-start | bytes 983048 | tf_op jit(solution)/shard_map/ppermute | solution.py:874
  332.0 17.5 %collective-permute-start.58 = (bf16[512,640]{1,0:T(8,128)(2,1)S(1)}, bf16[512,640]{1,0:T(8,128)(2,1)S(1)}, u32[]{:S(2)}, u32[]{:S(2)}) collective-permute-start(bf16[512,640]{1,0:T(8,128)(2,1)S(1)} %broadcast_select_fusion.2), channel_id=1, source_target_pairs={{0,2},{2,0},{4,6},{6,4},{8,10},{10,8},{12,14},{14,12},{1,3},{3,1},... | collective-permute-start | bytes 1966088 | tf_op jit(solution)/shard_map/ppermute | solution.py:874
  333.6 16.6 %collective-permute-start.59 = (bf16[160,2048]{1,0:T(8,128)(2,1)S(1)}, bf16[160,2048]{1,0:T(8,128)(2,1)S(1)}, u32[]{:S(2)}, u32[]{:S(2)}) collective-permute-start(bf16[160,2048]{1,0:T(8,128)(2,1)S(1)} %add_convert_fusion.1), channel_id=1, source_target_pairs={{4,8},{6,10},{8,4},{10,6},{5,9},{7,11},{9,5},{11,7},{20,24},{22,26... | collective-permute-start | bytes 1966088 | tf_op jit(solution)/shard_map/ppermute | solution.py:874
  341.2 22.3 %collective-permute-start.55 = (bf16[160,2048]{1,0:T(8,128)(2,1)S(1)}, bf16[160,2048]{1,0:T(8,128)(2,1)S(1)}, u32[]{:S(2)}, u32[]{:S(2)}) collective-permute-start(bf16[160,2048]{1,0:T(8,128)(2,1)S(1)} %broadcast_select_fusion.1), channel_id=1, source_target_pairs={{0,2},{2,0},{4,6},{6,4},{8,10},{10,8},{12,14},{14,12},{1,3},{3,1},... | collective-permute-start | bytes 1966088 | tf_op jit(solution)/shard_map/ppermute | solution.py:874
  350.5 19.6 %collective-permute-start.63 = (bf16[160,2048]{1,0:T(8,128)(2,1)S(1)}, bf16[160,2048]{1,0:T(8,128)(2,1)S(1)}, u32[]{:S(2)}, u32[]{:S(2)}) collective-permute-start(bf16[160,2048]{1,0:T(8,128)(2,1)S(1)} %add_convert_fusion), channel_id=1, source_target_pairs={{4,0},{6,2},{8,12},{10,14},{5,1},{7,3},{9,13},{11,15},{20,16},{22,... | collective-permute-start | bytes 1966088 | tf_op jit(solution)/shard_map/ppermute | solution.py:874
  370.2 18.4 %collective-permute-start.66 = (bf16[160,2048]{1,0:T(8,128)(2,1)S(1)}, bf16[160,2048]{1,0:T(8,128)(2,1)S(1)}, u32[]{:S(2)}, u32[]{:S(2)}) collective-permute-start(bf16[160,2048]{1,0:T(8,128)(2,1)S(1)} %broadcast_select_fusion), channel_id=1, source_target_pairs={{0,2},{2,0},{4,6},{6,4},{8,10},{10,8},{12,14},{14,12},{1,3},{3,1},... | collective-permute-start | bytes 1966088 | tf_op jit(solution)/shard_map/ppermute | solution.py:874
  374.9 18.1 %collective-permute-start.65 = (bf16[160,1024]{1,0:T(8,128)(2,1)S(1)}, bf16[160,1024]{1,0:T(8,128)(2,1)S(1)}, u32[]{:S(2)}, u32[]{:S(2)}) collective-permute-start(bf16[160,1024]{1,0:T(8,128)(2,1)S(1)} %broadcast_select_fusion.4), channel_id=1, source_target_pairs={{0,2},{2,0},{4,6},{6,4},{8,10},{10,8},{12,14},{14,12},{1,3},{3,1},... | collective-permute-start | bytes 983048 | tf_op jit(solution)/shard_map/ppermute | solution.py:874
  (76 other events, 722.7 us)

commit v5 on v4

--- a/solution.py
+++ b/solution.py
@@ -839,7 +839,7 @@
     return (jnp.where(y_index == 0, first, second), jnp.where(y_index == 0, second, first))
 
 
-def run_turns(sets, turns, held):
+def run_turns(sets, turns, beside, held):
     results = {}
     states = {
         name: dict(entries=list(one), active=[], turn=0, landed=None)
@@ -880,7 +880,8 @@
         if callable(turn):
             state, operands = latest
             got = turn(results, lambda value: after(value, operands))
-            got, state["landed"] = lax.optimization_barrier((got, state["landed"]))
+            if turn in beside:
+                got, state["landed"] = lax.optimization_barrier((got, state["landed"]))
             held.update(got)
         else:
             step(states[turn])
@@ -1064,11 +1065,12 @@
             "b": [[chunk("gate", 0)], [chunk("out", 0)], [chunk("query", 0)]],
             "kv": [[("kv", lambda: scatter_pairs(at["parts"]))]],
         }
+        beside = (do_attention, do_queries)
         turns = (
             ["a", "a", do_gate, "b", do_up, do_out, "b", do_attention, "a", do_queries, "b"]
             + ["a", "kv", "b", "a", "kv", "b", "kv", do_tail]
         )
-        sums = run_turns(sets, turns, at)
+        sums = run_turns(sets, turns, beside, at)
     else:
         for work in (do_gate, do_up, do_attention, do_queries, do_out, do_tail):
             at.update(work({}, lambda value: value))

time: 417 us -> 409 us (0.981)
  waiting for transfers between devices: 147 us -> 135 us
  starting transfers between devices: 106 us -> 111 us
    ppermute x40, waiting for transfers between devices: 88.5 us -> 76.5 us  [step(): lax.ppermute(value, axis, pairs)]
    ppermute x40, starting transfers between devices: 60.5 us -> 65 us  [step(): lax.ppermute(value, axis, pairs)]
  transfers between devices with their start and end apart: 71 -> 71, of which waited for: 31 -> 31; matrix products, arithmetic and copies ran while one was open for 6% -> 7% of each run, Pallas kernels for 12% -> 11%
where the time goes in v5:
time: 409 us; the launch traced here: 401 us
  waiting for transfers between devices  135 us (33%)
  Pallas kernels  115 us (28%)
  starting transfers between devices  111 us (27%)
  other arithmetic  27.2 us (7%)
  local copies, waits for them, and re-layouts  11.2 us (3%)
    pallas_call x21, Pallas kernels, call_kernel(): pl.pallas_call(body, out_shape=out_shapes, in_specs=[whole] * len(inputs)...  115 us
    ppermute x40, waiting for transfers between devices, step(): lax.ppermute(value, axis, pairs)  76.5 us
    ppermute x40, starting transfers between devices, step(): lax.ppermute(value, axis, pairs)  65 us
    ppermute x22, waiting for transfers between devices, xor_permute(): return lax.ppermute(shard, axis, [(i, i ^ mask) for i in range(count)])  38.1 us
    ppermute x22, starting transfers between devices, xor_permute(): return lax.ppermute(shard, axis, [(i, i ^ mask) for i in range(count)])  24.1 us
    ppermute x7, starting transfers between devices, run_alone(): lax.ppermute(value, axis, pairs)  16.4 us
    convert_element_type x27, other arithmetic, add_low(): return lax.optimization_barrier(total.astype(bf16))  13 us
  transfers between devices with their start and end apart: 71, of which 31 were waited for; matrix products, arithmetic and copies ran while one was open for 7% of the time, Pallas kernels for 11%

profile of v5, /device:TPU:0, one launch (start us, length us, event | category | flops | bytes accessed | tf_op | source)
XLA Modules:
  0.0 400.9 jit_solution(13289102283047103599)
XLA Ops:
  20.9 4.1 %shard_map.272 = (f32[256,1024]{1,0:T(8,128)}, bf16[2,512,256]{2,1,0:T(8,128)(2,1)}) custom-call(bf16[256,640]{1,0:T(8,128)(2,1)} %get-tuple-element.163.normed, bf16[1,1536]{1,0:T(2,128)(2,1)} %copy-done.16, bf16[1,1536]{1,0:T(2,128)(2,1)} %copy-done.17, f32[128,128]{1,0:T(8,128)} %get-tuple-element.352.cos_ref.refs_11_.refs_8_, ...), custom_call_target="tpu_custom_call" | custom-call | bytes 10045440 | tf_op jit(solution)/shard_map/pallas_call | solution.py:72
  31.4 8.0 %collective-permute-done.11.refs_10_ = bf16[2,128,512]{2,1,0:T(8,128)(2,1)} collective-permute-done((bf16[2,128,512]{2,1,0:T(8,128)(2,1)}, bf16[2,128,512]{2,1,0:T(8,128)(2,1)}, u32[]{:S(2)}, u32[]{:S(2)}) %collective-permute-start.11) | collective-permute-done | bytes 262176 | tf_op jit(solution)/shard_map/ppermute | solution.py:737
  49.8 9.6 %shard_map.273 = bf16[256,640]{1,0:T(8,128)(2,1)} custom-call(bf16[2,512,256]{2,1,0:T(8,128)(2,1)} %get-tuple-element.164.refs_0_, bf16[256,640]{1,0:T(8,128)(2,1)} %bitcast.84, bf16[1,1536]{1,0:T(2,128)(2,1)} %copy-done.16, bf16[1,1536]{1,0:T(2,128)(2,1)} %copy-done.17, s32[1,1024]{1,0:T(1,128)} %add.188.refs_4_, s32[512,1]{1,0:T(8,128)} %copy.33.refs_5_, ...), custom_call_target="tpu_custom_call" | custom-call | bytes 37392384 | tf_op jit(solution)/shard_map/pallas_call | solution.py:72
  59.5 3.6 collective-permute-start.15
  63.1 4.7 %collective-permute-done.15 = bf16[256,640]{1,0:T(8,128)(2,1)S(1)} collective-permute-done((bf16[256,640]{1,0:T(8,128)(2,1)}, bf16[256,640]{1,0:T(8,128)(2,1)S(1)}, u32[]{:S(2)}, u32[]{:S(2)}) %collective-permute-start.15) | collective-permute-done | bytes 327712 | tf_op jit(solution)/shard_map/ppermute | solution.py:1007
  80.1 4.1 %shard_map.275 = (f32[256,1024]{1,0:T(8,128)}, bf16[2,512,256]{2,1,0:T(8,128)(2,1)}) custom-call(bf16[256,640]{1,0:T(8,128)(2,1)} %get-tuple-element.170.normed.left, bf16[1,1536]{1,0:T(2,128)(2,1)} %copy-done.16, bf16[1,1536]{1,0:T(2,128)(2,1)} %copy-done.17, f32[128,128]{1,0:T(8,128)} %get-tuple-element.352.cos_ref.refs_11_.refs_8_, ...), custom_call_target="tpu_custom_call" | custom-call | bytes 10045440 | tf_op jit(solution)/shard_map/pallas_call | solution.py:72
  85.0 11.5 %collective-permute-done.19.refs_10_.refs_9_ = bf16[2,128,512]{2,1,0:T(8,128)(2,1)S(1)} collective-permute-done((bf16[2,128,512]{2,1,0:T(8,128)(2,1)}, bf16[2,128,512]{2,1,0:T(8,128)(2,1)S(1)}, u32[]{:S(2)}, u32[]{:S(2)}) %collective-permute-start.19) | collective-permute-done | bytes 262176 | tf_op jit(solution)/shard_map/ppermute | solution.py:737
  106.4 11.3 %shard_map.276 = (bf16[256,640]{1,0:T(8,128)(2,1)}, f32[2,512,1]{2,1,0:T(8,128)}, bf16[256,1024]{1,0:T(8,128)(2,1)}, f32[256,640]{1,0:T(8,128)}, f32[256,640]{1,...) custom-call(bf16[2,512,256]{2,1,0:T(8,128)(2,1)} %get-tuple-element., ...), custom_call_target="tpu_custom_call" | custom-call | bytes 61587456 | tf_op jit(solution)/shard_map/pallas_call | solution.py:72
  119.6 12.4 %shard_map.277 = (f32[256,640]{1,0:T(8,128)}, bf16[256,640]{1,0:T(8,128)(2,1)}, bf16[256,2048]{1,0:T(8,128)(2,1)}, bf16[256,2048]{1,0:T(8,128)(2,1)}, bf16[256,6...) custom-call(bf16[256,640]{1,0:T(8,128)(2,1)} %bitcast.103, ...), custom_call_target="tpu_custom_call" | custom-call | bytes 58827264 | tf_op jit(solution)/shard_map/pallas_call | solution.py:72
  132.0 8.4 %shard_map.278 = (f32[2,512,256]{2,1,0:T(8,128)}, bf16[2,128,512]{2,1,0:T(8,128)(2,1)}, bf16[2,128,512]{2,1,0:T(8,128)(2,1)}, bf16[2,128,512]{2,1,0:T(8,128)(2,1...) custom-call(bf16[256,1024]{1,0:T(8,128)(2,1)} %get-tuple-element.182, ...), custom_call_target="tpu_custom_call" | custom-call | bytes 18905088 | tf_op jit(solution)/shard_map/pallas_call | solution.py:72
  144.6 3.6 collective-permute-done.23
  153.2 6.0 %collective-permute-start.26 = (bf16[2,128,512]{2,1,0:T(8,128)(2,1)S(1)}, bf16[2,128,512]{2,1,0:T(8,128)(2,1)S(1)}, u32[]{:S(2)}, u32[]{:S(2)}) collective-permute-start(bf16[2,128,512]{2,1,0:T(8,128)(2,1)S(1)} %add_convert_fusion.21), channel_id=1, source_target_pairs={{0,8},{2,10},{4,12},{6,14},{8,0},{10,2},{12,4},{14,6},{1,9},{3,11}... | collective-permute-start | bytes 786440 | tf_op jit(solution)/shard_map/ppermute | solution.py:899
  162.6 4.4 %shard_map.279 = (bf16[256,1024]{1,0:T(8,128)(2,1)}, f32[256,640]{1,0:T(8,128)}, f32[1,256]{1,0:T(1,128)}) custom-call(f32[2,512,256]{2,1,0:T(8,128)} %get-tuple-element.193.query_grad, f32[256,1024]{1,0:T(8,128)} %get-tuple-element.194.query_lin, bf16[1,1536]{1,0:T(2,128)(2,1)} %copy-done.16, bf16[1,1536]{1,0:T(2,128)(2,1)} %copy-done.17, ...), custom_call_target="tpu_custom_call" | custom-call | bytes 14177280 | tf_op jit(solution)/shard_map/pallas_call | solution.py:72
  167.0 4.2 %collective-permute-done.26 = bf16[2,128,512]{2,1,0:T(8,128)(2,1)S(1)} collective-permute-done((bf16[2,128,512]{2,1,0:T(8,128)(2,1)S(1)}, bf16[2,128,512]{2,1,0:T(8,128)(2,1)S(1)}, u32[]{:S(2)}, u32[]{:S(2)}) %collective-permute-start.26) | collective-permute-done | bytes 262176 | tf_op jit(solution)/shard_map/ppermute | solution.py:899
  172.1 4.4 %shard_map.280 = (bf16[256,640]{1,0:T(8,128)(2,1)}, bf16[256,512]{1,0:T(8,128)(2,1)}, f32[1,640]{1,0:T(1,128)}, f32[1,256]{1,0:T(1,128)}) custom-call(bf16[256,512]{1,0:T(8,128)(2,1)} %bitcast.111, bf16[256,512]{1,0:T(8,128)(2,1)} %bitcast.112, bf16[256,512]{1,0:T(8,128)(2,1)} %bitcast.113, bf16[256,512]{1,0:T(8,128)(2,1)} %bitcast.109, ...), custom_call_target="tpu_custom_call" | custom-call | bytes 13791744 | tf_op jit(solution)/shard_map/pallas_call | solution.py:72
  178.2 7.5 %collective-permute-done.30 = bf16[256,640]{1,0:T(8,128)(2,1)S(1)} collective-permute-done((bf16[256,640]{1,0:T(8,128)(2,1)}, bf16[256,640]{1,0:T(8,128)(2,1)S(1)}, u32[]{:S(2)}, u32[]{:S(2)}) %collective-permute-start.30) | collective-permute-done | bytes 327712 | tf_op jit(solution)/shard_map/ppermute | solution.py:1017
  186.5 12.1 %shard_map.281 = (f32[256,640]{1,0:T(8,128)}, bf16[256,640]{1,0:T(8,128)(2,1)}, bf16[256,2048]{1,0:T(8,128)(2,1)}, bf16[256,2048]{1,0:T(8,128)(2,1)}, bf16[256,6...) custom-call(bf16[256,640]{1,0:T(8,128)(2,1)} %broadcast_select_fusion, ...), custom_call_target="tpu_custom_call" | custom-call | bytes 58827264 | tf_op jit(solution)/shard_map/pallas_call | solution.py:72
  198.6 3.6 shard_map.282
  222.8 7.2 %collective-permute-done.38 = bf16[512,640]{1,0:T(8,128)(2,1)} collective-permute-done((bf16[512,640]{1,0:T(8,128)(2,1)}, bf16[512,640]{1,0:T(8,128)(2,1)}, u32[]{:S(2)}, u32[]{:S(2)}) %collective-permute-start.38) | collective-permute-done | bytes 655392 | tf_op jit(solution)/shard_map/ppermute | solution.py:874
  233.4 8.5 %shard_map.285 = (f32[2,512,256]{2,1,0:T(8,128)}, bf16[2,2,128,512]{3,2,1,0:T(8,128)(2,1)}, bf16[2,2,128,512]{3,2,1,0:T(8,128)(2,1)}, bf16[2,2,128,512]{3,2,1,0:T(8,128)(2,1)}, bf16[2,2,128,512]{3,2,1,0:T(8,128)(2,1)}) custom-call(bf16[256,1024]{1,0:T(8,128)(2,1)} %get-tuple-element.212.refs_0_, bf16[2,512,256]{2,1,0:T(8,128)(2,1)} %get-tuple-element.171.refs_0_.refs_1_, ...), custom_call_target="tpu_custom_call" | custom-call | bytes 18905088 | tf_op jit(solution)/shard_map/pallas_call | solution.py:72
  244.8 5.3 %collective-permute-start.39 = (bf16[160,2048]{1,0:T(8,128)(2,1)S(1)}, bf16[160,2048]{1,0:T(8,128)(2,1)S(1)}, u32[]{:S(2)}, u32[]{:S(2)}) collective-permute-start(bf16[160,2048]{1,0:T(8,128)(2,1)S(1)} %add_convert_fusion.8), channel_id=1, source_target_pairs={{0,4},{2,6},{12,8},{14,10},{1,5},{3,7},{13,9},{15,11},{16,20},{18,... | collective-permute-start | bytes 1966088 | tf_op jit(solution)/shard_map/ppermute | solution.py:874
  251.2 4.3 %shard_map.287 = (bf16[256,1024]{1,0:T(8,128)(2,1)}, f32[256,640]{1,0:T(8,128)}, f32[1,256]{1,0:T(1,128)}) custom-call(f32[2,512,256]{2,1,0:T(8,128)} %get-tuple-element.233.query_grad, f32[256,1024]{1,0:T(8,128)} %get-tuple-element.194.query_lin, bf16[1,1536]{1,0:T(2,128)(2,1)} %copy-done.16, bf16[1,1536]{1,0:T(2,128)(2,1)} %copy-done.17, ...), custom_call_target="tpu_custom_call" | custom-call | bytes 14177280 | tf_op jit(solution)/shard_map/pallas_call | solution.py:72
  260.3 6.4 %collective-permute-done.40 = bf16[256,640]{1,0:T(8,128)(2,1)S(1)} collective-permute-done((bf16[256,640]{1,0:T(8,128)(2,1)S(1)}, bf16[256,640]{1,0:T(8,128)(2,1)S(1)}, u32[]{:S(2)}, u32[]{:S(2)}) %collective-permute-start.40) | collective-permute-done | bytes 327712 | tf_op jit(solution)/shard_map/ppermute | solution.py:874
  266.6 18.3 %collective-permute-done.39 = bf16[160,2048]{1,0:T(8,128)(2,1)S(1)} collective-permute-done((bf16[160,2048]{1,0:T(8,128)(2,1)S(1)}, bf16[160,2048]{1,0:T(8,128)(2,1)S(1)}, u32[]{:S(2)}, u32[]{:S(2)}) %collective-permute-start.39) | collective-permute-done | bytes 655392 | tf_op jit(solution)/shard_map/ppermute | solution.py:874
  289.5 8.8 %collective-permute-start.48 = (bf16[256,640]{1,0:T(8,128)(2,1)S(1)}, bf16[256,640]{1,0:T(8,128)(2,1)S(1)}, u32[]{:S(2)}, u32[]{:S(2)}) collective-permute-start(bf16[256,640]{1,0:T(8,128)(2,1)S(1)} %add_convert_fusion.18), channel_id=1, source_target_pairs={{0,4},{2,6},{12,8},{14,10},{1,5},{3,7},{13,9},{15,11},{16,20},{18,... | collective-permute-start | bytes 983048 | tf_op jit(solution)/shard_map/ppermute | solution.py:874
  303.4 7.5 %collective-permute-start.54 = (bf16[160,2048]{1,0:T(8,128)(2,1)S(1)}, bf16[160,2048]{1,0:T(8,128)(2,1)S(1)}, u32[]{:S(2)}, u32[]{:S(2)}) collective-permute-start(bf16[160,2048]{1,0:T(8,128)(2,1)S(1)} %add_convert_fusion.3), channel_id=1, source_target_pairs={{0,4},{2,6},{12,8},{14,10},{1,5},{3,7},{13,9},{15,11},{16,20},{18,... | collective-permute-start | bytes 1966088 | tf_op jit(solution)/shard_map/ppermute | solution.py:874
  317.7 6.9 %collective-permute-start.52 = (bf16[160,1024]{1,0:T(8,128)(2,1)S(1)}, bf16[160,1024]{1,0:T(8,128)(2,1)S(1)}, u32[]{:S(2)}, u32[]{:S(2)}) collective-permute-start(bf16[160,1024]{1,0:T(8,128)(2,1)S(1)} %add_convert_fusion.15), channel_id=1, source_target_pairs={{0,4},{2,6},{12,8},{14,10},{1,5},{3,7},{13,9},{15,11},{16,20},{18,... | collective-permute-start | bytes 983048 | tf_op jit(solution)/shard_map/ppermute | solution.py:874
  327.5 4.2 %shard_map.289 = (bf16[256,640]{1,0:T(8,128)(2,1)}, bf16[256,512]{1,0:T(8,128)(2,1)}, f32[1,640]{1,0:T(1,128)}, f32[1,256]{1,0:T(1,128)}) custom-call(f32[256,512]{1,0:T(8,128)} %bitcast.102, bf16[256,512]{1,0:T(8,128)(2,1)} %bitcast.114, f32[256,256]{1,0:T(8,128)} %get-tuple-element.192.refs_5_.refs_2_, ...), custom_call_target="tpu_custom_call" | custom-call | bytes 12218880 | tf_op jit(solution)/shard_map/pallas_call | solution.py:72
  337.1 3.9 collective-permute-done.58
  347.4 7.6 %collective-permute-done.55 = bf16[160,2048]{1,0:T(8,128)(2,1)S(1)} collective-permute-done((bf16[160,2048]{1,0:T(8,128)(2,1)S(1)}, bf16[160,2048]{1,0:T(8,128)(2,1)S(1)}, u32[]{:S(2)}, u32[]{:S(2)}) %collective-permute-start.55) | collective-permute-done | bytes 655392 | tf_op jit(solution)/shard_map/ppermute | solution.py:874
  370.6 8.7 %collective-permute-done.66 = bf16[160,2048]{1,0:T(8,128)(2,1)S(1)} collective-permute-done((bf16[160,2048]{1,0:T(8,128)(2,1)S(1)}, bf16[160,2048]{1,0:T(8,128)(2,1)S(1)}, u32[]{:S(2)}, u32[]{:S(2)}) %collective-permute-start.66) | collective-permute-done | bytes 655392 | tf_op jit(solution)/shard_map/ppermute | solution.py:874
  380.2 5.0 %collective-permute-done.65 = bf16[160,1024]{1,0:T(8,128)(2,1)S(1)} collective-permute-done((bf16[160,1024]{1,0:T(8,128)(2,1)S(1)}, bf16[160,1024]{1,0:T(8,128)(2,1)S(1)}, u32[]{:S(2)}, u32[]{:S(2)}) %collective-permute-start.65) | collective-permute-done | bytes 327712 | tf_op jit(solution)/shard_map/ppermute | solution.py:874
  (268 shorter events, 172.8 us)
Async XLA Ops:
  17.8 21.6 %collective-permute-start.11 = (bf16[2,128,512]{2,1,0:T(8,128)(2,1)}, bf16[2,128,512]{2,1,0:T(8,128)(2,1)}, u32[]{:S(2)}, u32[]{:S(2)}) collective-permute-start(bf16[2,128,512]{2,1,0:T(8,128)(2,1)} %bitcast.105), channel_id=1, source_target_pairs={{0,8},{2,10},{4,12},{6,14},{8,0},{10,2},{12,4},{14,6},{1,9},{3,11}... | collective-permute-start | bytes 786440 | tf_op jit(solution)/shard_map/ppermute | solution.py:737
  20.4 20.6 %collective-permute-start.13 = (bf16[2,128,512]{2,1,0:T(8,128)(2,1)}, bf16[2,128,512]{2,1,0:T(8,128)(2,1)}, u32[]{:S(2)}, u32[]{:S(2)}) collective-permute-start(bf16[2,128,512]{2,1,0:T(8,128)(2,1)} %bitcast.106), channel_id=1, source_target_pairs={{0,12},{2,14},{4,8},{6,10},{8,4},{10,6},{12,0},{14,2},{1,13},{3,15... | collective-permute-start | bytes 786440 | tf_op jit(solution)/shard_map/ppermute | solution.py:737
  25.0 18.8 %collective-permute-start.8 = (bf16[2,128,512]{2,1,0:T(8,128)(2,1)S(1)}, bf16[2,128,512]{2,1,0:T(8,128)(2,1)}, u32[]{:S(2)}, u32[]{:S(2)}) collective-permute-start(bf16[2,128,512]{2,1,0:T(8,128)(2,1)S(1)} %bitcast.108), channel_id=1, source_target_pairs={{0,2},{2,0},{4,6},{6,4},{8,10},{10,8},{12,14},{14,12},{1,3},{3,1},... | collective-permute-start | bytes 786440 | tf_op jit(solution)/shard_map/ppermute | solution.py:737
  76.1 20.3 %collective-permute-start.19 = (bf16[2,128,512]{2,1,0:T(8,128)(2,1)}, bf16[2,128,512]{2,1,0:T(8,128)(2,1)S(1)}, u32[]{:S(2)}, u32[]{:S(2)}) collective-permute-start(bf16[2,128,512]{2,1,0:T(8,128)(2,1)} %bitcast.96), channel_id=1, source_target_pairs={{0,8},{2,10},{4,12},{6,14},{8,0},{10,2},{12,4},{14,6},{1,9},{3,11}... | collective-permute-start | bytes 786440 | tf_op jit(solution)/shard_map/ppermute | solution.py:737
  77.9 20.1 %collective-permute-start.21 = (bf16[2,128,512]{2,1,0:T(8,128)(2,1)}, bf16[2,128,512]{2,1,0:T(8,128)(2,1)S(1)}, u32[]{:S(2)}, u32[]{:S(2)}) collective-permute-start(bf16[2,128,512]{2,1,0:T(8,128)(2,1)} %bitcast.97), channel_id=1, source_target_pairs={{0,12},{2,14},{4,8},{6,10},{8,4},{10,6},{12,0},{14,2},{1,13},{3,15... | collective-permute-start | bytes 786440 | tf_op jit(solution)/shard_map/ppermute | solution.py:737
  78.5 21.2 %collective-permute-start.16 = (bf16[2,128,512]{2,1,0:T(8,128)(2,1)}, bf16[2,128,512]{2,1,0:T(8,128)(2,1)S(1)}, u32[]{:S(2)}, u32[]{:S(2)}) collective-permute-start(bf16[2,128,512]{2,1,0:T(8,128)(2,1)} %bitcast.98), channel_id=1, source_target_pairs={{0,2},{2,0},{4,6},{6,4},{8,10},{10,8},{12,14},{14,12},{1,3},{3,1},... | collective-permute-start | bytes 786440 | tf_op jit(solution)/shard_map/ppermute | solution.py:737
  142.5 16.6 %collective-permute-start.27 = (bf16[2,128,512]{2,1,0:T(8,128)(2,1)}, bf16[2,128,512]{2,1,0:T(8,128)(2,1)S(1)}, u32[]{:S(2)}, u32[]{:S(2)}) collective-permute-start(bf16[2,128,512]{2,1,0:T(8,128)(2,1)} %get-tuple-element.189), channel_id=1, source_target_pairs={{0,2},{2,0},{4,6},{6,4},{8,10},{10,8},{12,14},{14,12},{1,3},{3,1},... | collective-permute-start | bytes 786440 | tf_op jit(solution)/shard_map/ppermute | solution.py:899
  144.1 22.9 %collective-permute-start.29 = (bf16[2,128,512]{2,1,0:T(8,128)(2,1)}, bf16[2,128,512]{2,1,0:T(8,128)(2,1)S(1)}, u32[]{:S(2)}, u32[]{:S(2)}) collective-permute-start(bf16[2,128,512]{2,1,0:T(8,128)(2,1)} %get-tuple-element.191), channel_id=1, source_target_pairs={{0,2},{2,0},{4,6},{6,4},{8,10},{10,8},{12,14},{14,12},{1,3},{3,1},... | collective-permute-start | bytes 786440 | tf_op jit(solution)/shard_map/ppermute | solution.py:899
  149.2 17.8 %collective-permute-start.24 = (bf16[2,128,512]{2,1,0:T(8,128)(2,1)S(1)}, bf16[2,128,512]{2,1,0:T(8,128)(2,1)S(1)}, u32[]{:S(2)}, u32[]{:S(2)}) collective-permute-start(bf16[2,128,512]{2,1,0:T(8,128)(2,1)S(1)} %add_convert_fusion.22), channel_id=1, source_target_pairs={{0,12},{2,14},{4,8},{6,10},{8,4},{10,6},{12,0},{14,2},{1,13},{3,15... | collective-permute-start | bytes 786440 | tf_op jit(solution)/shard_map/ppermute | solution.py:899
  153.2 18.1 %collective-permute-start.26 = (bf16[2,128,512]{2,1,0:T(8,128)(2,1)S(1)}, bf16[2,128,512]{2,1,0:T(8,128)(2,1)S(1)}, u32[]{:S(2)}, u32[]{:S(2)}) collective-permute-start(bf16[2,128,512]{2,1,0:T(8,128)(2,1)S(1)} %add_convert_fusion.21), channel_id=1, source_target_pairs={{0,8},{2,10},{4,12},{6,14},{8,0},{10,2},{12,4},{14,6},{1,9},{3,11}... | collective-permute-start | bytes 786440 | tf_op jit(solution)/shard_map/ppermute | solution.py:899
  212.2 17.9 %collective-permute-start.38 = (bf16[512,640]{1,0:T(8,128)(2,1)}, bf16[512,640]{1,0:T(8,128)(2,1)}, u32[]{:S(2)}, u32[]{:S(2)}) collective-permute-start(bf16[512,640]{1,0:T(8,128)(2,1)} %add_convert_fusion.11), channel_id=1, source_target_pairs={{0,2},{2,0},{4,6},{6,4},{8,10},{10,8},{12,14},{14,12},{1,3},{3,1},... | collective-permute-start | bytes 1966088 | tf_op jit(solution)/shard_map/ppermute | solution.py:874
  216.5 25.4 %collective-permute-start.34 = (bf16[512,640]{1,0:T(8,128)(2,1)}, bf16[512,640]{1,0:T(8,128)(2,1)}, u32[]{:S(2)}, u32[]{:S(2)}) collective-permute-start(bf16[512,640]{1,0:T(8,128)(2,1)} %get-tuple-element.211), channel_id=1, source_target_pairs={{0,1},{1,0},{2,3},{3,2},{4,5},{5,4},{6,7},{7,6},{8,9},{9,8},{10,11... | collective-permute-start | bytes 1966088 | tf_op jit(solution)/shard_map/ppermute | solution.py:874
  218.8 24.7 %collective-permute-start.33 = (bf16[160,2048]{1,0:T(8,128)(2,1)}, bf16[160,2048]{1,0:T(8,128)(2,1)S(1)}, u32[]{:S(2)}, u32[]{:S(2)}) collective-permute-start(bf16[160,2048]{1,0:T(8,128)(2,1)} %add_convert_fusion.10), channel_id=1, source_target_pairs={{0,2},{2,0},{4,6},{6,4},{8,10},{10,8},{12,14},{14,12},{1,3},{3,1},... | collective-permute-start | bytes 1966088 | tf_op jit(solution)/shard_map/ppermute | solution.py:874
  222.7 35.6 %collective-permute-start.42 = (bf16[320,2048]{1,0:T(8,128)(2,1)}, bf16[320,2048]{1,0:T(8,128)(2,1)S(1)}, u32[]{:S(2)}, u32[]{:S(2)}) collective-permute-start(bf16[320,2048]{1,0:T(8,128)(2,1)} %get-tuple-element.228), channel_id=1, source_target_pairs={{0,1},{1,0},{2,3},{3,2},{4,5},{5,4},{6,7},{7,6},{8,9},{9,8},{10,11... | collective-permute-start | bytes 3932168 | tf_op jit(solution)/shard_map/ppermute | solution.py:874
  231.8 28.0 %collective-permute-start.41 = (bf16[512,640]{1,0:T(8,128)(2,1)S(1)}, bf16[512,640]{1,0:T(8,128)(2,1)S(1)}, u32[]{:S(2)}, u32[]{:S(2)}) collective-permute-start(bf16[512,640]{1,0:T(8,128)(2,1)S(1)} %add_convert_fusion.9), channel_id=1, source_target_pairs={{0,4},{2,6},{12,8},{14,10},{1,5},{3,7},{13,9},{15,11},{16,20},{18,... | collective-permute-start | bytes 1966088 | tf_op jit(solution)/shard_map/ppermute | solution.py:874
  243.5 45.3 %collective-permute-start.35 = (bf16[2,2,128,512]{3,2,1,0:T(8,128)(2,1)}, bf16[2,2,128,512]{3,2,1,0:T(8,128)(2,1)}, u32[]{:S(2)}, u32[]{:S(2)}) collective-permute-start(bf16[2,2,128,512]{3,2,1,0:T(8,128)(2,1)} %get-tuple-element.219), channel_id=1, source_target_pairs={{0,12},{2,14},{4,8},{6,10},{8,4},{10,6},{12,0},{14,2},{1,13},{3,15... | collective-permute-start | bytes 1572872 | tf_op jit(solution)/shard_map/ppermute | solution.py:874
  244.5 45.0 %collective-permute-start.36 = (bf16[2,2,128,512]{3,2,1,0:T(8,128)(2,1)}, bf16[2,2,128,512]{3,2,1,0:T(8,128)(2,1)}, u32[]{:S(2)}, u32[]{:S(2)}) collective-permute-start(bf16[2,2,128,512]{3,2,1,0:T(8,128)(2,1)} %get-tuple-element.220), channel_id=1, source_target_pairs={{0,8},{2,10},{4,12},{6,14},{8,0},{10,2},{12,4},{14,6},{1,9},{3,11}... | collective-permute-start | bytes 1572872 | tf_op jit(solution)/shard_map/ppermute | solution.py:874
  244.8 40.1 %collective-permute-start.39 = (bf16[160,2048]{1,0:T(8,128)(2,1)S(1)}, bf16[160,2048]{1,0:T(8,128)(2,1)S(1)}, u32[]{:S(2)}, u32[]{:S(2)}) collective-permute-start(bf16[160,2048]{1,0:T(8,128)(2,1)S(1)} %add_convert_fusion.8), channel_id=1, source_target_pairs={{0,4},{2,6},{12,8},{14,10},{1,5},{3,7},{13,9},{15,11},{16,20},{18,... | collective-permute-start | bytes 1966088 | tf_op jit(solution)/shard_map/ppermute | solution.py:874
  259.9 25.8 %collective-permute-start.43 = (bf16[320,1024]{1,0:T(8,128)(2,1)}, bf16[320,1024]{1,0:T(8,128)(2,1)S(1)}, u32[]{:S(2)}, u32[]{:S(2)}) collective-permute-start(bf16[320,1024]{1,0:T(8,128)(2,1)} %get-tuple-element.239), channel_id=1, source_target_pairs={{0,1},{1,0},{2,3},{3,2},{4,5},{5,4},{6,7},{7,6},{8,9},{9,8},{10,11... | collective-permute-start | bytes 1966088 | tf_op jit(solution)/shard_map/ppermute | solution.py:874
  266.6 31.7 %collective-permute-start.37 = (bf16[2,2,128,512]{3,2,1,0:T(8,128)(2,1)S(1)}, bf16[2,2,128,512]{3,2,1,0:T(8,128)(2,1)S(1)}, u32[]{:S(2)}, u32[]{:S(2)}) collective-permute-start(bf16[2,2,128,512]{3,2,1,0:T(8,128)(2,1)S(1)} %copy-done.34), channel_id=1, source_target_pairs={{0,4},{2,6},{4,0},{6,2},{8,12},{10,14},{12,8},{14,10},{1,5},{3,7},... | collective-permute-start | bytes 1572872 | tf_op jit(solution)/shard_map/ppermute | solution.py:874
  288.7 26.1 %collective-permute-start.47 = (bf16[160,2048]{1,0:T(8,128)(2,1)S(1)}, bf16[160,2048]{1,0:T(8,128)(2,1)S(1)}, u32[]{:S(2)}, u32[]{:S(2)}) collective-permute-start(bf16[160,2048]{1,0:T(8,128)(2,1)S(1)} %add_convert_fusion.5), channel_id=1, source_target_pairs={{4,8},{6,10},{8,4},{10,6},{5,9},{7,11},{9,5},{11,7},{20,24},{22,26... | collective-permute-start | bytes 1966088 | tf_op jit(solution)/shard_map/ppermute | solution.py:874
  289.5 23.7 %collective-permute-start.48 = (bf16[256,640]{1,0:T(8,128)(2,1)S(1)}, bf16[256,640]{1,0:T(8,128)(2,1)S(1)}, u32[]{:S(2)}, u32[]{:S(2)}) collective-permute-start(bf16[256,640]{1,0:T(8,128)(2,1)S(1)} %add_convert_fusion.18), channel_id=1, source_target_pairs={{0,4},{2,6},{12,8},{14,10},{1,5},{3,7},{13,9},{15,11},{16,20},{18,... | collective-permute-start | bytes 983048 | tf_op jit(solution)/shard_map/ppermute | solution.py:874
  298.3 16.5 %collective-permute-start.49 = (bf16[160,1024]{1,0:T(8,128)(2,1)S(1)}, bf16[160,1024]{1,0:T(8,128)(2,1)S(1)}, u32[]{:S(2)}, u32[]{:S(2)}) collective-permute-start(bf16[160,1024]{1,0:T(8,128)(2,1)S(1)} %add_convert_fusion.17), channel_id=1, source_target_pairs={{0,2},{2,0},{4,6},{6,4},{8,10},{10,8},{12,14},{14,12},{1,3},{3,1},... | collective-permute-start | bytes 983048 | tf_op jit(solution)/shard_map/ppermute | solution.py:874
  303.4 21.2 %collective-permute-start.54 = (bf16[160,2048]{1,0:T(8,128)(2,1)S(1)}, bf16[160,2048]{1,0:T(8,128)(2,1)S(1)}, u32[]{:S(2)}, u32[]{:S(2)}) collective-permute-start(bf16[160,2048]{1,0:T(8,128)(2,1)S(1)} %add_convert_fusion.3), channel_id=1, source_target_pairs={{0,4},{2,6},{12,8},{14,10},{1,5},{3,7},{13,9},{15,11},{16,20},{18,... | collective-permute-start | bytes 1966088 | tf_op jit(solution)/shard_map/ppermute | solution.py:874
  315.3 18.7 %collective-permute-start.50 = (bf16[160,2048]{1,0:T(8,128)(2,1)S(1)}, bf16[160,2048]{1,0:T(8,128)(2,1)S(1)}, u32[]{:S(2)}, u32[]{:S(2)}) collective-permute-start(bf16[160,2048]{1,0:T(8,128)(2,1)S(1)} %add_convert_fusion.2), channel_id=1, source_target_pairs={{4,0},{6,2},{8,12},{10,14},{5,1},{7,3},{9,13},{11,15},{20,16},{22,... | collective-permute-start | bytes 1966088 | tf_op jit(solution)/shard_map/ppermute | solution.py:874
  316.6 17.4 %collective-permute-start.51 = (bf16[256,640]{1,0:T(8,128)(2,1)S(1)}, bf16[256,640]{1,0:T(8,128)(2,1)S(1)}, u32[]{:S(2)}, u32[]{:S(2)}) collective-permute-start(bf16[256,640]{1,0:T(8,128)(2,1)S(1)} %add_convert_fusion.16), channel_id=1, source_target_pairs={{4,8},{6,10},{8,4},{10,6},{5,9},{7,11},{9,5},{11,7},{20,24},{22,26... | collective-permute-start | bytes 983048 | tf_op jit(solution)/shard_map/ppermute | solution.py:874
  317.7 16.3 %collective-permute-start.52 = (bf16[160,1024]{1,0:T(8,128)(2,1)S(1)}, bf16[160,1024]{1,0:T(8,128)(2,1)S(1)}, u32[]{:S(2)}, u32[]{:S(2)}) collective-permute-start(bf16[160,1024]{1,0:T(8,128)(2,1)S(1)} %add_convert_fusion.15), channel_id=1, source_target_pairs={{0,4},{2,6},{12,8},{14,10},{1,5},{3,7},{13,9},{15,11},{16,20},{18,... | collective-permute-start | bytes 983048 | tf_op jit(solution)/shard_map/ppermute | solution.py:874
  334.2 20.9 %collective-permute-start.55 = (bf16[160,2048]{1,0:T(8,128)(2,1)S(1)}, bf16[160,2048]{1,0:T(8,128)(2,1)S(1)}, u32[]{:S(2)}, u32[]{:S(2)}) collective-permute-start(bf16[160,2048]{1,0:T(8,128)(2,1)S(1)} %broadcast_select_fusion.1), channel_id=1, source_target_pairs={{0,2},{2,0},{4,6},{6,4},{8,10},{10,8},{12,14},{14,12},{1,3},{3,1},... | collective-permute-start | bytes 1966088 | tf_op jit(solution)/shard_map/ppermute | solution.py:874
  341.3 20.2 %collective-permute-start.63 = (bf16[160,2048]{1,0:T(8,128)(2,1)S(1)}, bf16[160,2048]{1,0:T(8,128)(2,1)S(1)}, u32[]{:S(2)}, u32[]{:S(2)}) collective-permute-start(bf16[160,2048]{1,0:T(8,128)(2,1)S(1)} %add_convert_fusion), channel_id=1, source_target_pairs={{4,0},{6,2},{8,12},{10,14},{5,1},{7,3},{9,13},{11,15},{20,16},{22,... | collective-permute-start | bytes 1966088 | tf_op jit(solution)/shard_map/ppermute | solution.py:874
  342.6 16.5 %collective-permute-start.64 = (bf16[176,512]{1,0:T(8,128)(2,1)S(1)}, bf16[176,512]{1,0:T(8,128)(2,1)S(1)}, u32[]{:S(2)}, u32[]{:S(2)}) collective-permute-start(bf16[176,512]{1,0:T(8,128)(2,1)S(1)} %add_convert_fusion.26), channel_id=1, source_target_pairs={{0,2},{2,0},{4,6},{6,4},{8,10},{10,8},{12,14},{14,12},{1,3},{3,1},... | collective-permute-start | bytes 540680 | tf_op jit(solution)/shard_map/ppermute | solution.py:874
  361.6 17.7 %collective-permute-start.66 = (bf16[160,2048]{1,0:T(8,128)(2,1)S(1)}, bf16[160,2048]{1,0:T(8,128)(2,1)S(1)}, u32[]{:S(2)}, u32[]{:S(2)}) collective-permute-start(bf16[160,2048]{1,0:T(8,128)(2,1)S(1)} %broadcast_select_fusion), channel_id=1, source_target_pairs={{0,2},{2,0},{4,6},{6,4},{8,10},{10,8},{12,14},{14,12},{1,3},{3,1},... | collective-permute-start | bytes 1966088 | tf_op jit(solution)/shard_map/ppermute | solution.py:874
  367.8 17.4 %collective-permute-start.65 = (bf16[160,1024]{1,0:T(8,128)(2,1)S(1)}, bf16[160,1024]{1,0:T(8,128)(2,1)S(1)}, u32[]{:S(2)}, u32[]{:S(2)}) collective-permute-start(bf16[160,1024]{1,0:T(8,128)(2,1)S(1)} %broadcast_select_fusion.4), channel_id=1, source_target_pairs={{0,2},{2,0},{4,6},{6,4},{8,10},{10,8},{12,14},{14,12},{1,3},{3,1},... | collective-permute-start | bytes 983048 | tf_op jit(solution)/shard_map/ppermute | solution.py:874
  (74 other events, 729.3 us)
